TPU v7x, 256 devices: a whole 4x4x8 slice. The times are simulated.
256 devices in a mesh: sim: 8 (over z_hi, y), slab: 32 (over z_lo, x, core).
Axes of the slice: x: 4, y: 4, z: 8 (z_hi: 2, z_lo: 4; z = z_hi * 4 + z_lo), core: 2. Of those that a mesh axis runs over, the one named last changes fastest.
Arguments:
- velocity: float32 [8, 3, 256, 256, 128], P('sim', None, None, 'slab'), may hold values from -3 to 5
- viscosity: float32 [8, 256, 256, 128], P('sim', None, 'slab'), may hold values from 0.02 to 0.12
- turbines: int32 [8, 256, 256, 128], P('sim', None, 'slab'), may hold values from 0 to 1, as said below
- fringe_start: int32 [1], replicated, may hold values from 0 to 224
Outputs:
- projected: float32 [8, 3, 256, 256, 128], P('sim', None, None, 'slab')
Inputs may be any that keep to these rules, and one draw needn't show every extreme that they name: `turbines`: group 0, the precursor, holds no turbine cells.
All inputs are finite; a program needn't handle non-finite values.
Results may differ from a plain program's by a relative error of at most 0.0003.
Values sent between devices are 32-bit elements; how exact they have to be, the bound alone decides.
No kernel may reach another device: no remote copies, remote signals or barrier semaphores. Data moves between devices by JAX's collectives and lax.ppermute only.
A program may use at most 128 MiB of HBM per device.

v0:
```python
import math

import jax
import jax.numpy as jnp
from jax import lax
from jax.sharding import PartitionSpec as P

FR = 32


highest = lax.Precision.HIGHEST
thrust_coef = 0.75


def broadcast(value, axis, source):
    kept = jnp.where(lax.axis_index(axis) == source, value, 0).astype(value.dtype)
    return lax.psum(kept, axis)


def with_halo(cells, sides, width):
    for axis, dim in sides:
        count = lax.axis_size(axis)
        head = lax.slice_in_dim(cells, 0, width, axis=dim)
        tail = lax.slice_in_dim(cells, cells.shape[dim] - width, cells.shape[dim], axis=dim)
        cells = jnp.concatenate(
            [
                lax.ppermute(tail, axis, [(i, (i + 1) % count) for i in range(count)]),
                cells,
                lax.ppermute(head, axis, [((i + 1) % count, i) for i in range(count)]),
            ],
            axis=dim,
        )
    return cells


def diffuse(fields, viscous):
    faces_x = 0.5 * (viscous + jnp.roll(viscous, -1, -3))
    flux_x = faces_x * (jnp.roll(fields, -1, -3) - fields)
    across_x = flux_x - jnp.roll(flux_x, 1, -3)
    faces_y = 0.5 * (viscous[..., 1:, :] + viscous[..., :-1, :])
    flux_y = faces_y * (fields[..., 1:, :] - fields[..., :-1, :])
    across_y = flux_y[..., 1:, :] - flux_y[..., :-1, :]
    faces_z = 0.5 * (viscous[..., 1:] + viscous[..., :-1])
    flux_z = faces_z * (fields[..., 1:] - fields[..., :-1])
    nothing = jnp.zeros_like(flux_z[..., :1])
    upper_flux = jnp.concatenate([flux_z, nothing], -1)
    lower_flux = jnp.concatenate([nothing, flux_z], -1)
    across_z = upper_flux - lower_flux
    return fields[..., 1:-1, :] + across_x[..., 1:-1, :] + across_y + across_z[..., 1:-1, :]


def drag(fields, turbine_cells):
    streamwise = fields[0]
    disc_mask = turbine_cells.astype(jnp.float32)
    streamwise = streamwise - 0.5 * thrust_coef * disc_mask * streamwise * jnp.abs(streamwise)
    return jnp.concatenate([streamwise[None], fields[1:]], 0)


def blend_rows(fields, precursor, first_row, active):
    length = precursor.shape[1]
    slab_rows = lax.dynamic_slice_in_dim(fields, first_row, length, 1)
    profile = (
        jnp.sin(math.pi * (jnp.arange(length, dtype=jnp.float32) + 0.5) / length) ** 2 * active
    )
    new_rows = slab_rows + profile[None, :, None, None] * (precursor - slab_rows)
    return lax.dynamic_update_slice_in_dim(fields, new_rows, first_row, 1)


def centered_x(values):
    return 0.5 * (jnp.roll(values, -1, -3) - jnp.roll(values, 1, -3))


def centered_y(extended):
    return 0.5 * (extended[..., 2:, :] - extended[..., :-2, :])


def centered_z(values):
    padded = jnp.concatenate([values[..., :1], values, values[..., -1:]], -1)
    return 0.5 * (padded[..., 2:] - padded[..., :-2])


def dft_tables(length):
    index_a = jnp.arange(length, dtype=jnp.int32)
    product = index_a[:, None] * index_a[None, :] % length
    angles = 2.0 * math.pi / length * product.astype(jnp.float32)
    return (jnp.cos(angles), jnp.sin(angles))


def dct_table(length):
    index_m = jnp.arange(length, dtype=jnp.int32)
    product = index_m[:, None] * (2 * index_m[None, :] + 1) % (4 * length)
    angles = math.pi / (2.0 * length) * product.astype(jnp.float32)
    return jnp.cos(angles)


def inverse_eigen(wave_x, wave_y, wave_z, length_x, length_y, length_z):
    eigen_x = 2.0 * jnp.cos(2.0 * math.pi * wave_x.astype(jnp.float32) / length_x) - 2.0
    eigen_y = 2.0 * jnp.cos(2.0 * math.pi * wave_y.astype(jnp.float32) / length_y) - 2.0
    eigen_z = 2.0 * jnp.cos(math.pi * wave_z.astype(jnp.float32) / length_z) - 2.0
    eigen_sum = eigen_x[:, None, None] + eigen_y[None, :, None] + eigen_z[None, None, :]
    zero_mode = (
        (wave_x[:, None, None] == 0) & (wave_y[None, :, None] == 0) & (wave_z[None, None, :] == 0)
    )
    guarded = jnp.where(zero_mode, 1.0, eigen_sum)
    return jnp.where(zero_mode, 0.0, 1.0 / guarded)


def forward_y(spectral, cos_y, sin_y):
    mixing = jnp.stack([jnp.stack([cos_y, sin_y]), jnp.stack([-sin_y, cos_y])])
    return jnp.einsum("abky,bxyz->axkz", mixing, spectral, precision=highest)


def backward_y(press_both, cos_y, sin_y, total_y):
    mixing = jnp.stack([jnp.stack([cos_y, -sin_y]), jnp.stack([sin_y, cos_y])])
    return jnp.einsum("abky,bxyz->axkz", mixing, press_both, precision=highest) / total_y


def poisson_slab(source):
    width_x, slab_rows, depth_z = source.shape
    slab_count = lax.axis_size("slab")
    total_y = slab_rows * slab_count
    cos_z = dct_table(depth_z)
    z_modes = jnp.dot(source.reshape(width_x * slab_rows, depth_z), cos_z.T, precision=highest)
    cos_x, sin_x = dft_tables(width_x)
    cos_y, sin_y = dft_tables(total_y)
    flattened = z_modes.reshape(width_x, slab_rows * depth_z)
    waves_y = jnp.arange(total_y, dtype=jnp.int32)
    waves_z = jnp.arange(depth_z, dtype=jnp.int32)
    columns = width_x // slab_count
    forward_table = jnp.concatenate([cos_x, -sin_x], 0)
    stacked = jnp.dot(forward_table, flattened, precision=highest).reshape(
        2, width_x, slab_rows, depth_z
    )
    spectral = lax.all_to_all(stacked, "slab", split_axis=1, concat_axis=2, tiled=True)
    y_both = forward_y(spectral, cos_y, sin_y)
    first_col = lax.axis_index("slab") * columns + jnp.arange(columns, dtype=jnp.int32)
    inverse = inverse_eigen(first_col, waves_y, waves_z, width_x, total_y, depth_z)
    back = backward_y(y_both * inverse[None], cos_y, sin_y, total_y)
    returned = lax.all_to_all(back, "slab", split_axis=2, concat_axis=1, tiled=True)
    inverse_table = jnp.concatenate([cos_x, -sin_x], 1)
    spatial_x = (
        jnp.dot(
            inverse_table, returned.reshape(2 * width_x, slab_rows * depth_z), precision=highest
        )
        / width_x
    )
    weights = jnp.where(jnp.arange(depth_z, dtype=jnp.int32) == 0, 1.0, 2.0) / depth_z
    spatial = jnp.dot(
        spatial_x.reshape(width_x * slab_rows, depth_z), cos_z * weights[:, None], precision=highest
    )
    return spatial.reshape(width_x, slab_rows, depth_z)


def local(velocity, viscosity, turbines, fringe_start):
    fields = velocity[0]
    viscous = viscosity[0]
    first_row = fringe_start[0]
    precursor = broadcast(lax.dynamic_slice_in_dim(fields, first_row, FR, 1), "sim", 0)
    combined = jnp.concatenate([fields, viscous[None]], 0)
    extended = with_halo(combined, (("slab", 2),), 1)
    fields = diffuse(extended[:3], extended[3])
    fields = drag(fields, turbines[0])
    active = (lax.axis_index("sim") != 0).astype(jnp.float32)
    fields = blend_rows(fields, precursor, first_row, active)
    spanwise_rim = with_halo(fields[1], (("slab", 1),), 1)
    divergence = centered_x(fields[0]) + centered_y(spanwise_rim) + centered_z(fields[2])
    pressure = poisson_slab(divergence)
    pressure_ext = with_halo(pressure, (("slab", 1),), 1)
    gradient = jnp.stack([centered_x(pressure), centered_y(pressure_ext), centered_z(pressure)])
    return (fields - gradient)[None]


def solution(mesh):
    return jax.shard_map(
        local,
        mesh=mesh,
        in_specs=(
            P("sim", None, None, "slab", None),
            P("sim", None, "slab", None),
            P("sim", None, "slab", None),
            P(),
        ),
        out_specs=P("sim", None, None, "slab", None),
        check_vma=False,
    )
```

profile of v0, /device:TPU:0, one launch (start us, length us, event | category | flops | bytes accessed | tf_op | source)
XLA Modules:
  0.0 310.1 jit_solution(14810466515378491795)
XLA Ops:
  6.5 5.3 %pad_maximum_fusion.28 = (f32[4,256,1,128]{3,2,1,0:T(1,128)}, f32[4,256,1,128]{3,2,1,0:T(1,128)}) fusion(f32[1,256,8,128]{3,2,1,0:T(8,128)} %param.5, f32[3,256,8,128]{3,2,1,0:T(8,128)} %bitcast.113), kind=kLoop, calls=%fused_computation.111 | loop fusion | flops 262144 | bytes 5242880 | tf_op jit(solution)/shard_map/slice | solution.py:24
  11.9 5.9 %collective-permute-start.1 = (f32[4,256,1,128]{3,2,1,0:T(1,128)}, f32[4,256,1,128]{3,2,1,0:T(1,128)}, u32[]{:S(2)}, u32[]{:S(2)}) collective-permute-start(f32[4,256,1,128]{3,2,1,0:T(1,128)} %get-tuple-element.8), channel_id=1, source_target_pairs={{1,0},{2,1},{3,2},{4,3},{5,4},{6,5},{7,6},{8,7},{9,8},{10,9},{11,1... | collective-permute-start | bytes 1572872 | tf_op jit(solution)/shard_map/ppermute | solution.py:29
  19.3 1.0 sine_negate_fusion
  20.4 0.9 pad_maximum_fusion.29
  21.3 3.4 %collective-permute-done = f32[4,256,1,128]{3,2,1,0:T(1,128)} collective-permute-done((f32[4,256,1,128]{3,2,1,0:T(1,128)}, f32[4,256,1,128]{3,2,1,0:T(1,128)}, u32[]{:S(2)}, u32[]{:S(2)}) %collective-permute-start) | collective-permute-done | bytes 524320 | tf_op jit(solution)/shard_map/ppermute | solution.py:27
  24.8 2.9 pad_maximum_fusion
  28.3 0.8 copy-done.2
  29.1 2.3 fusion.17
  31.4 5.0 %fusion.3 = f32[3,256,10,128]{3,2,1,0:T(8,128)S(1)} fusion(f32[4,256,10,128]{3,2,1,0:T(8,128)S(1)} %pad_maximum_fusion, f32[4,256,1,128]{3,2,1,0:T(1,128)} %collective-permute-done.1, f32[4,256,1,128]{3,2,1,0:T(1,128)} %collective-permute-done, f32[1,256,8,128]{3,2,1,0:T(8,128)S(1)} %copy-done.2, f32[3,256,8,128]{3,2,1,0:T(8,128)S(1)} %bitcast.116, ...), kind=kLoop, calls=%fused_computation.10 | loop fusion | flops 5898240 | bytes 18334720 | tf_op jit(solution)/shard_map/mul | solution.py:38
  36.4 2.6 copy-done.1
  39.1 1.9 fusion.12
  41.0 1.6 fusion.13
  42.6 5.9 %fusion = f32[3,256,10,127]{3,2,1,0:T(8,128)} fusion(f32[4,256,10,128]{3,2,1,0:T(8,128)S(1)} %pad_maximum_fusion, f32[256,10,127]{2,1,0:T(8,128)} %fusion.12), kind=kLoop, calls=%fused_computation.2 | loop fusion | flops 1950720 | bytes 13004800 | tf_op jit(solution)/shard_map/mul | solution.py:44
  48.6 5.0 %fusion.2 = f32[3,256,9,128]{3,2,1,0:T(8,128)} fusion(f32[4,256,1,128]{3,2,1,0:T(1,128)} %collective-permute-done, f32[1,256,8,128]{3,2,1,0:T(8,128)S(1)} %copy-done.2, f32[3,256,8,128]{3,2,1,0:T(8,128)S(1)} %bitcast.117, f32[4,256,1,128]{3,2,1,0:T(1,128)} %collective-permute-done.1, f32[256,9,128]{2,1,0:T(8,128)} %fusion.13), kind=kLoop, calls=%fused_computation.5 | loop fusion | flops 5308416 | bytes 9961472 | tf_op jit(solution)/shard_map/mul | solution.py:41
  53.6 10.6 %fusion.5 = f32[3,256,8,128]{3,2,1,0:T(8,128)S(1)} fusion(f32[3,256,10,127]{3,2,1,0:T(8,128)} %fusion, f32[3,256,9,128]{3,2,1,0:T(8,128)} %fusion.2, f32[3,256,10,128]{3,2,1,0:T(8,128)} %copy-done.1, f32[3,255,10,128]{3,2,1,0:T(8,128)S(1)} %slice-done, f32[3,1,10,128]{3,2,1,0:T(8,128)S(1)} %slice-done.1, f32[1,3,256,8,128]{4,3,2,1,0:T(8,128)S(1)} %copy-done), kind=kLoop, calls=%fused_computation.19 | loop fusion | flops 5505024 | bytes 23562240 | tf_op jit(solution)/shard_map/add | solution.py:49
  64.4 1.1 copy-done.10
  65.6 1.1 copy-done.3
  66.8 1.0 copy-done.4
  67.9 57.9 %all-reduce.4.cloned.1.call-done = f32[3,32,8,128]{3,2,1,0:T(8,128)} async-done(((f32[3,32,8,128]{3,2,1,0:T(8,128)}), f32[3,32,8,128]{3,2,1,0:T(8,128)}) %all-reduce.4.cloned.1.call-update) | async-done | bytes 393232 | tf_op jit(solution)/shard_map/psum | solution.py:17
  125.8 1.2 add_dynamic-update-slice_fusion
  127.9 1.0 collective-permute-start.3
  128.9 1.5 collective-permute-done.2
  130.4 6.4 %collective-permute-done.3 = f32[256,1,128]{2,1,0:T(1,128)S(1)} collective-permute-done((f32[256,1,128]{2,1,0:T(1,128)S(1)}, f32[256,1,128]{2,1,0:T(1,128)S(1)}, u32[]{:S(2)}, u32[]{:S(2)}) %collective-permute-start.3) | collective-permute-done | bytes 131104 | tf_op jit(solution)/shard_map/ppermute | solution.py:27
  136.8 2.9 fusion.39
  139.7 2.4 reshape.309
  142.1 2.5 copy.16
  144.6 3.3 %fusion.114 = f32[2,256,8,128]{3,1,2,0:T(8,128)S(1)} fusion(f32[2,256,256,1]{2,1,3,0:T(8,128)} %bitcast.125, f32[8,128,256,1]{2,1,0,3:T(8,128)} %bitcast.123), kind=kOutput, calls=%fused_computation.189 | convolution fusion | flops 1610612736 | bytes 3670016 | tf_op jit(solution)/shard_map/dot_general | solution.py:131
  147.9 2.5 copy.17
  150.4 4.9 %all-to-all-start = ((f32[2,256,8,128]{3,2,0,1:T(8,128)}), f32[2,256,8,128]{3,2,0,1:T(8,128)}, u32[]{:S(2)}, u32[]{:S(2)}) async-start(f32[2,256,8,128]{3,2,0,1:T(8,128)} %copy.17), calls=%async_computation | async-start | bytes 4194304 | tf_op jit(solution)/shard_map/all_to_all | solution.py:134
  155.5 1.0 fusion.83
  156.5 1.0 fusion.80
  157.6 1.4 fusion.62
  159.1 1.4 and_select_fusion
  160.5 43.4 %all-to-all-done = f32[2,256,8,128]{3,2,0,1:T(8,128)} async-done(((f32[2,256,8,128]{3,2,0,1:T(8,128)}), f32[2,256,8,128]{3,2,0,1:T(8,128)}, u32[]{:S(2)}, u32[]{:S(2)}) %all-to-all-start) | async-done | bytes 2097184 | tf_op jit(solution)/shard_map/all_to_all | solution.py:134
  203.9 8.7 %fusion.21 = f32[8,128,2,256,1]{3,1,4,2,0:T(8,128)S(1)} fusion(f32[1,2,256,256]{3,2,1,0:T(8,128)} %get-tuple-element.30, f32[1,2,256,256]{3,2,1,0:T(8,128)} %get-tuple-element.33, f32[2,8,32,8,128]{4,3,0,1,2:T(8,128)} %bitcast.20), kind=kOutput, calls=%fused_computation.46 | convolution fusion | flops 3221487616 | bytes 5242880 | tf_op jit(solution)/shard_map/abky,bxyz->axkz/dot_general | solution.py:110
  212.6 5.0 %fusion.20 = f32[2,8,256,128]{2,3,0,1:T(8,128)} fusion(f32[8,128,2,256,1]{3,1,4,2,0:T(8,128)S(1)} %fusion.21, f32[1,2,256,256]{3,2,1,0:T(8,128)S(1)} %copy-done.9, f32[1,2,256,256]{3,2,1,0:T(8,128)S(1)} %copy-done.8, f32[8,256,128]{1,2,0:T(8,128)S(1)} %copy-done.5), kind=kOutput, calls=%fused_computation.45 | convolution fusion | flops 3222536192 | bytes 6291456 | tf_op jit(solution)/shard_map/abky,bxyz->axkz/dot_general | solution.py:115
  217.7 4.2 %copy.21 = f32[2,8,256,128]{3,0,1,2:T(2,128)} copy(f32[2,8,256,128]{2,3,0,1:T(8,128)} %fusion.20) | data formatting | bytes 4194304 | tf_op jit(solution)/shard_map/div | solution.py:115
  221.8 5.8 %all-to-all-start.1 = ((f32[2,8,256,128]{3,0,1,2:T(2,128)}), f32[2,8,256,128]{3,0,1,2:T(2,128)}, u32[]{:S(2)}, u32[]{:S(2)}) async-start(f32[2,8,256,128]{3,0,1,2:T(2,128)} %copy.21), calls=%async_computation.1 | async-start | bytes 4194304 | tf_op jit(solution)/shard_map/all_to_all | solution.py:139
  227.6 48.7 %all-to-all-done.1 = f32[2,8,256,128]{3,0,1,2:T(2,128)} async-done(((f32[2,8,256,128]{3,0,1,2:T(2,128)}), f32[2,8,256,128]{3,0,1,2:T(2,128)}, u32[]{:S(2)}, u32[]{:S(2)}) %all-to-all-start.1) | async-done | bytes 2097184 | tf_op jit(solution)/shard_map/all_to_all | solution.py:139
  276.4 2.3 copy.45
  279.6 3.1 %fusion.25 = f32[256,1024]{1,0:T(8,128)} fusion(f32[64,8,8,128]{3,2,1,0:T(8,128)S(1)} %bitcast.121, f32[256,256]{1,0:T(8,128)S(1)} %get-tuple-element.35, f32[256,256]{1,0:T(8,128)S(1)} %copy-done.7), kind=kOutput, calls=%fused_computation.51 | convolution fusion | flops 1611005952 | bytes 3670016 | tf_op jit(solution)/shard_map/dot_general | solution.py:142
  282.7 2.4 reshape.311
  285.1 2.4 fusion.88
  288.2 3.3 %collective-permute-start.4 = (f32[256,1,128]{2,1,0:T(1,128)S(1)}, f32[256,1,128]{2,1,0:T(1,128)S(1)}, u32[]{:S(2)}, u32[]{:S(2)}) collective-permute-start(f32[256,1,128]{2,1,0:T(1,128)S(1)} %get-tuple-element.21), channel_id=1, source_target_pairs={{1,0},{2,1},{3,2},{4,3},{5,4},{6,5},{7,6},{8,7},{9,8},{10,9},{11,1... | collective-permute-start | bytes 393224 | tf_op jit(solution)/shard_map/ppermute | solution.py:29
  291.7 2.3 collective-permute-done.4
  294.0 5.8 %collective-permute-done.5 = f32[256,1,128]{2,1,0:T(1,128)S(1)} collective-permute-done((f32[256,1,128]{2,1,0:T(1,128)S(1)}, f32[256,1,128]{2,1,0:T(1,128)S(1)}, u32[]{:S(2)}, u32[]{:S(2)}) %collective-permute-start.5) | collective-permute-done | bytes 131104 | tf_op jit(solution)/shard_map/ppermute | solution.py:27
  299.8 1.2 fusion.34
  301.0 2.0 fusion.8
  (55 shorter events, 5.0 us)
Async XLA Ops:
  6.5 11.9 %copy-start = (f32[1,3,256,8,128]{4,3,2,1,0:T(8,128)S(1)}, f32[1,3,256,8,128]{4,3,2,1,0:T(8,128)}, u32[]{:S(2)}) copy-start(f32[1,3,256,8,128]{4,3,2,1,0:T(8,128)} %param.4) | copy-start | bytes 9437188
  6.5 119.3 %all-reduce.4.cloned.1.call-start = ((), (), s32[]{:S(2)}) async-start(), calls=%async_computation.2 | async-start | bytes 786432 | tf_op jit(solution)/shard_map/psum | solution.py:17
  11.9 12.8 %collective-permute-start = (f32[4,256,1,128]{3,2,1,0:T(1,128)}, f32[4,256,1,128]{3,2,1,0:T(1,128)}, u32[]{:S(2)}, u32[]{:S(2)}) collective-permute-start(f32[4,256,1,128]{3,2,1,0:T(1,128)} %get-tuple-element.7), channel_id=1, source_target_pairs={{0,1},{1,2},{2,3},{3,4},{4,5},{5,6},{6,7},{7,8},{8,9},{9,10},{10,1... | collective-permute-start | bytes 1572872 | tf_op jit(solution)/shard_map/ppermute | solution.py:27
  11.9 12.9 %collective-permute-start.1 = (f32[4,256,1,128]{3,2,1,0:T(1,128)}, f32[4,256,1,128]{3,2,1,0:T(1,128)}, u32[]{:S(2)}, u32[]{:S(2)}) collective-permute-start(f32[4,256,1,128]{3,2,1,0:T(1,128)} %get-tuple-element.8), channel_id=1, source_target_pairs={{1,0},{2,1},{3,2},{4,3},{5,4},{6,5},{7,6},{8,7},{9,8},{10,9},{11,1... | collective-permute-start | bytes 1572872 | tf_op jit(solution)/shard_map/ppermute | solution.py:29
  20.4 4.3 %copy-start.6 = (f32[256,256]{1,0:T(8,128)}, f32[256,256]{1,0:T(8,128)S(1)}, u32[]{:S(2)}) copy-start(f32[256,256]{1,0:T(8,128)S(1)} %get-tuple-element.36) | copy-start | bytes 786436
  27.9 1.2 copy-start.2
  36.4 2.6 copy-start.1
  48.6 5.0 %slice-start = ((f32[3,256,10,128]{3,2,1,0:T(8,128)}), f32[3,255,10,128]{3,2,1,0:T(8,128)S(1)}, s32[]{:S(2)}) async-start(f32[3,256,10,128]{3,2,1,0:T(8,128)} %copy-done.1), calls=%async_computation.3 | async-start | bytes 12533760 | tf_op jit(solution)/shard_map/jit(_roll_static)/slice | solution.py:39
  48.6 5.0 %slice-start.1 = ((f32[3,256,10,128]{3,2,1,0:T(8,128)}), f32[3,1,10,128]{3,2,1,0:T(8,128)S(1)}, s32[]{:S(2)}) async-start(f32[3,256,10,128]{3,2,1,0:T(8,128)} %copy-done.1), calls=%async_computation.4 | async-start | bytes 49152 | tf_op jit(solution)/shard_map/jit(_roll_static)/slice | solution.py:39
  64.2 1.2 copy-start.10
  65.4 1.3 copy-start.3
  66.8 1.0 copy-start.4
  127.8 2.6 collective-permute-start.2
  127.9 8.9 %collective-permute-start.3 = (f32[256,1,128]{2,1,0:T(1,128)S(1)}, f32[256,1,128]{2,1,0:T(1,128)S(1)}, u32[]{:S(2)}, u32[]{:S(2)}) collective-permute-start(f32[256,1,128]{2,1,0:T(1,128)S(1)} %get-tuple-element.26), channel_id=1, source_target_pairs={{0,1},{1,2},{2,3},{3,4},{4,5},{5,6},{6,7},{7,8},{8,9},{9,10},{10,1... | collective-permute-start | bytes 393224 | tf_op jit(solution)/shard_map/ppermute | solution.py:27
  150.4 53.5 %all-to-all-start = ((f32[2,256,8,128]{3,2,0,1:T(8,128)}), f32[2,256,8,128]{3,2,0,1:T(8,128)}, u32[]{:S(2)}, u32[]{:S(2)}) async-start(f32[2,256,8,128]{3,2,0,1:T(8,128)} %copy.17), calls=%async_computation | async-start | bytes 4194304 | tf_op jit(solution)/shard_map/all_to_all | solution.py:134
  203.9 8.7 %copy-start.5 = (f32[8,256,128]{1,2,0:T(8,128)S(1)}, f32[8,256,128]{1,2,0:T(8,128)}, u32[]{:S(2)}) copy-start(f32[8,256,128]{1,2,0:T(8,128)} %and_select_fusion) | copy-start | bytes 3145732
  203.9 8.7 %copy-start.8 = (f32[1,2,256,256]{3,2,1,0:T(8,128)S(1)}, f32[1,2,256,256]{3,2,1,0:T(8,128)}, u32[]{:S(2)}) copy-start(f32[1,2,256,256]{3,2,1,0:T(8,128)} %get-tuple-element.29) | copy-start | bytes 1572868
  203.9 8.7 %copy-start.9 = (f32[1,2,256,256]{3,2,1,0:T(8,128)S(1)}, f32[1,2,256,256]{3,2,1,0:T(8,128)}, u32[]{:S(2)}) copy-start(f32[1,2,256,256]{3,2,1,0:T(8,128)} %get-tuple-element.34) | copy-start | bytes 1572868
  221.8 54.5 %all-to-all-start.1 = ((f32[2,8,256,128]{3,0,1,2:T(2,128)}), f32[2,8,256,128]{3,0,1,2:T(2,128)}, u32[]{:S(2)}, u32[]{:S(2)}) async-start(f32[2,8,256,128]{3,0,1,2:T(2,128)} %copy.21), calls=%async_computation.1 | async-start | bytes 4194304 | tf_op jit(solution)/shard_map/all_to_all | solution.py:139
  278.6 1.0 copy-start.7
  288.2 5.8 %collective-permute-start.4 = (f32[256,1,128]{2,1,0:T(1,128)S(1)}, f32[256,1,128]{2,1,0:T(1,128)S(1)}, u32[]{:S(2)}, u32[]{:S(2)}) collective-permute-start(f32[256,1,128]{2,1,0:T(1,128)S(1)} %get-tuple-element.21), channel_id=1, source_target_pairs={{1,0},{2,1},{3,2},{4,3},{5,4},{6,5},{7,6},{8,7},{9,8},{10,9},{11,1... | collective-permute-start | bytes 393224 | tf_op jit(solution)/shard_map/ppermute | solution.py:29
  291.5 8.3 %collective-permute-start.5 = (f32[256,1,128]{2,1,0:T(1,128)S(1)}, f32[256,1,128]{2,1,0:T(1,128)S(1)}, u32[]{:S(2)}, u32[]{:S(2)}) collective-permute-start(f32[256,1,128]{2,1,0:T(1,128)S(1)} %get-tuple-element.22), channel_id=1, source_target_pairs={{0,1},{1,2},{2,3},{3,4},{4,5},{5,6},{6,7},{7,8},{8,9},{9,10},{10,1... | collective-permute-start | bytes 393224 | tf_op jit(solution)/shard_map/ppermute | solution.py:27
Sparse Core Ops, SparseCore 0:
  19.4 106.3 all-reduce.3
where the time goes:
time: 313 us; the launch traced here: 310 us
  waiting for transfers between devices  170 us (54%)
  other arithmetic  53.6 us (17%)
  local copies, waits for them, and re-layouts  25.9 us (8%)
  matrix products  25.4 us (8%)
  starting transfers between devices  21 us (7%)
  between operations  14.6 us (5%)
    psum x1, waiting for transfers between devices, broadcast(): return lax.psum(kept, axis)  57.9 us
    all_to_all x1, waiting for transfers between devices, poisson_slab(): lax.all_to_all(back, 'slab', split_axis=2, concat_axis=1, tiled=True)  48.7 us
    all_to_all x1, waiting for transfers between devices, poisson_slab(): lax.all_to_all(stacked, 'slab', split_axis=1, concat_axis=2, tiled=True)  43.4 us
    ppermute x3, waiting for transfers between devices, with_halo(): lax.ppermute(tail, axis, [(i, (i + 1) % count) for i in range(count)])  15.6 us
    add x1, other arithmetic, diffuse(): fields[..., 1:-1, :] + across_x[..., 1:-1, :] + across_y  10.6 us
    ppermute x3, starting transfers between devices, with_halo(): lax.ppermute(head, axis, [((i + 1) % count, i) for i in range(count)])  9.33 us
    dot_general x1, matrix products, forward_y(): return jnp.einsum('abky,bxyz->axkz', mixing, spectral, precision=highest)  8.65 us
    mul x2, other arithmetic, diffuse(): flux_x = faces_x * (jnp.roll(fields, -1, -3) - fields)  7.32 us
  transfers between devices with their start and end apart: 9, of which 9 were waited for; matrix products, arithmetic and copies ran while one was open for 14% of the time, Pallas kernels for 0%

commit v1 on v0

v1 whole, which is shorter than its diff:
```python
import functools
import math

import jax
import jax.numpy as jnp
import ml_dtypes
import numpy as np
from jax import lax
from jax.experimental import pallas as pl
from jax.experimental.pallas import tpu as pltpu
from jax.sharding import PartitionSpec as P

FR = 32
NX = 256
NY = 256
NZ = 128
SLABS = 32
ROWS = 8
EXT = ROWS + 2
CELLS = NX * ROWS
DRAG = 0.5 * 0.75
VMEM_LIMIT = 48 * 2**20


def split_bf16(table):
    high = table.astype(np.float32).astype(ml_dtypes.bfloat16)
    low = (table - high.astype(np.float64)).astype(np.float32).astype(ml_dtypes.bfloat16)
    return high, low


def x_table():
    half = NX // 2
    x = np.arange(NX)
    wave = np.concatenate([np.arange(half + 1), np.arange(1, half)])
    angle = 2.0 * math.pi / NX * ((wave[:, None] * x[None, :]) % NX)
    basis = np.where((np.arange(NX) <= half)[:, None], np.cos(angle), np.sin(angle))
    weight = np.where((wave == 0) | (wave == half), 1.0, 2.0) / NX
    return basis * np.sqrt(weight)[:, None], wave


def z_table():
    m = np.arange(NZ)
    angle = math.pi / (2.0 * NZ) * ((m[:, None] * (2 * m[None, :] + 1)) % (4 * NZ))
    weight = np.where(m == 0, 1.0, 2.0) / NZ
    return np.cos(angle) * np.sqrt(weight)[:, None]


def line_tables():
    wave = x_table()[1]
    minus_x = 4.0 * np.sin(math.pi * wave / NX) ** 2
    minus_z = 4.0 * np.sin(math.pi * np.arange(NZ) / (2.0 * NZ)) ** 2
    total = minus_x[:, None] + minus_z[None, :]
    theta = 2.0 * np.arcsinh(np.sqrt(total) / 2.0)
    zero = total == 0.0
    theta = np.where(zero, 1.0, theta)
    mu = np.exp(-theta)
    scale = -1.0 / (2.0 * np.sinh(theta))
    wrap = 1.0 / (-np.expm1(-NY * theta))
    tables = [mu, np.exp(theta), scale, np.exp(-ROWS * theta), wrap]
    return [np.where(zero, 0.0, t).astype(np.float32) for t in tables]


def dot3(a_high, a_low, b_high, b_low):
    dot = functools.partial(jnp.dot, preferred_element_type=jnp.float32)
    return dot(a_high, b_high) + (dot(a_high, b_low) + dot(a_low, b_high))


def parts(value):
    high = value.astype(jnp.bfloat16)
    low = (value - high.astype(jnp.float32)).astype(jnp.bfloat16)
    return high, low


def call(body, outs, name, scratch=(), in_specs=None, flops=0, nbytes=0, **kw):
    return pl.pallas_call(
        body,
        out_shape=[jax.ShapeDtypeStruct(s, jnp.float32) for s in outs],
        in_specs=in_specs,
        out_specs=[pl.BlockSpec(memory_space=pltpu.VMEM)] * len(outs),
        scratch_shapes=list(scratch),
        compiler_params=pltpu.CompilerParams(vmem_limit_bytes=VMEM_LIMIT),
        cost_estimate=pl.CostEstimate(flops=flops, bytes_accessed=nbytes, transcendentals=0),
        name=name,
        **kw,
    )


VM = pl.BlockSpec(memory_space=pltpu.VMEM)
SM = pl.BlockSpec(memory_space=pltpu.SMEM)


def every8(first, count=NX):
    return pl.ds(first, count, stride=ROWS)


def edges_kernel(start_ref, vel_ref, visc_ref, low_ref, high_ref, fringe_ref):
    for row, out in ((0, low_ref), (ROWS - 1, high_ref)):
        for c in range(3):
            out[c] = vel_ref[c, every8(row), :]
        out[3] = visc_ref[every8(row), :]
    first = pl.multiple_of(start_ref[0] * ROWS, ROWS)
    for c in range(3):
        fringe_ref[pl.ds(c * FR * ROWS, FR * ROWS), :] = vel_ref[c, pl.ds(first, FR * ROWS), :]


def iotas():
    return (
        lax.broadcasted_iota(jnp.int32, (ROWS, NZ), 0),
        lax.broadcasted_iota(jnp.int32, (ROWS, NZ), 1),
    )


def tile(x):
    return pl.ds(pl.multiple_of(x * ROWS, ROWS), ROWS)


def diffuse_kernel(vel_ref, visc_ref, turb_ref, own_low, own_high, prev_ref, next_ref, out_ref, rim):
    del own_low, own_high
    for c in range(4):
        rim[c, every8(0), :] = prev_ref[c]
        rim[c, every8(ROWS - 1), :] = next_ref[c]
    row, lane = iotas()
    first_row, last_row = row == 0, row == ROWS - 1
    first_lane, last_lane = lane == 0, lane == NZ - 1

    def fields_at(x):
        return [vel_ref[c, tile(x), :] for c in range(3)], visc_ref[tile(x), :]

    def flux(nu_sum, a, b):
        return nu_sum * (b - a)

    def step(x, carry):
        now, nu, back = carry
        ahead, nu_ahead = fields_at(lax.rem(x + 1, NX))
        nu_rim = rim[3, tile(x), :]
        half = 0.5 * nu
        sum_x = half + 0.5 * nu_ahead
        half_rim = half + 0.5 * nu_rim
        sum_y = jnp.where(last_row, half_rim, half + pltpu.roll(half, ROWS - 1, 0))
        sum_z = jnp.where(last_lane, 0.0, half + pltpu.roll(half, NZ - 1, 1))
        fluxes = []
        for c in range(3):
            u = now[c]
            edge = rim[c, tile(x), :]
            flux_x = sum_x * (ahead[c] - u)
            flux_y = sum_y * (jnp.where(last_row, edge, pltpu.roll(u, ROWS - 1, 0)) - u)
            down_y = jnp.where(first_row, half_rim * (u - edge), pltpu.roll(flux_y, 1, 0))
            flux_z = sum_z * (pltpu.roll(u, NZ - 1, 1) - u)
            down_z = pltpu.roll(flux_z, 1, 1)
            new = u + (flux_x - back[c]) + (flux_y - down_y) + (flux_z - down_z)
            if c == 0:
                disc = turb_ref[tile(x), :].astype(jnp.float32)
                new = new - DRAG * disc * new * jnp.abs(new)
            out_ref[c, tile(x), :] = new
            fluxes.append(flux_x)
        return ahead, nu_ahead, fluxes

    del first_lane
    last, nu_last = fields_at(NX - 1)
    now, nu = fields_at(0)
    sum_x = 0.5 * nu_last + 0.5 * nu
    back = [flux(sum_x, last[c], now[c]) for c in range(3)]
    lax.fori_loop(0, NX, step, (now, nu, back), unroll=4)


def centred_z(value, first_lane, last_lane):
    up = jnp.where(last_lane, value, pltpu.roll(value, NZ - 1, 1))
    down = jnp.where(first_lane, value, pltpu.roll(value, 1, 1))
    return up - down


def forward_kernel(
    start_ref, field_ref, q0, q1, q2, q3, profile_ref, xh, xl, zh, zl, mu_ref,
    out_ref, hat_ref, pay_ref, rim_ref, fringe, div, modes,
):
    me = lax.axis_index("sim")
    active = jnp.where(me == 0, 0.0, 1.0).astype(jnp.float32)
    quarter = 3 * FR * ROWS // 4
    for k, part in enumerate((q0, q1, q2, q3)):
        at = lax.rem(lax.rem(me, 4) + 4 - k, 4)
        fringe[pl.ds(pl.multiple_of(at * quarter, ROWS), quarter), :] = part[...]
    row, lane = iotas()
    first_row, last_row = row == 0, row == ROWS - 1
    first_lane, last_lane = lane == 0, lane == NZ - 1

    for c in range(3):
        out_ref[c] = field_ref[c]
    start = start_ref[0]

    def blend(i, _):
        weight = profile_ref[i] * active
        for c in range(3):
            old = out_ref[c, tile(start + i), :]
            out_ref[c, tile(start + i), :] = old + weight * (fringe[tile(c * FR + i), :] - old)
        return 0

    lax.fori_loop(0, FR, blend, 0, unroll=4)

    def source(x, carry):
        behind, now = carry
        ahead = out_ref[0, tile(lax.rem(x + 1, NX)), :]
        v = out_ref[1, tile(x), :]
        w = out_ref[2, tile(x), :]
        up = jnp.where(last_row, 0.0, pltpu.roll(v, ROWS - 1, 0))
        down = jnp.where(first_row, 0.0, pltpu.roll(v, 1, 0))
        div[tile(x), :] = 0.5 * ((ahead - behind) + (up - down) + centred_z(w, first_lane, last_lane))
        return now, ahead

    lax.fori_loop(0, NX, source, (out_ref[0, tile(NX - 1), :], out_ref[0, tile(0), :]), unroll=4)

    z_high, z_low = zh[...], zl[...]
    for block in range(8):
        rows = pl.ds(block * NX, NX)
        modes[rows, :] = dot3(*parts(div[rows, :]), z_high, z_low)
    low = out_ref[1, every8(0), :]
    high = out_ref[1, every8(ROWS - 1), :]
    rim_ref[0] = low
    rim_ref[1] = high
    low = dot3(*parts(0.5 * low), z_high, z_low)
    high = dot3(*parts(-0.5 * high), z_high, z_low)
    x_high, x_low = xh[...], xl[...]
    for r in range(0, EXT, 2):
        pair = []
        for k in (r, r + 1):
            pair.append(low if k == 0 else high if k == EXT - 1 else modes[every8(k - 1), :])
        both = dot3(x_high, x_low, *parts(jnp.concatenate(pair, 1)))
        hat_ref[r] = both[:, :NZ]
        hat_ref[r + 1] = both[:, NZ:]

    origin = (row == 0) & (lane == 0)

    def sums(block, at):
        mu = mu_ref[at, :]
        rows = [hat_ref[r, at, :] for r in range(EXT)]
        right = rows[0]
        for value in rows[1:]:
            right = mu * right + value
        left = rows[-1]
        for value in rows[-2::-1]:
            left = mu * left + value
        return right, left, rows

    def weigh(block, _):
        right, left, _ = sums(block, tile(block))
        pay_ref[block, 0] = right
        pay_ref[block, 1] = left
        return 0

    lax.fori_loop(1, NX // ROWS, weigh, 0, unroll=2)
    right, left, rows = sums(0, tile(0))
    moment0 = functools.reduce(jnp.add, rows)
    moment1 = functools.reduce(jnp.add, [float(r - 1) * rows[r] for r in range(EXT) if r != 1])
    pay_ref[0, 0] = jnp.where(origin, moment0, right)
    pay_ref[0, 1] = jnp.where(origin, moment1, left)


def far_kernel(pay_ref, step_ref, wrap_ref, out_ref):
    slab = lax.axis_index("slab")
    step = step_ref[tile(slab), :]
    wrap = wrap_ref[tile(slab), :]
    row, lane = iotas()
    origin = (row == 0) & (lane == 0) & (slab == 0)
    right = jnp.zeros((ROWS, NZ), jnp.float32)
    left = right
    total0 = right
    total1 = right
    ramp = right
    for s in range(SLABS):
        right = step * right + pay_ref[s, 0]
        left = step * left + pay_ref[SLABS - 1 - s, 1]
        total0 = total0 + pay_ref[s, 0]
        total1 = total1 + pay_ref[s, 1]
        ramp = ramp + float((SLABS - s) % SLABS) * pay_ref[s, 0]
    right = right * wrap
    left = left * wrap
    for s in range(SLABS):
        m0, m1 = pay_ref[s, 0], pay_ref[s, 1]
        if s:
            ramp = ramp + total0 - float(SLABS) * m0
        slope = 0.5 * (total0 - m0) - (ROWS / NY) * ramp + (1.0 / NY) * (total1 - m1)
        out_ref[s, 0] = jnp.where(origin, slope, right)
        right = step * right + m0
        t = SLABS - 1 - s
        curve = (-0.5 / NY) * (total0 - pay_ref[t, 0])
        out_ref[t, 1] = jnp.where(origin, curve, left)
        left = step * left + pay_ref[t, 1]


def green0(j):
    return 0.5 * j - j * j / (2.0 * NY)


def final_kernel(
    field_ref, hat_ref, ret_ref, prev_ref, next_ref, xh, xl, zh, zl, mu_ref, inv_ref, scale_ref,
    out_ref, press, field, rim,
):
    row, lane = iotas()
    first_row, last_row = row == 0, row == ROWS - 1
    first_lane, last_lane = lane == 0, lane == NZ - 1
    origin = (row == 0) & (lane == 0)

    def solve(block, at):
        mu, inv, scale = mu_ref[at, :], inv_ref[at, :], scale_ref[at, :]
        rows = [hat_ref[r, at, :] for r in range(EXT)]
        below = [ret_ref[block, 0] * inv + rows[0]]
        for value in rows[1:]:
            below.append(mu * below[-1] + value)
        above = [ret_ref[block, 1] * inv]
        for value in rows[:0:-1]:
            above.append(mu * (above[-1] + value))
        above.reverse()
        return [scale * (a + b) for a, b in zip(below, above)], rows

    def line(block, _):
        at = tile(block)
        values, _ = solve(block, at)
        for r in range(EXT):
            press[r, at, :] = values[r]
        return 0

    lax.fori_loop(1, NX // ROWS, line, 0, unroll=2)
    at = pl.ds(0, ROWS)
    values, rows = solve(0, at)
    slope, curve = ret_ref[0, 0], ret_ref[0, 1]
    for r in range(EXT):
        y = float(r - 1)
        mean_line = slope * y + curve * (y * y)
        for k in range(EXT):
            if k != r:
                mean_line = mean_line + green0(float(abs(r - k))) * rows[k]
        press[r, at, :] = jnp.where(origin, mean_line, values[r])

    x_high, x_low = xh[...], xl[...]
    z_high, z_low = zh[...], zl[...]
    for r in range(0, EXT, 2):
        pair = jnp.concatenate([press[r], press[r + 1]], 1)
        both = dot3(x_high, x_low, *parts(pair))
        for k in (r, r + 1):
            plane = both[:, :NZ] if k == r else both[:, NZ:]
            plane = dot3(*parts(plane), z_high, z_low)
            if k == 0:
                rim[every8(0), :] = plane - 0.5 * prev_ref[...]
            elif k == EXT - 1:
                rim[every8(ROWS - 1), :] = plane + 0.5 * next_ref[...]
            else:
                field[every8(k - 1), :] = plane

    def project(x, carry):
        behind, now = carry
        ahead = field[tile(lax.rem(x + 1, NX)), :]
        edge = rim[tile(x), :]
        up = jnp.where(last_row, edge, pltpu.roll(now, ROWS - 1, 0))
        down = jnp.where(first_row, edge, pltpu.roll(now, 1, 0))
        grads = (ahead - behind, up - down, centred_z(now, first_lane, last_lane))
        for c in range(3):
            out_ref[c, tile(x), :] = field_ref[c, tile(x), :] - 0.5 * grads[c]
        return now, ahead

    lax.fori_loop(0, NX, project, (field[tile(NX - 1), :], field[tile(0), :]), unroll=4)


def fringe_quarters(fringe):
    quarter = fringe.shape[0] // 4
    me = lax.axis_index("sim")
    piece = [fringe[k * quarter : (k + 1) * quarter] for k in range(4)]
    mine = piece[0]
    for k in (1, 2, 3):
        came = lax.ppermute(piece[k], "sim", [(0, k)])
        mine = jnp.where(me == k, came, mine)
    came = lax.ppermute(mine, "sim", [(i, i + 4) for i in range(4)])
    mine = jnp.where(me >= 4, came, mine)
    quarters = [mine]
    for k in (1, 2, 3):
        pairs = [(4 * z + i, 4 * z + (i + k) % 4) for z in range(2) for i in range(4)]
        quarters.append(lax.ppermute(mine, "sim", pairs))
    return quarters


def local(velocity, viscosity, turbines, fringe_start):
    vel = velocity.reshape(3, CELLS, NZ)
    visc = viscosity.reshape(CELLS, NZ)
    turb = turbines.reshape(CELLS, NZ)
    x_basis = x_table()[0]
    z_basis = z_table()
    to_x, from_x = split_bf16(x_basis), split_bf16(x_basis.T)
    to_z, from_z = split_bf16(z_basis.T), split_bf16(z_basis)
    mu, inv, scale, step, wrap = line_tables()
    profile = (np.sin(math.pi * (np.arange(FR) + 0.5) / FR) ** 2).astype(np.float32)
    upward = [(i, (i + 1) % SLABS) for i in range(SLABS)]
    downward = [((i + 1) % SLABS, i) for i in range(SLABS)]

    low, high, fringe = call(
        edges_kernel,
        [(4, NX, NZ), (4, NX, NZ), (3 * FR * ROWS, NZ)],
        "edges",
        in_specs=[SM, VM, VM],
        nbytes=6 * 2**20,
    )(fringe_start, vel, visc)
    prev = lax.ppermute(high, "slab", upward)
    following = lax.ppermute(low, "slab", downward)
    quarters = fringe_quarters(fringe)
    (fields,) = call(
        diffuse_kernel,
        [(3, CELLS, NZ)],
        "diffuse",
        in_specs=[VM] * 7,
        scratch=[pltpu.VMEM((4, CELLS, NZ), jnp.float32)],
        flops=2**26,
        nbytes=12 * 2**20,
    )(vel, visc, turb, low, high, prev, following)
    fields, hat, pay, rims = call(
        forward_kernel,
        [(3, CELLS, NZ), (EXT, NX, NZ), (SLABS, 2, ROWS, NZ), (2, NX, NZ)],
        "forward",
        in_specs=[SM] + [VM] * 5 + [SM] + [VM] * 5,
        scratch=[
            pltpu.VMEM((3 * FR * ROWS, NZ), jnp.float32),
            pltpu.VMEM((CELLS, NZ), jnp.float32),
            pltpu.VMEM((CELLS, NZ), jnp.float32),
        ],
        flops=2**30,
        nbytes=10 * 2**20,
    )(fringe_start, fields, *quarters, profile, *to_x, *to_z, mu)
    v_prev = lax.ppermute(rims[1], "slab", upward)
    v_next = lax.ppermute(rims[0], "slab", downward)
    pay = lax.all_to_all(pay, "slab", split_axis=0, concat_axis=0, tiled=True)
    (ret,) = call(
        far_kernel,
        [(SLABS, 2, ROWS, NZ)],
        "far",
        in_specs=[VM] * 3,
        nbytes=2**19,
    )(pay, step, wrap)
    ret = lax.all_to_all(ret, "slab", split_axis=0, concat_axis=0, tiled=True)
    (out,) = call(
        final_kernel,
        [(3, CELLS, NZ)],
        "final",
        in_specs=[VM] * 12,
        scratch=[
            pltpu.VMEM((EXT, NX, NZ), jnp.float32),
            pltpu.VMEM((CELLS, NZ), jnp.float32),
            pltpu.VMEM((CELLS, NZ), jnp.float32),
        ],
        flops=2**30,
        nbytes=10 * 2**20,
    )(fields, hat, ret, v_prev, v_next, *from_x, *from_z, mu, inv, scale)
    return out.reshape(velocity.shape)


def solution(mesh):
    return jax.shard_map(
        local,
        mesh=mesh,
        in_specs=(
            P("sim", None, None, "slab", None),
            P("sim", None, "slab", None),
            P("sim", None, "slab", None),
            P(),
        ),
        out_specs=P("sim", None, None, "slab", None),
        check_vma=False,
    )
```

time: 313 us -> 114 us (0.36)
  the two profiles are of different devices: /device:TPU:0 before, /device:TPU:16 now
where the time goes in v1:
time: 114 us
  Pallas kernels  33.7 us (30%)
  starting transfers between devices  31.8 us (28%)
  blocking collectives  17.8 us (16%)
  local copies, waits for them, and re-layouts  16.9 us (15%)
  waiting for transfers between devices  10.2 us (9%)
  other arithmetic  2.47 us (2%)
    all_to_all x1, blocking collectives, local(): pay = lax.all_to_all(pay, 'slab', split_axis=0, concat_axis=0, tiled=True)  17.8 us
    unnamed x52, local copies, waits for them, and re-layouts  15.2 us
    pallas_call x1, Pallas kernels, local(): call(diffuse_kernel, [(3, CELLS, NZ)], 'diffuse', in_specs=[VM] * 7, scra...  14.8 us
    pallas_call x1, Pallas kernels, local(): call(final_kernel, [(3, CELLS, NZ)], 'final', in_specs=[VM] * 12, scratch...  9.41 us
    pallas_call x1, Pallas kernels, local(): call(forward_kernel, [(3, CELLS, NZ), (EXT, NX, NZ), (SLABS, 2, ROWS, NZ)...  9.08 us
    ppermute x3, starting transfers between devices, fringe_quarters(): quarters.append(lax.ppermute(mine, 'sim', pairs))  6.7 us
    ppermute x1, starting transfers between devices, local(): following = lax.ppermute(low, 'slab', downward)  6.26 us
    ppermute x1, starting transfers between devices, local(): v_next = lax.ppermute(rims[0], 'slab', downward)  5.61 us
  transfers between devices with their start and end apart: 12, of which 3 were waited for; matrix products, arithmetic and copies ran while one was open for 3% of the time, Pallas kernels for 13%

profile of v1, /device:TPU:16, one launch (start us, length us, event | category | flops | bytes accessed | tf_op | source)
XLA Modules:
  0.0 113.7 jit_solution(11835792889196317755)
XLA Ops:
  0.7 0.0 copy-start
  0.7 1.9 %copy-done = f32[1,3,256,8,128]{4,3,2,1,0:T(8,128)S(1)} copy-done((f32[1,3,256,8,128]{4,3,2,1,0:T(8,128)S(1)}, f32[1,3,256,8,128]{4,3,2,1,0:T(8,128)}, u32[]{:S(2)}) %copy-start) | copy-done | bytes 3145752
  2.5 1.2 %copy-done.1 = f32[1,256,8,128]{3,2,1,0:T(8,128)S(1)} copy-done((f32[1,256,8,128]{3,2,1,0:T(8,128)S(1)}, f32[1,256,8,128]{3,2,1,0:T(8,128)}, u32[]{:S(2)}) %copy-start.1) | copy-done | bytes 1048600
  3.8 0.3 edges.1
  4.1 0.7 fusion
  4.8 1.3 %collective-permute-start.4 = (f32[192,128]{1,0:T(8,128)}, f32[192,128]{1,0:T(8,128)}, u32[]{:S(2)}, u32[]{:S(2)}) collective-permute-start(f32[192,128]{1,0:T(8,128)} %get-tuple-element.19), channel_id=1, source_target_pairs={{0,32},{1,33},{2,34},{3,35},{4,36},{5,37},{6,38},{7,39},{8,40},{9,... | collective-permute-start | bytes 294920 | tf_op jit(solution)/shard_map/ppermute | solution.py:368
  6.1 1.3 %collective-permute-start.3 = (f32[192,128]{1,0:T(8,128)}, f32[192,128]{1,0:T(8,128)}, u32[]{:S(2)}, u32[]{:S(2)}) collective-permute-start(f32[192,128]{1,0:T(8,128)} %get-tuple-element.20), channel_id=1, source_target_pairs={{0,64},{1,65},{2,66},{3,67},{4,68},{5,69},{6,70},{7,71},{8,72},{9,... | collective-permute-start | bytes 294920 | tf_op jit(solution)/shard_map/ppermute | solution.py:368
  7.4 1.3 %collective-permute-start.2 = (f32[192,128]{1,0:T(8,128)}, f32[192,128]{1,0:T(8,128)}, u32[]{:S(2)}, u32[]{:S(2)}) collective-permute-start(f32[192,128]{1,0:T(8,128)} %get-tuple-element.21), channel_id=1, source_target_pairs={{0,96},{1,97},{2,98},{3,99},{4,100},{5,101},{6,102},{7,103},{8,104... | collective-permute-start | bytes 294920 | tf_op jit(solution)/shard_map/ppermute | solution.py:368
  8.7 6.3 %collective-permute-start.1 = (f32[4,256,128]{2,1,0:T(8,128)S(1)}, f32[4,256,128]{2,1,0:T(8,128)}, u32[]{:S(2)}, u32[]{:S(2)}) collective-permute-start(f32[4,256,128]{2,1,0:T(8,128)S(1)} %get-tuple-element.12.own_low), channel_id=1, source_target_pairs={{1,0},{2,1},{3,2},{4,3},{5,4},{6,5},{7,6},{8,7},{9,8},{10,9},{11,1... | collective-permute-start | bytes 1572872 | tf_op jit(solution)/shard_map/ppermute | solution.py:400
  14.9 0.0 collective-permute-start
  15.0 1.6 %select_select_fusion = f32[192,128]{1,0:T(8,128)} fusion(f32[192,128]{1,0:T(8,128)} %collective-permute-done.2, f32[192,128]{1,0:T(8,128)} %collective-permute-done.3, f32[192,128]{1,0:T(8,128)} %collective-permute-done.4, f32[768,128]{1,0:T(8,128)S(1)} %get-tuple-element.14, pred[]{:T(512)S(6)} %eq.11, pred[]{:T(512)S(6)} %eq.10, pred[]{:T(512)S(6)} %eq.9), kind=kLoop, calls=%fused_computation.2 | loop fusion | flops 73728 | bytes 491523 | tf_op jit(solution)/shard_map/jit(_where)/select_n | solution.py:369
  16.5 5.5 %collective-permute-start.5 = (f32[192,128]{1,0:T(8,128)}, f32[192,128]{1,0:T(8,128)S(1)}, u32[]{:S(2)}, u32[]{:S(2)}) collective-permute-start(f32[192,128]{1,0:T(8,128)} %select_select_fusion), channel_id=1, source_target_pairs={{0,128},{32,160},{64,192},{96,224},{1,129},{33,161},{65,193},{97,2... | collective-permute-start | bytes 294920 | tf_op jit(solution)/shard_map/ppermute | solution.py:370
  22.0 2.5 %collective-permute-done.5 = f32[192,128]{1,0:T(8,128)S(1)} collective-permute-done((f32[192,128]{1,0:T(8,128)}, f32[192,128]{1,0:T(8,128)S(1)}, u32[]{:S(2)}, u32[]{:S(2)}) %collective-permute-start.5) | collective-permute-done | bytes 98336 | tf_op jit(solution)/shard_map/ppermute | solution.py:370
  24.5 0.9 broadcast_select_fusion.q0
  25.4 0.5 collective-permute-start.8
  26.0 3.6 %collective-permute-start.7 = (f32[192,128]{1,0:T(8,128)S(1)}, f32[192,128]{1,0:T(8,128)S(1)}, u32[]{:S(2)}, u32[]{:S(2)}) collective-permute-start(f32[192,128]{1,0:T(8,128)S(1)} %broadcast_select_fusion.q0), channel_id=1, source_target_pairs={{0,64},{32,96},{64,0},{96,32},{128,192},{160,224},{192,128},{224,1... | collective-permute-start | bytes 294920 | tf_op jit(solution)/shard_map/ppermute | solution.py:375
  29.6 2.5 %collective-permute-start.6 = (f32[192,128]{1,0:T(8,128)S(1)}, f32[192,128]{1,0:T(8,128)S(1)}, u32[]{:S(2)}, u32[]{:S(2)}) collective-permute-start(f32[192,128]{1,0:T(8,128)S(1)} %broadcast_select_fusion.q0), channel_id=1, source_target_pairs={{0,32},{32,64},{64,96},{96,0},{128,160},{160,192},{192,224},{224,1... | collective-permute-start | bytes 294920 | tf_op jit(solution)/shard_map/ppermute | solution.py:375
  32.2 0.0 copy-start.7
  32.2 0.0 copy-start.17
  32.2 0.0 copy-start.18
  32.2 0.0 copy-start.23
  32.2 0.0 copy-start.24
  32.2 0.0 copy-start.25
  32.2 14.8 %diffuse.1.field_ref = f32[3,2048,128]{2,1,0:T(8,128)} custom-call(f32[3,2048,128]{2,1,0:T(8,128)} %bitcast.8, f32[2048,128]{1,0:T(8,128)S(1)} %bitcast.11, s32[2048,128]{1,0:T(8,128)S(1)} %bitcast.12, f32[4,256,128]{2,1,0:T(8,128)S(1)} %get-tuple-element.12.own_low, f32[4,256,128]{2,1,0:T(8,128)S(1)} %get-tuple-element.13.own_high, ...), custom_call_target="tpu_custom_call" | custom-call | flops 67108864 | bytes 12582912 | tf_op jit(solution)/shard_map/diffuse/pallas_call | solution.py:402
  47.1 9.1 %forward.1 = (f32[3,2048,128]{2,1,0:T(8,128)S(1)}, f32[10,256,128]{2,1,0:T(8,128)S(1)}, f32[32,2,8,128]{3,2,1,0:T(8,128)S(1)}, f32[2,256,128]{2,1,0:T(8,128)S(1)}) custom-call(s32[1]{0:T(128)S(6)} %copy.19.start_ref, f32[3,2048,128]{2,1,0:T(8,128)} %diffuse.1.field_ref, f32[192,128]{1,0:T(8,128)S(1)} %broadcast_select_fusion.q0, ...), custom_call_target="tpu_custom_call" | custom-call | flops 1073741824 | bytes 10485760 | tf_op jit(solution)/shard_map/forward/pallas_call | solution.py:411
  56.2 0.0 copy-start.3
  56.2 1.0 copy-done.3
  57.3 0.7 copy-done.8
  58.0 17.8 %all_to_all.10.pay_ref = f32[32,2,8,128]{3,2,1,0:T(8,128)S(1)} all-to-all(f32[32,2,8,128]{3,2,1,0:T(8,128)S(1)} %get-tuple-element.17), channel_id=1, replica_groups=mesh['sim'=8,'slab'=32] {'slab'}, dimensions={0} | all-to-all | bytes 524288 | tf_op jit(solution)/shard_map/all_to_all | solution.py:426
  75.8 0.1 far.1
  75.9 0.7 copy-done.6
  76.6 3.9 %all-to-all-start.1 = ((f32[32,2,8,128]{3,2,1,0:T(8,128)}), f32[32,2,8,128]{3,2,1,0:T(8,128)S(1)}, u32[]{:S(2)}, u32[]{:S(2)}) async-start(f32[32,2,8,128]{3,2,1,0:T(8,128)} %copy-done.6), calls=%async_computation.1 | async-start | bytes 524288 | tf_op jit(solution)/shard_map/all_to_all | solution.py:434
  80.5 1.0 slice_bitcast_fusion
  81.5 5.6 %collective-permute-start.10 = (f32[256,128]{1,0:T(8,128)S(1)}, f32[256,128]{1,0:T(8,128)S(1)}, u32[]{:S(2)}, u32[]{:S(2)}) collective-permute-start(f32[256,128]{1,0:T(8,128)S(1)} %get-tuple-element.22), channel_id=1, source_target_pairs={{1,0},{2,1},{3,2},{4,3},{5,4},{6,5},{7,6},{8,7},{9,8},{10,9},{11,1... | collective-permute-start | bytes 393224 | tf_op jit(solution)/shard_map/ppermute | solution.py:425
  87.1 2.5 %collective-permute-done.10.next_ref = f32[256,128]{1,0:T(8,128)S(1)} collective-permute-done((f32[256,128]{1,0:T(8,128)S(1)}, f32[256,128]{1,0:T(8,128)S(1)}, u32[]{:S(2)}, u32[]{:S(2)}) %collective-permute-start.10) | collective-permute-done | bytes 131104 | tf_op jit(solution)/shard_map/ppermute | solution.py:425
  89.6 0.6 copy-done.13
  90.2 5.1 %collective-permute-done.9.prev_ref = f32[256,128]{1,0:T(8,128)S(1)} collective-permute-done((f32[256,128]{1,0:T(8,128)S(1)}, f32[256,128]{1,0:T(8,128)S(1)}, u32[]{:S(2)}, u32[]{:S(2)}) %collective-permute-start.9) | collective-permute-done | bytes 131104 | tf_op jit(solution)/shard_map/ppermute | solution.py:424
  95.4 0.7 copy-done.15
  96.0 1.3 %copy-done.4 = f32[10,256,128]{2,1,0:T(8,128)S(1)} copy-done((f32[10,256,128]{2,1,0:T(8,128)S(1)}, f32[10,256,128]{2,1,0:T(8,128)}, u32[]{:S(2)}) %copy-start.4) | copy-done | bytes 1310744
  97.4 0.9 copy-done.9
  98.3 0.9 copy-done.10
  99.2 0.9 copy-done.11
  100.1 0.9 copy-done.12
  101.0 0.9 copy-done.14
  101.9 0.9 copy-done.16
  102.8 0.8 copy-done.21
  103.5 0.8 copy-done.22
  104.3 9.4 %final.1 = f32[3,2048,128]{2,1,0:T(8,128)} custom-call(f32[3,2048,128]{2,1,0:T(8,128)S(1)} %get-tuple-element.15.field_ref, f32[10,256,128]{2,1,0:T(8,128)S(1)} %copy-done.4, f32[32,2,8,128]{3,2,1,0:T(8,128)S(1)} %all-to-all-done.1.ret_ref, f32[256,128]{1,0:T(8,128)S(1)} %copy-done.16, f32[256,128]{1,0:T(8,128)S(1)} %copy-done.14, ...), custom_call_target="tpu_custom_call" | custom-call | flops 1073741824 | bytes 10485760 | tf_op jit(solution)/shard_map/final/pallas_call | solution.py:435
  (38 shorter events, 0.1 us)
Async XLA Ops:
  0.7 1.9 %copy-start = (f32[1,3,256,8,128]{4,3,2,1,0:T(8,128)S(1)}, f32[1,3,256,8,128]{4,3,2,1,0:T(8,128)}, u32[]{:S(2)}) copy-start(f32[1,3,256,8,128]{4,3,2,1,0:T(8,128)} %param.18) | copy-start | bytes 9437188
  2.5 1.2 %copy-start.1 = (f32[1,256,8,128]{3,2,1,0:T(8,128)S(1)}, f32[1,256,8,128]{3,2,1,0:T(8,128)}, u32[]{:S(2)}) copy-start(f32[1,256,8,128]{3,2,1,0:T(8,128)} %param.19) | copy-start | bytes 3145732
  3.8 28.4 %copy-start.2 = (f32[1,256,8,128]{3,2,1,0:T(8,128)S(1)}, f32[1,256,8,128]{3,2,1,0:T(8,128)}, u32[]{:S(2)}) copy-start(f32[1,256,8,128]{3,2,1,0:T(8,128)} %param.19) | copy-start | bytes 3145732
  3.8 28.4 %copy-start.5 = (s32[1,256,8,128]{3,2,1,0:T(8,128)S(1)}, s32[1,256,8,128]{3,2,1,0:T(8,128)}, u32[]{:S(2)}) copy-start(s32[1,256,8,128]{3,2,1,0:T(8,128)} %param.20) | copy-start | bytes 3145732
  4.8 10.2 %collective-permute-start.4 = (f32[192,128]{1,0:T(8,128)}, f32[192,128]{1,0:T(8,128)}, u32[]{:S(2)}, u32[]{:S(2)}) collective-permute-start(f32[192,128]{1,0:T(8,128)} %get-tuple-element.19), channel_id=1, source_target_pairs={{0,32},{1,33},{2,34},{3,35},{4,36},{5,37},{6,38},{7,39},{8,40},{9,... | collective-permute-start | bytes 294920 | tf_op jit(solution)/shard_map/ppermute | solution.py:368
  6.1 8.9 %collective-permute-start.3 = (f32[192,128]{1,0:T(8,128)}, f32[192,128]{1,0:T(8,128)}, u32[]{:S(2)}, u32[]{:S(2)}) collective-permute-start(f32[192,128]{1,0:T(8,128)} %get-tuple-element.20), channel_id=1, source_target_pairs={{0,64},{1,65},{2,66},{3,67},{4,68},{5,69},{6,70},{7,71},{8,72},{9,... | collective-permute-start | bytes 294920 | tf_op jit(solution)/shard_map/ppermute | solution.py:368
  7.4 7.6 %collective-permute-start.2 = (f32[192,128]{1,0:T(8,128)}, f32[192,128]{1,0:T(8,128)}, u32[]{:S(2)}, u32[]{:S(2)}) collective-permute-start(f32[192,128]{1,0:T(8,128)} %get-tuple-element.21), channel_id=1, source_target_pairs={{0,96},{1,97},{2,98},{3,99},{4,100},{5,101},{6,102},{7,103},{8,104... | collective-permute-start | bytes 294920 | tf_op jit(solution)/shard_map/ppermute | solution.py:368
  8.7 23.5 %collective-permute-start.1 = (f32[4,256,128]{2,1,0:T(8,128)S(1)}, f32[4,256,128]{2,1,0:T(8,128)}, u32[]{:S(2)}, u32[]{:S(2)}) collective-permute-start(f32[4,256,128]{2,1,0:T(8,128)S(1)} %get-tuple-element.12.own_low), channel_id=1, source_target_pairs={{1,0},{2,1},{3,2},{4,3},{5,4},{6,5},{7,6},{8,7},{9,8},{10,9},{11,1... | collective-permute-start | bytes 1572872 | tf_op jit(solution)/shard_map/ppermute | solution.py:400
  14.9 17.2 %collective-permute-start = (f32[4,256,128]{2,1,0:T(8,128)S(1)}, f32[4,256,128]{2,1,0:T(8,128)}, u32[]{:S(2)}, u32[]{:S(2)}) collective-permute-start(f32[4,256,128]{2,1,0:T(8,128)S(1)} %get-tuple-element.13.own_high), channel_id=1, source_target_pairs={{0,1},{1,2},{2,3},{3,4},{4,5},{5,6},{6,7},{7,8},{8,9},{9,10},{10,1... | collective-permute-start | bytes 1572872 | tf_op jit(solution)/shard_map/ppermute | solution.py:399
  16.5 8.0 %collective-permute-start.5 = (f32[192,128]{1,0:T(8,128)}, f32[192,128]{1,0:T(8,128)S(1)}, u32[]{:S(2)}, u32[]{:S(2)}) collective-permute-start(f32[192,128]{1,0:T(8,128)} %select_select_fusion), channel_id=1, source_target_pairs={{0,128},{32,160},{64,192},{96,224},{1,129},{33,161},{65,193},{97,2... | collective-permute-start | bytes 294920 | tf_op jit(solution)/shard_map/ppermute | solution.py:370
  25.4 21.6 %collective-permute-start.8 = (f32[192,128]{1,0:T(8,128)S(1)}, f32[192,128]{1,0:T(8,128)S(1)}, u32[]{:S(2)}, u32[]{:S(2)}) collective-permute-start(f32[192,128]{1,0:T(8,128)S(1)} %broadcast_select_fusion.q0), channel_id=1, source_target_pairs={{0,96},{32,0},{64,32},{96,64},{128,224},{160,128},{192,160},{224,1... | collective-permute-start | bytes 294920 | tf_op jit(solution)/shard_map/ppermute | solution.py:375
  26.0 21.1 %collective-permute-start.7 = (f32[192,128]{1,0:T(8,128)S(1)}, f32[192,128]{1,0:T(8,128)S(1)}, u32[]{:S(2)}, u32[]{:S(2)}) collective-permute-start(f32[192,128]{1,0:T(8,128)S(1)} %broadcast_select_fusion.q0), channel_id=1, source_target_pairs={{0,64},{32,96},{64,0},{96,32},{128,192},{160,224},{192,128},{224,1... | collective-permute-start | bytes 294920 | tf_op jit(solution)/shard_map/ppermute | solution.py:375
  29.6 17.5 %collective-permute-start.6 = (f32[192,128]{1,0:T(8,128)S(1)}, f32[192,128]{1,0:T(8,128)S(1)}, u32[]{:S(2)}, u32[]{:S(2)}) collective-permute-start(f32[192,128]{1,0:T(8,128)S(1)} %broadcast_select_fusion.q0), channel_id=1, source_target_pairs={{0,32},{32,64},{64,96},{96,0},{128,160},{160,192},{192,224},{224,1... | collective-permute-start | bytes 294920 | tf_op jit(solution)/shard_map/ppermute | solution.py:375
  32.2 14.9 %copy-start.7 = (f32[256,128]{1,0:T(8,128)S(1)}, f32[256,128]{1,0:T(8,128)}, u32[]{:S(2)}) copy-start(f32[256,128]{1,0:T(8,128)} %constant.47.clone.mu_ref) | copy-start | bytes 393220
  32.2 14.9 %copy-start.17 = (bf16[256,256]{1,0:T(8,128)(2,1)S(1)}, bf16[256,256]{1,0:T(8,128)(2,1)}, u32[]{:S(2)}) copy-start(bf16[256,256]{1,0:T(8,128)(2,1)} %constant.44.clone.xl) | copy-start | bytes 393220
  32.2 14.9 %copy-start.18 = (bf16[256,256]{1,0:T(8,128)(2,1)S(1)}, bf16[256,256]{1,0:T(8,128)(2,1)}, u32[]{:S(2)}) copy-start(bf16[256,256]{1,0:T(8,128)(2,1)} %constant.43.clone.xh) | copy-start | bytes 393220
  32.2 14.9 %copy-start.23 = (bf16[128,128]{1,0:T(8,128)(2,1)S(1)}, bf16[128,128]{1,0:T(8,128)(2,1)}, u32[]{:S(2)}) copy-start(bf16[128,128]{1,0:T(8,128)(2,1)} %constant.46.clone.zl) | copy-start | bytes 98308
  32.2 14.9 %copy-start.24 = (bf16[128,128]{1,0:T(8,128)(2,1)S(1)}, bf16[128,128]{1,0:T(8,128)(2,1)}, u32[]{:S(2)}) copy-start(bf16[128,128]{1,0:T(8,128)(2,1)} %constant.45.clone.zh) | copy-start | bytes 98308
  32.2 14.9 %copy-start.25 = (f32[32]{0:T(128)S(1)}, f32[32]{0:T(128)}, u32[]{:S(2)}) copy-start(f32[32]{0:T(128)} %constant.42.clone.profile_ref) | copy-start | bytes 388
  47.1 28.7 %copy-start.19 = (f32[256,128]{1,0:T(8,128)S(1)}, f32[256,128]{1,0:T(8,128)}, u32[]{:S(2)}) copy-start(f32[256,128]{1,0:T(8,128)} %constant.49.clone.wrap_ref) | copy-start | bytes 393220
  47.1 28.7 %copy-start.20 = (f32[256,128]{1,0:T(8,128)S(1)}, f32[256,128]{1,0:T(8,128)}, u32[]{:S(2)}) copy-start(f32[256,128]{1,0:T(8,128)} %constant.48.clone.step_ref) | copy-start | bytes 393220
  56.2 1.1 copy-start.3
  57.3 0.7 copy-start.8
  75.9 0.7 copy-start.6
  76.6 19.4 %all-to-all-start.1 = ((f32[32,2,8,128]{3,2,1,0:T(8,128)}), f32[32,2,8,128]{3,2,1,0:T(8,128)S(1)}, u32[]{:S(2)}, u32[]{:S(2)}) async-start(f32[32,2,8,128]{3,2,1,0:T(8,128)} %copy-done.6), calls=%async_computation.1 | async-start | bytes 524288 | tf_op jit(solution)/shard_map/all_to_all | solution.py:434
  81.5 8.1 %collective-permute-start.10 = (f32[256,128]{1,0:T(8,128)S(1)}, f32[256,128]{1,0:T(8,128)S(1)}, u32[]{:S(2)}, u32[]{:S(2)}) collective-permute-start(f32[256,128]{1,0:T(8,128)S(1)} %get-tuple-element.22), channel_id=1, source_target_pairs={{1,0},{2,1},{3,2},{4,3},{5,4},{6,5},{7,6},{8,7},{9,8},{10,9},{11,1... | collective-permute-start | bytes 393224 | tf_op jit(solution)/shard_map/ppermute | solution.py:425
  87.1 8.3 %collective-permute-start.9 = (f32[256,128]{1,0:T(8,128)S(1)}, f32[256,128]{1,0:T(8,128)S(1)}, u32[]{:S(2)}, u32[]{:S(2)}) collective-permute-start(f32[256,128]{1,0:T(8,128)S(1)} %get-tuple-element.23), channel_id=1, source_target_pairs={{0,1},{1,2},{2,3},{3,4},{4,5},{5,6},{6,7},{7,8},{8,9},{9,10},{10,1... | collective-permute-start | bytes 393224 | tf_op jit(solution)/shard_map/ppermute | solution.py:424
  89.6 0.6 copy-start.13
  95.4 0.7 copy-start.15
  96.0 1.3 %copy-start.4 = (f32[10,256,128]{2,1,0:T(8,128)S(1)}, f32[10,256,128]{2,1,0:T(8,128)}, u32[]{:S(2)}) copy-start(f32[10,256,128]{2,1,0:T(8,128)} %copy-done.3) | copy-start | bytes 3932164
  97.4 0.9 copy-start.9
  98.3 0.9 copy-start.10
  99.2 0.9 copy-start.11
  100.1 0.9 copy-start.12
  101.0 0.9 copy-start.14
  101.9 0.9 copy-start.16
  102.8 0.8 copy-start.21
  103.5 0.8 copy-start.22

commit v2 on v1

--- a/solution.py
+++ b/solution.py
@@ -3,7 +3,6 @@
 
 import jax
 import jax.numpy as jnp
-import ml_dtypes
 import numpy as np
 from jax import lax
 from jax.experimental import pallas as pl
@@ -19,13 +18,9 @@
 EXT = ROWS + 2
 CELLS = NX * ROWS
 DRAG = 0.5 * 0.75
-VMEM_LIMIT = 48 * 2**20
-
-
-def split_bf16(table):
-    high = table.astype(np.float32).astype(ml_dtypes.bfloat16)
-    low = (table - high.astype(np.float64)).astype(np.float32).astype(ml_dtypes.bfloat16)
-    return high, low
+MIB = 2**20
+DIFFUSE_ROOM = 40
+FORWARD_ROOM = 40
 
 
 def x_table():
@@ -54,9 +49,8 @@
     zero = total == 0.0
     theta = np.where(zero, 1.0, theta)
     mu = np.exp(-theta)
-    scale = -1.0 / (2.0 * np.sinh(theta))
     wrap = 1.0 / (-np.expm1(-NY * theta))
-    tables = [mu, np.exp(theta), scale, np.exp(-ROWS * theta), wrap]
+    tables = [mu, np.exp(-ROWS * theta), wrap]
     return [np.where(zero, 0.0, t).astype(np.float32) for t in tables]
 
 
@@ -71,14 +65,14 @@
     return high, low
 
 
-def call(body, outs, name, scratch=(), in_specs=None, flops=0, nbytes=0, **kw):
+def call(body, outs, name, scratch=(), in_specs=None, out_specs=None, room=20, flops=0, nbytes=0, **kw):
     return pl.pallas_call(
         body,
         out_shape=[jax.ShapeDtypeStruct(s, jnp.float32) for s in outs],
         in_specs=in_specs,
-        out_specs=[pl.BlockSpec(memory_space=pltpu.VMEM)] * len(outs),
+        out_specs=out_specs or [VM] * len(outs),
         scratch_shapes=list(scratch),
-        compiler_params=pltpu.CompilerParams(vmem_limit_bytes=VMEM_LIMIT),
+        compiler_params=pltpu.CompilerParams(vmem_limit_bytes=room * MIB),
         cost_estimate=pl.CostEstimate(flops=flops, bytes_accessed=nbytes, transcendentals=0),
         name=name,
         **kw,
@@ -87,20 +81,58 @@
 
 VM = pl.BlockSpec(memory_space=pltpu.VMEM)
 SM = pl.BlockSpec(memory_space=pltpu.SMEM)
+HB = pl.BlockSpec(memory_space=pltpu.HBM)
+
+
+def start_all(pairs, sems):
+    copies = [pltpu.make_async_copy(a, b, sems.at[k]) for k, (a, b) in enumerate(pairs)]
+    for copy in copies:
+        copy.start()
+    return copies
+
+
+def wait_all(copies):
+    for copy in copies:
+        copy.wait()
 
 
 def every8(first, count=NX):
     return pl.ds(first, count, stride=ROWS)
 
 
-def edges_kernel(start_ref, vel_ref, visc_ref, low_ref, high_ref, fringe_ref):
-    for row, out in ((0, low_ref), (ROWS - 1, high_ref)):
-        for c in range(3):
-            out[c] = vel_ref[c, every8(row), :]
-        out[3] = visc_ref[every8(row), :]
+def fringe_kernel(start_ref, vel_ref, q0, q1, q2, q3, sems):
     first = pl.multiple_of(start_ref[0] * ROWS, ROWS)
-    for c in range(3):
-        fringe_ref[pl.ds(c * FR * ROWS, FR * ROWS), :] = vel_ref[c, pl.ds(first, FR * ROWS), :]
+    rows = FR * ROWS
+    quarter = 3 * rows // 4
+    pairs = []
+    for k, out in enumerate((q0, q1, q2, q3)):
+        at = k * quarter
+        while at < (k + 1) * quarter:
+            c, inner = divmod(at, rows)
+            size = min(rows - inner, (k + 1) * quarter - at)
+            pairs.append((vel_ref.at[c, pl.ds(first + inner, size)], out.at[pl.ds(at - k * quarter, size)]))
+            at += size
+    wait_all(start_all(pairs, sems))
+
+
+EDGE_CHUNKS = 4
+
+
+def edges_kernel(vel_in, visc_in, low_ref, high_ref, vel_ref, visc_ref, sems):
+    part = CELLS // EDGE_CHUNKS
+    pairs = []
+    for k in range(EDGE_CHUNKS):
+        rows = pl.ds(k * part, part)
+        pairs += [(vel_in.at[c, rows], vel_ref.at[c, rows]) for c in range(3)]
+        pairs.append((visc_in.at[rows], visc_ref.at[rows]))
+    copies = start_all(pairs, sems)
+    count = NX // EDGE_CHUNKS
+    for k in range(EDGE_CHUNKS):
+        wait_all(copies[4 * k : 4 * k + 4])
+        for row, out in ((0, low_ref), (ROWS - 1, high_ref)):
+            for c in range(3):
+                out[c, pl.ds(k * count, count), :] = vel_ref[c, every8(k * part + row, count), :]
+            out[3, pl.ds(k * count, count), :] = visc_ref[every8(k * part + row, count), :]
 
 
 def iotas():
@@ -114,11 +146,22 @@
     return pl.ds(pl.multiple_of(x * ROWS, ROWS), ROWS)
 
 
-def diffuse_kernel(vel_ref, visc_ref, turb_ref, own_low, own_high, prev_ref, next_ref, out_ref, rim):
-    del own_low, own_high
+CHUNKS = 8
+
+
+def diffuse_kernel(vel_in, visc_in, turb_in, prev_in, next_in, out_ref, vel_ref, visc_ref, turb_ref, prev_ref, next_ref, rim, sems):
+    part = CELLS // CHUNKS
+    spans = [pl.ds(k * part, part) for k in (CHUNKS - 1, *range(CHUNKS - 1))]
+    pairs = [(prev_in, prev_ref), (next_in, next_ref)]
+    for span in spans:
+        pairs += [(vel_in.at[:, span], vel_ref.at[:, span]), (visc_in.at[span], visc_ref.at[span])]
+        pairs.append((turb_in.at[span], turb_ref.at[span]))
+    copies = start_all(pairs, sems)
+    wait_all(copies[:2])
     for c in range(4):
         rim[c, every8(0), :] = prev_ref[c]
         rim[c, every8(ROWS - 1), :] = next_ref[c]
+    wait_all(copies[2:8])
     row, lane = iotas()
     first_row, last_row = row == 0, row == ROWS - 1
     first_lane, last_lane = lane == 0, lane == NZ - 1
@@ -160,7 +203,12 @@
     now, nu = fields_at(0)
     sum_x = 0.5 * nu_last + 0.5 * nu
     back = [flux(sum_x, last[c], now[c]) for c in range(3)]
-    lax.fori_loop(0, NX, step, (now, nu, back), unroll=4)
+    carry = (now, nu, back)
+    count = NX // CHUNKS
+    for k in range(CHUNKS):
+        if k < CHUNKS - 2:
+            wait_all(copies[8 + 3 * k : 11 + 3 * k])
+        carry = lax.fori_loop(k * count, (k + 1) * count, step, carry, unroll=16)
 
 
 def centred_z(value, first_lane, last_lane):
@@ -169,10 +217,23 @@
     return up - down
 
 
+TAB_X = NX
+TAB_Z = TAB_X + 2 * NX
+LATER = TAB_Z + NZ
+STORE_HAT = 3 * CELLS
+STORE_LATER = STORE_HAT + EXT * NX
+STORE = 40 * 2**11
+
+
+def x_matrix(table_ref):
+    return jnp.concatenate([table_ref[pl.ds(TAB_X, NX), :], table_ref[pl.ds(TAB_X + NX, NX), :]], 1)
+
+
 def forward_kernel(
-    start_ref, field_ref, q0, q1, q2, q3, profile_ref, xh, xl, zh, zl, mu_ref,
-    out_ref, hat_ref, pay_ref, rim_ref, fringe, div, modes,
+    start_ref, field_ref, q0, q1, q2, q3, profile_ref, table_ref, later_ref,
+    store, pay_ref, low_ref, high_ref, out_ref, fringe, div, modes, hat_ref, sems,
 ):
+    copies = start_all([(later_ref, store.at[pl.ds(STORE_LATER, LATER)])], sems)
     me = lax.axis_index("sim")
     active = jnp.where(me == 0, 0.0, 1.0).astype(jnp.float32)
     quarter = 3 * FR * ROWS // 4
@@ -194,7 +255,10 @@
             out_ref[c, tile(start + i), :] = old + weight * (fringe[tile(c * FR + i), :] - old)
         return 0
 
-    lax.fori_loop(0, FR, blend, 0, unroll=4)
+    lax.fori_loop(0, FR, blend, 0, unroll=8)
+    for c in range(3):
+        copies.append(pltpu.make_async_copy(out_ref.at[c], store.at[pl.ds(c * CELLS, CELLS)], sems.at[1 + c]))
+        copies[-1].start()
 
     def source(x, carry):
         behind, now = carry
@@ -206,19 +270,19 @@
         div[tile(x), :] = 0.5 * ((ahead - behind) + (up - down) + centred_z(w, first_lane, last_lane))
         return now, ahead
 
-    lax.fori_loop(0, NX, source, (out_ref[0, tile(NX - 1), :], out_ref[0, tile(0), :]), unroll=4)
-
-    z_high, z_low = zh[...], zl[...]
+    lax.fori_loop(0, NX, source, (out_ref[0, tile(NX - 1), :], out_ref[0, tile(0), :]), unroll=16)
+
+    z_high, z_low = parts(table_ref[pl.ds(TAB_Z, NZ), :])
     for block in range(8):
         rows = pl.ds(block * NX, NX)
         modes[rows, :] = dot3(*parts(div[rows, :]), z_high, z_low)
     low = out_ref[1, every8(0), :]
     high = out_ref[1, every8(ROWS - 1), :]
-    rim_ref[0] = low
-    rim_ref[1] = high
+    low_ref[...] = low
+    high_ref[...] = high
     low = dot3(*parts(0.5 * low), z_high, z_low)
     high = dot3(*parts(-0.5 * high), z_high, z_low)
-    x_high, x_low = xh[...], xl[...]
+    x_high, x_low = parts(x_matrix(table_ref))
     for r in range(0, EXT, 2):
         pair = []
         for k in (r, r + 1):
@@ -226,11 +290,15 @@
         both = dot3(x_high, x_low, *parts(jnp.concatenate(pair, 1)))
         hat_ref[r] = both[:, :NZ]
         hat_ref[r + 1] = both[:, NZ:]
+        for k in (r, r + 1):
+            to = store.at[pl.ds(STORE_HAT + k * NX, NX)]
+            copies.append(pltpu.make_async_copy(hat_ref.at[k], to, sems.at[4 + k]))
+            copies[-1].start()
 
     origin = (row == 0) & (lane == 0)
 
     def sums(block, at):
-        mu = mu_ref[at, :]
+        mu = table_ref[at, :]
         rows = [hat_ref[r, at, :] for r in range(EXT)]
         right = rows[0]
         for value in rows[1:]:
@@ -246,12 +314,13 @@
         pay_ref[block, 1] = left
         return 0
 
-    lax.fori_loop(1, NX // ROWS, weigh, 0, unroll=2)
+    lax.fori_loop(1, NX // ROWS, weigh, 0, unroll=4)
     right, left, rows = sums(0, tile(0))
     moment0 = functools.reduce(jnp.add, rows)
     moment1 = functools.reduce(jnp.add, [float(r - 1) * rows[r] for r in range(EXT) if r != 1])
     pay_ref[0, 0] = jnp.where(origin, moment0, right)
     pay_ref[0, 1] = jnp.where(origin, moment1, left)
+    wait_all(copies)
 
 
 def far_kernel(pay_ref, step_ref, wrap_ref, out_ref):
@@ -286,21 +355,32 @@
         left = step * left + pay_ref[t, 1]
 
 
+OUT_CHUNKS = 4
+
+
 def green0(j):
     return 0.5 * j - j * j / (2.0 * NY)
 
 
 def final_kernel(
-    field_ref, hat_ref, ret_ref, prev_ref, next_ref, xh, xl, zh, zl, mu_ref, inv_ref, scale_ref,
-    out_ref, press, field, rim,
+    ret_ref, prev_ref, next_ref, store,
+    out_hbm, press, field, rim, out_ref, field_ref, hat_ref, table_ref, sems, out_sems,
 ):
+    hats = [(store.at[pl.ds(STORE_HAT + r * NX, NX)], hat_ref.at[r]) for r in range(EXT)]
+    lines = (pl.ds(0, NX), pl.ds(NX, LATER - NX))
+    later = [(store.at[pl.ds(STORE_LATER + s.start, s.size)], table_ref.at[s]) for s in lines]
+    fields = [(store.at[pl.ds(c * CELLS, CELLS)], field_ref.at[c]) for c in range(3)]
+    copies = start_all([later[0], *hats, later[1], *fields], sems)
+    wait_all(copies[: 1 + EXT])
     row, lane = iotas()
     first_row, last_row = row == 0, row == ROWS - 1
     first_lane, last_lane = lane == 0, lane == NZ - 1
     origin = (row == 0) & (lane == 0)
 
     def solve(block, at):
-        mu, inv, scale = mu_ref[at, :], inv_ref[at, :], scale_ref[at, :]
+        mu = table_ref[at, :]
+        inv = 1.0 / jnp.where(mu == 0.0, 1.0, mu)
+        scale = jnp.where(mu == 0.0, 0.0, -1.0 / ((1.0 + mu) * (1.0 - mu) * inv))
         rows = [hat_ref[r, at, :] for r in range(EXT)]
         below = [ret_ref[block, 0] * inv + rows[0]]
         for value in rows[1:]:
@@ -318,7 +398,7 @@
             press[r, at, :] = values[r]
         return 0
 
-    lax.fori_loop(1, NX // ROWS, line, 0, unroll=2)
+    lax.fori_loop(1, NX // ROWS, line, 0, unroll=4)
     at = pl.ds(0, ROWS)
     values, rows = solve(0, at)
     slope, curve = ret_ref[0, 0], ret_ref[0, 1]
@@ -330,8 +410,9 @@
                 mean_line = mean_line + green0(float(abs(r - k))) * rows[k]
         press[r, at, :] = jnp.where(origin, mean_line, values[r])
 
-    x_high, x_low = xh[...], xl[...]
-    z_high, z_low = zh[...], zl[...]
+    copies[1 + EXT].wait()
+    x_high, x_low = parts(x_matrix(table_ref))
+    z_high, z_low = parts(table_ref[pl.ds(TAB_Z, NZ), :])
     for r in range(0, EXT, 2):
         pair = jnp.concatenate([press[r], press[r + 1]], 1)
         both = dot3(x_high, x_low, *parts(pair))
@@ -356,13 +437,21 @@
             out_ref[c, tile(x), :] = field_ref[c, tile(x), :] - 0.5 * grads[c]
         return now, ahead
 
-    lax.fori_loop(0, NX, project, (field[tile(NX - 1), :], field[tile(0), :]), unroll=4)
-
-
-def fringe_quarters(fringe):
-    quarter = fringe.shape[0] // 4
+    carry = (field[tile(NX - 1), :], field[tile(0), :])
+    wait_all(copies[2 + EXT :])
+    copies = []
+    part = CELLS // OUT_CHUNKS
+    count = NX // OUT_CHUNKS
+    for k in range(OUT_CHUNKS):
+        carry = lax.fori_loop(k * count, (k + 1) * count, project, carry, unroll=16)
+        rows = pl.ds(k * part, part)
+        copies.append(pltpu.make_async_copy(out_ref.at[:, rows], out_hbm.at[:, rows], out_sems.at[k]))
+        copies[-1].start()
+    wait_all(copies)
+
+
+def fringe_quarters(piece):
     me = lax.axis_index("sim")
-    piece = [fringe[k * quarter : (k + 1) * quarter] for k in range(4)]
     mine = piece[0]
     for k in (1, 2, 3):
         came = lax.ppermute(piece[k], "sim", [(0, k)])
@@ -382,47 +471,81 @@
     turb = turbines.reshape(CELLS, NZ)
     x_basis = x_table()[0]
     z_basis = z_table()
-    to_x, from_x = split_bf16(x_basis), split_bf16(x_basis.T)
-    to_z, from_z = split_bf16(z_basis.T), split_bf16(z_basis)
-    mu, inv, scale, step, wrap = line_tables()
+    mu, step, wrap = line_tables()
+    table, later = (
+        np.concatenate([mu, x[:, :NZ], x[:, NZ:], z]).astype(np.float32)
+        for x, z in ((x_basis, z_basis.T), (x_basis.T, z_basis))
+    )
     profile = (np.sin(math.pi * (np.arange(FR) + 0.5) / FR) ** 2).astype(np.float32)
     upward = [(i, (i + 1) % SLABS) for i in range(SLABS)]
     downward = [((i + 1) % SLABS, i) for i in range(SLABS)]
 
-    low, high, fringe = call(
+    f32 = jnp.float32
+    quarter = (3 * FR * ROWS // 4, NZ)
+    plane = (NX, NZ)
+    pieces = call(
+        fringe_kernel,
+        [quarter] * 4,
+        "fringe",
+        room=60,
+        in_specs=[SM, HB],
+        scratch=[pltpu.SemaphoreType.DMA((6,))],
+        nbytes=2**19,
+    )(fringe_start, vel)
+    quarters = fringe_quarters(pieces)
+    low, high = call(
         edges_kernel,
-        [(4, NX, NZ), (4, NX, NZ), (3 * FR * ROWS, NZ)],
+        [(4, NX, NZ), (4, NX, NZ)],
         "edges",
-        in_specs=[SM, VM, VM],
+        room=60,
+        in_specs=[HB, HB],
+        scratch=[
+            pltpu.VMEM((3, CELLS, NZ), f32),
+            pltpu.VMEM((CELLS, NZ), f32),
+            pltpu.SemaphoreType.DMA((4 * EDGE_CHUNKS,)),
+        ],
         nbytes=6 * 2**20,
-    )(fringe_start, vel, visc)
+    )(vel, visc)
     prev = lax.ppermute(high, "slab", upward)
     following = lax.ppermute(low, "slab", downward)
-    quarters = fringe_quarters(fringe)
     (fields,) = call(
         diffuse_kernel,
         [(3, CELLS, NZ)],
         "diffuse",
-        in_specs=[VM] * 7,
-        scratch=[pltpu.VMEM((4, CELLS, NZ), jnp.float32)],
+        room=DIFFUSE_ROOM,
+        in_specs=[HB] * 5,
+        scratch=[
+            pltpu.VMEM((3, CELLS, NZ), f32),
+            pltpu.VMEM((CELLS, NZ), f32),
+            pltpu.VMEM((CELLS, NZ), jnp.int32),
+            pltpu.VMEM((4, NX, NZ), f32),
+            pltpu.VMEM((4, NX, NZ), f32),
+            pltpu.VMEM((4, CELLS, NZ), f32),
+            pltpu.SemaphoreType.DMA((2 + 3 * CHUNKS,)),
+        ],
         flops=2**26,
         nbytes=12 * 2**20,
-    )(vel, visc, turb, low, high, prev, following)
-    fields, hat, pay, rims = call(
+    )(vel, visc, turb, prev, following)
+    store, pay, v_low, v_high = call(
         forward_kernel,
-        [(3, CELLS, NZ), (EXT, NX, NZ), (SLABS, 2, ROWS, NZ), (2, NX, NZ)],
+        [(STORE, NZ), (SLABS, 2, ROWS, NZ), plane, plane],
         "forward",
-        in_specs=[SM] + [VM] * 5 + [SM] + [VM] * 5,
+        room=FORWARD_ROOM,
+        in_specs=[SM] + [VM] * 5 + [SM] + [VM] * 2,
+        out_specs=[HB, VM, VM, VM],
         scratch=[
-            pltpu.VMEM((3 * FR * ROWS, NZ), jnp.float32),
-            pltpu.VMEM((CELLS, NZ), jnp.float32),
-            pltpu.VMEM((CELLS, NZ), jnp.float32),
+            pltpu.VMEM((3, CELLS, NZ), f32),
+            pltpu.VMEM((3 * FR * ROWS, NZ), f32),
+            pltpu.VMEM((CELLS, NZ), f32),
+            pltpu.VMEM((CELLS, NZ), f32),
+            pltpu.VMEM((EXT, NX, NZ), f32),
+            pltpu.SemaphoreType.DMA((4 + EXT,)),
         ],
         flops=2**30,
         nbytes=10 * 2**20,
-    )(fringe_start, fields, *quarters, profile, *to_x, *to_z, mu)
-    v_prev = lax.ppermute(rims[1], "slab", upward)
-    v_next = lax.ppermute(rims[0], "slab", downward)
+    )(fringe_start, fields, *quarters, profile, table, later)
+    v_prev = lax.ppermute(v_high, "slab", upward)
+    v_next = lax.ppermute(v_low, "slab", downward)
     pay = lax.all_to_all(pay, "slab", split_axis=0, concat_axis=0, tiled=True)
     (ret,) = call(
         far_kernel,
@@ -436,15 +559,23 @@
         final_kernel,
         [(3, CELLS, NZ)],
         "final",
-        in_specs=[VM] * 12,
+        room=FORWARD_ROOM,
+        in_specs=[VM, VM, VM, HB],
+        out_specs=[HB],
         scratch=[
-            pltpu.VMEM((EXT, NX, NZ), jnp.float32),
-            pltpu.VMEM((CELLS, NZ), jnp.float32),
-            pltpu.VMEM((CELLS, NZ), jnp.float32),
+            pltpu.VMEM((EXT, NX, NZ), f32),
+            pltpu.VMEM((CELLS, NZ), f32),
+            pltpu.VMEM((CELLS, NZ), f32),
+            pltpu.VMEM((3, CELLS, NZ), f32),
+            pltpu.VMEM((3, CELLS, NZ), f32),
+            pltpu.VMEM((EXT, NX, NZ), f32),
+            pltpu.VMEM((LATER, NZ), f32),
+            pltpu.SemaphoreType.DMA((5 + EXT,)),
+            pltpu.SemaphoreType.DMA((OUT_CHUNKS,)),
         ],
         flops=2**30,
         nbytes=10 * 2**20,
-    )(fields, hat, ret, v_prev, v_next, *from_x, *from_z, mu, inv, scale)
+    )(ret, v_prev, v_next, store)
     return out.reshape(velocity.shape)
 
 

time: 114 us -> 86.1 us (0.76)
  the two profiles are of different devices: /device:TPU:16 before, /device:TPU:1 now
where the time goes in v2:
time: 86.1 us; the launch traced here: 85 us
  Pallas kernels  25.1 us (29%)
  starting transfers between devices  24.2 us (28%)
  blocking collectives  20.4 us (24%)
  waiting for transfers between devices  11.4 us (13%)
  local copies, waits for them, and re-layouts  3.11 us (4%)
    all_to_all x1, blocking collectives, local(): pay = lax.all_to_all(pay, 'slab', split_axis=0, concat_axis=0, tiled=True)  20.4 us
    ppermute x3, starting transfers between devices, fringe_quarters(): came = lax.ppermute(piece[k], 'sim', [(0, k)])  8.33 us
    pallas_call x1, Pallas kernels, local(): call(diffuse_kernel, [(3, CELLS, NZ)], 'diffuse', room=DIFFUSE_ROOM, in_s...  7.67 us
    pallas_call x1, Pallas kernels, local(): call(final_kernel, [(3, CELLS, NZ)], 'final', room=FORWARD_ROOM, in_specs...  6.64 us
    ppermute x3, starting transfers between devices, fringe_quarters(): quarters.append(lax.ppermute(mine, 'sim', pairs))  4.89 us
    pallas_call x1, Pallas kernels, local(): call(forward_kernel, [(STORE, NZ), (SLABS, 2, ROWS, NZ), plane, plane], '...  4.76 us
    all_to_all x1, waiting for transfers between devices, local(): ret = lax.all_to_all(ret, 'slab', split_axis=0, concat_axis=0, tiled=True)  4.39 us
    all_to_all x1, starting transfers between devices, local(): ret = lax.all_to_all(ret, 'slab', split_axis=0, concat_axis=0, tiled=True)  3.83 us
  transfers between devices with their start and end apart: 12, of which 4 were waited for; matrix products, arithmetic and copies ran while one was open for 0% of the time, Pallas kernels for 13%

profile of v2, /device:TPU:1, one launch (start us, length us, event | category | flops | bytes accessed | tf_op | source)
XLA Modules:
  0.0 85.0 jit_solution(9965018028699540050)
XLA Ops:
  0.7 1.9 %fringe.1 = (f32[192,128]{1,0:T(8,128)}, f32[192,128]{1,0:T(8,128)}, f32[192,128]{1,0:T(8,128)}, f32[192,128]{1,0:T(8,128)}) custom-call(s32[1]{0:T(128)S(6)} %copy.10.start_ref, f32[3,2048,128]{2,1,0:T(8,128)} %bitcast.4), custom_call_target="tpu_custom_call" | custom-call | bytes 524288 | tf_op jit(solution)/shard_map/fringe/pallas_call | solution.py:486
  2.5 0.0 copy-start.8
  2.5 0.0 copy-start
  2.6 5.7 %collective-permute-start.2 = (f32[192,128]{1,0:T(8,128)}, f32[192,128]{1,0:T(8,128)S(1)}, u32[]{:S(2)}, u32[]{:S(2)}) collective-permute-start(f32[192,128]{1,0:T(8,128)} %get-tuple-element.17), channel_id=1, source_target_pairs={{0,96},{1,97},{2,98},{3,99},{4,100},{5,101},{6,102},{7,103},{8,104... | collective-permute-start | bytes 294920 | tf_op jit(solution)/shard_map/ppermute | solution.py:457
  8.3 1.3 %collective-permute-start.3 = (f32[192,128]{1,0:T(8,128)}, f32[192,128]{1,0:T(8,128)S(1)}, u32[]{:S(2)}, u32[]{:S(2)}) collective-permute-start(f32[192,128]{1,0:T(8,128)} %get-tuple-element.18), channel_id=1, source_target_pairs={{0,64},{1,65},{2,66},{3,67},{4,68},{5,69},{6,70},{7,71},{8,72},{9,... | collective-permute-start | bytes 294920 | tf_op jit(solution)/shard_map/ppermute | solution.py:457
  9.6 1.3 %collective-permute-start.4 = (f32[192,128]{1,0:T(8,128)}, f32[192,128]{1,0:T(8,128)S(1)}, u32[]{:S(2)}, u32[]{:S(2)}) collective-permute-start(f32[192,128]{1,0:T(8,128)} %get-tuple-element.19), channel_id=1, source_target_pairs={{0,32},{1,33},{2,34},{3,35},{4,36},{5,37},{6,38},{7,39},{8,40},{9,... | collective-permute-start | bytes 294920 | tf_op jit(solution)/shard_map/ppermute | solution.py:457
  10.9 3.3 %edges.1 = (f32[4,256,128]{2,1,0:T(8,128)}, f32[4,256,128]{2,1,0:T(8,128)}) custom-call(f32[3,2048,128]{2,1,0:T(8,128)} %bitcast.5, f32[2048,128]{1,0:T(8,128)} %bitcast.7), custom_call_target="tpu_custom_call" | custom-call | bytes 6291456 | tf_op jit(solution)/shard_map/edges/pallas_call | solution.py:496
  14.2 2.1 %collective-permute-start = (f32[4,256,128]{2,1,0:T(8,128)}, f32[4,256,128]{2,1,0:T(8,128)}, u32[]{:S(2)}, u32[]{:S(2)}) collective-permute-start(f32[4,256,128]{2,1,0:T(8,128)} %get-tuple-element.15), channel_id=1, source_target_pairs={{0,1},{1,2},{2,3},{3,4},{4,5},{5,6},{6,7},{7,8},{8,9},{9,10},{10,1... | collective-permute-start | bytes 1572872 | tf_op jit(solution)/shard_map/ppermute | solution.py:509
  16.3 0.0 collective-permute-start.1
  16.3 0.0 collective-permute-done.2
  16.3 0.0 collective-permute-done.3
  16.3 0.0 collective-permute-done.4
  16.4 0.0 copy-start.9
  16.4 0.6 copy-done.9
  17.0 0.0 copy-done.8
  17.0 3.3 %collective-permute-start.5 = (f32[192,128]{1,0:T(8,128)S(1)}, f32[192,128]{1,0:T(8,128)S(1)}, u32[]{:S(2)}, u32[]{:S(2)}) collective-permute-start(f32[192,128]{1,0:T(8,128)S(1)} %select_select_fusion), channel_id=1, source_target_pairs={{0,128},{32,160},{64,192},{96,224},{1,129},{33,161},{65,193},{97,2... | collective-permute-start | bytes 294920 | tf_op jit(solution)/shard_map/ppermute | solution.py:459
  20.3 1.6 %collective-permute-done.5 = f32[192,128]{1,0:T(8,128)S(1)} collective-permute-done((f32[192,128]{1,0:T(8,128)S(1)}, f32[192,128]{1,0:T(8,128)S(1)}, u32[]{:S(2)}, u32[]{:S(2)}) %collective-permute-start.5) | collective-permute-done | bytes 98336 | tf_op jit(solution)/shard_map/ppermute | solution.py:459
  22.0 3.8 %collective-permute-start.8 = (f32[192,128]{1,0:T(8,128)S(1)}, f32[192,128]{1,0:T(8,128)S(1)}, u32[]{:S(2)}, u32[]{:S(2)}) collective-permute-start(f32[192,128]{1,0:T(8,128)S(1)} %broadcast_select_fusion.q0), channel_id=1, source_target_pairs={{0,96},{32,0},{64,32},{96,64},{128,224},{160,128},{192,160},{224,1... | collective-permute-start | bytes 294920 | tf_op jit(solution)/shard_map/ppermute | solution.py:464
  25.8 0.4 collective-permute-start.7
  26.2 0.7 collective-permute-start.6
  26.9 0.0 collective-permute-done.prev_in
  26.9 0.0 collective-permute-done.1.next_in
  26.9 0.0 copy-done
  26.9 0.0 copy-start.1
  26.9 1.2 %copy-done.1 = f32[1,256,8,128]{3,2,1,0:T(8,128)S(1)} copy-done((f32[1,256,8,128]{3,2,1,0:T(8,128)S(1)}, f32[1,256,8,128]{3,2,1,0:T(8,128)}, u32[]{:S(2)}) %copy-start.1) | copy-done | bytes 1048600
  28.1 0.0 copy-start.2
  28.1 1.2 %copy-done.2 = s32[1,256,8,128]{3,2,1,0:T(8,128)S(1)} copy-done((s32[1,256,8,128]{3,2,1,0:T(8,128)S(1)}, s32[1,256,8,128]{3,2,1,0:T(8,128)}, u32[]{:S(2)}) %copy-start.2) | copy-done | bytes 1048600
  29.3 7.7 %diffuse.1.field_ref = f32[3,2048,128]{2,1,0:T(8,128)S(1)} custom-call(f32[3,2048,128]{2,1,0:T(8,128)S(1)} %bitcast.6, f32[2048,128]{1,0:T(8,128)S(1)} %bitcast.8, s32[2048,128]{1,0:T(8,128)S(1)} %bitcast.9, f32[4,256,128]{2,1,0:T(8,128)} %collective-permute-done.prev_in, f32[4,256,128]{2,1,0:T(8,128)} %collective-permute-done.1.next_in), custom_call_target="tpu_custom_call" | custom-call | flops 67108864 | bytes 12582912 | tf_op jit(solution)/shard_map/diffuse/pallas_call | solution.py:511
  37.0 0.0 copy-start.5
  37.0 0.0 copy-start.6
  37.0 0.0 collective-permute-done.8.q3
  37.0 0.0 collective-permute-done.7.q2
  37.1 0.0 collective-permute-done.6.q1
  37.1 0.0 copy-done.3
  37.1 0.0 copy-done.4
  37.1 0.0 copy-done.7
  37.1 4.8 %forward.1 = (f32[81920,128]{1,0:T(8,128)}, f32[32,2,8,128]{3,2,1,0:T(8,128)S(1)}, f32[256,128]{1,0:T(8,128)S(1)}, f32[256,128]{1,0:T(8,128)S(1)}) custom-call(s32[1]{0:T(128)S(6)} %copy.10.start_ref, f32[3,2048,128]{2,1,0:T(8,128)S(1)} %diffuse.1.field_ref, f32[192,128]{1,0:T(8,128)S(1)} %broadcast_select_fusion.q0, ...), custom_call_target="tpu_custom_call" | custom-call | flops 1073741824 | bytes 10485760 | tf_op jit(solution)/shard_map/forward/pallas_call | solution.py:529
  41.9 20.4 %all_to_all.10.pay_ref = f32[32,2,8,128]{3,2,1,0:T(8,128)S(1)} all-to-all(f32[32,2,8,128]{3,2,1,0:T(8,128)S(1)} %get-tuple-element.21), channel_id=1, replica_groups=mesh['sim'=8,'slab'=32] {'slab'}, dimensions={0} | all-to-all | bytes 524288 | tf_op jit(solution)/shard_map/all_to_all | solution.py:549
  62.3 0.0 copy-done.5
  62.3 0.0 copy-done.6
  62.3 0.8 far.1
  63.1 3.8 %all-to-all-start.1 = ((f32[32,2,8,128]{3,2,1,0:T(8,128)}), f32[32,2,8,128]{3,2,1,0:T(8,128)S(1)}, u32[]{:S(2)}, u32[]{:S(2)}) async-start(f32[32,2,8,128]{3,2,1,0:T(8,128)} %far.1), calls=%async_computation.1 | async-start | bytes 524288 | tf_op jit(solution)/shard_map/all_to_all | solution.py:557
  66.9 1.7 %collective-permute-start.9 = (f32[256,128]{1,0:T(8,128)S(1)}, f32[256,128]{1,0:T(8,128)S(1)}, u32[]{:S(2)}, u32[]{:S(2)}) collective-permute-start(f32[256,128]{1,0:T(8,128)S(1)} %get-tuple-element.22), channel_id=1, source_target_pairs={{0,1},{1,2},{2,3},{3,4},{4,5},{5,6},{6,7},{7,8},{8,9},{9,10},{10,1... | collective-permute-start | bytes 393224 | tf_op jit(solution)/shard_map/ppermute | solution.py:547
  68.7 0.0 collective-permute-start.10
  68.7 3.0 %collective-permute-done.9.prev_ref = f32[256,128]{1,0:T(8,128)S(1)} collective-permute-done((f32[256,128]{1,0:T(8,128)S(1)}, f32[256,128]{1,0:T(8,128)S(1)}, u32[]{:S(2)}, u32[]{:S(2)}) %collective-permute-start.9) | collective-permute-done | bytes 131104 | tf_op jit(solution)/shard_map/ppermute | solution.py:547
  71.6 2.4 %collective-permute-done.10.next_ref = f32[256,128]{1,0:T(8,128)S(1)} collective-permute-done((f32[256,128]{1,0:T(8,128)S(1)}, f32[256,128]{1,0:T(8,128)S(1)}, u32[]{:S(2)}, u32[]{:S(2)}) %collective-permute-start.10) | collective-permute-done | bytes 131104 | tf_op jit(solution)/shard_map/ppermute | solution.py:548
  74.0 4.4 %all-to-all-done.1.ret_ref = f32[32,2,8,128]{3,2,1,0:T(8,128)S(1)} async-done(((f32[32,2,8,128]{3,2,1,0:T(8,128)}), f32[32,2,8,128]{3,2,1,0:T(8,128)S(1)}, u32[]{:S(2)}, u32[]{:S(2)}) %all-to-all-start.1) | async-done | bytes 262176 | tf_op jit(solution)/shard_map/all_to_all | solution.py:557
  78.4 6.6 %final.1 = f32[3,2048,128]{2,1,0:T(8,128)} custom-call(f32[32,2,8,128]{3,2,1,0:T(8,128)S(1)} %all-to-all-done.1.ret_ref, f32[256,128]{1,0:T(8,128)S(1)} %collective-permute-done.9.prev_ref, f32[256,128]{1,0:T(8,128)S(1)} %collective-permute-done.10.next_ref, f32[81920,128]{1,0:T(8,128)} %get-tuple-element.24.store), custom_call_target="tpu_custom_call" | custom-call | flops 1073741824 | bytes 10485760 | tf_op jit(solution)/shard_map/final/pallas_call | solution.py:558
  (5 shorter events, 0.0 us)
Async XLA Ops:
  2.5 14.5 %copy-start.8 = (f32[192,128]{1,0:T(8,128)S(1)}, f32[192,128]{1,0:T(8,128)}, u32[]{:S(2)}) copy-start(f32[192,128]{1,0:T(8,128)} %get-tuple-element.20) | copy-start | bytes 294916
  2.5 24.3 %copy-start = (f32[1,3,256,8,128]{4,3,2,1,0:T(8,128)S(1)}, f32[1,3,256,8,128]{4,3,2,1,0:T(8,128)}, u32[]{:S(2)}) copy-start(f32[1,3,256,8,128]{4,3,2,1,0:T(8,128)} %param.9) | copy-start | bytes 9437188
  2.6 13.8 %collective-permute-start.2 = (f32[192,128]{1,0:T(8,128)}, f32[192,128]{1,0:T(8,128)S(1)}, u32[]{:S(2)}, u32[]{:S(2)}) collective-permute-start(f32[192,128]{1,0:T(8,128)} %get-tuple-element.17), channel_id=1, source_target_pairs={{0,96},{1,97},{2,98},{3,99},{4,100},{5,101},{6,102},{7,103},{8,104... | collective-permute-start | bytes 294920 | tf_op jit(solution)/shard_map/ppermute | solution.py:457
  8.3 8.0 %collective-permute-start.3 = (f32[192,128]{1,0:T(8,128)}, f32[192,128]{1,0:T(8,128)S(1)}, u32[]{:S(2)}, u32[]{:S(2)}) collective-permute-start(f32[192,128]{1,0:T(8,128)} %get-tuple-element.18), channel_id=1, source_target_pairs={{0,64},{1,65},{2,66},{3,67},{4,68},{5,69},{6,70},{7,71},{8,72},{9,... | collective-permute-start | bytes 294920 | tf_op jit(solution)/shard_map/ppermute | solution.py:457
  9.6 6.7 %collective-permute-start.4 = (f32[192,128]{1,0:T(8,128)}, f32[192,128]{1,0:T(8,128)S(1)}, u32[]{:S(2)}, u32[]{:S(2)}) collective-permute-start(f32[192,128]{1,0:T(8,128)} %get-tuple-element.19), channel_id=1, source_target_pairs={{0,32},{1,33},{2,34},{3,35},{4,36},{5,37},{6,38},{7,39},{8,40},{9,... | collective-permute-start | bytes 294920 | tf_op jit(solution)/shard_map/ppermute | solution.py:457
  14.2 12.7 %collective-permute-start = (f32[4,256,128]{2,1,0:T(8,128)}, f32[4,256,128]{2,1,0:T(8,128)}, u32[]{:S(2)}, u32[]{:S(2)}) collective-permute-start(f32[4,256,128]{2,1,0:T(8,128)} %get-tuple-element.15), channel_id=1, source_target_pairs={{0,1},{1,2},{2,3},{3,4},{4,5},{5,6},{6,7},{7,8},{8,9},{9,10},{10,1... | collective-permute-start | bytes 1572872 | tf_op jit(solution)/shard_map/ppermute | solution.py:509
  16.3 10.5 %collective-permute-start.1 = (f32[4,256,128]{2,1,0:T(8,128)}, f32[4,256,128]{2,1,0:T(8,128)}, u32[]{:S(2)}, u32[]{:S(2)}) collective-permute-start(f32[4,256,128]{2,1,0:T(8,128)} %get-tuple-element.16), channel_id=1, source_target_pairs={{1,0},{2,1},{3,2},{4,3},{5,4},{6,5},{7,6},{8,7},{9,8},{10,9},{11,1... | collective-permute-start | bytes 1572872 | tf_op jit(solution)/shard_map/ppermute | solution.py:510
  16.4 0.6 copy-start.9
  17.0 4.9 %collective-permute-start.5 = (f32[192,128]{1,0:T(8,128)S(1)}, f32[192,128]{1,0:T(8,128)S(1)}, u32[]{:S(2)}, u32[]{:S(2)}) collective-permute-start(f32[192,128]{1,0:T(8,128)S(1)} %select_select_fusion), channel_id=1, source_target_pairs={{0,128},{32,160},{64,192},{96,224},{1,129},{33,161},{65,193},{97,2... | collective-permute-start | bytes 294920 | tf_op jit(solution)/shard_map/ppermute | solution.py:459
  22.0 15.1 %collective-permute-start.8 = (f32[192,128]{1,0:T(8,128)S(1)}, f32[192,128]{1,0:T(8,128)S(1)}, u32[]{:S(2)}, u32[]{:S(2)}) collective-permute-start(f32[192,128]{1,0:T(8,128)S(1)} %broadcast_select_fusion.q0), channel_id=1, source_target_pairs={{0,96},{32,0},{64,32},{96,64},{128,224},{160,128},{192,160},{224,1... | collective-permute-start | bytes 294920 | tf_op jit(solution)/shard_map/ppermute | solution.py:464
  25.8 11.2 %collective-permute-start.7 = (f32[192,128]{1,0:T(8,128)S(1)}, f32[192,128]{1,0:T(8,128)S(1)}, u32[]{:S(2)}, u32[]{:S(2)}) collective-permute-start(f32[192,128]{1,0:T(8,128)S(1)} %broadcast_select_fusion.q0), channel_id=1, source_target_pairs={{0,64},{32,96},{64,0},{96,32},{128,192},{160,224},{192,128},{224,1... | collective-permute-start | bytes 294920 | tf_op jit(solution)/shard_map/ppermute | solution.py:464
  26.2 10.9 %collective-permute-start.6 = (f32[192,128]{1,0:T(8,128)S(1)}, f32[192,128]{1,0:T(8,128)S(1)}, u32[]{:S(2)}, u32[]{:S(2)}) collective-permute-start(f32[192,128]{1,0:T(8,128)S(1)} %broadcast_select_fusion.q0), channel_id=1, source_target_pairs={{0,32},{32,64},{64,96},{96,0},{128,160},{160,192},{192,224},{224,1... | collective-permute-start | bytes 294920 | tf_op jit(solution)/shard_map/ppermute | solution.py:464
  26.9 1.2 %copy-start.1 = (f32[1,256,8,128]{3,2,1,0:T(8,128)S(1)}, f32[1,256,8,128]{3,2,1,0:T(8,128)}, u32[]{:S(2)}) copy-start(f32[1,256,8,128]{3,2,1,0:T(8,128)} %param.10) | copy-start | bytes 3145732
  28.1 1.2 %copy-start.2 = (s32[1,256,8,128]{3,2,1,0:T(8,128)S(1)}, s32[1,256,8,128]{3,2,1,0:T(8,128)}, u32[]{:S(2)}) copy-start(s32[1,256,8,128]{3,2,1,0:T(8,128)} %param.11) | copy-start | bytes 3145732
  29.3 7.7 %copy-start.3 = (f32[896,128]{1,0:T(8,128)S(1)}, f32[896,128]{1,0:T(8,128)}, u32[]{:S(2)}) copy-start(f32[896,128]{1,0:T(8,128)} %constant.26.clone.later_ref) | copy-start | bytes 1376260
  29.3 7.7 %copy-start.4 = (f32[896,128]{1,0:T(8,128)S(1)}, f32[896,128]{1,0:T(8,128)}, u32[]{:S(2)}) copy-start(f32[896,128]{1,0:T(8,128)} %constant.25.clone.table_ref) | copy-start | bytes 1376260
  29.3 7.8 %copy-start.7 = (f32[32]{0:T(128)S(1)}, f32[32]{0:T(128)}, u32[]{:S(2)}) copy-start(f32[32]{0:T(128)} %constant.24.clone.profile_ref) | copy-start | bytes 388
  37.0 25.3 %copy-start.5 = (f32[256,128]{1,0:T(8,128)S(1)}, f32[256,128]{1,0:T(8,128)}, u32[]{:S(2)}) copy-start(f32[256,128]{1,0:T(8,128)} %constant.28.clone.wrap_ref) | copy-start | bytes 393220
  37.0 25.2 %copy-start.6 = (f32[256,128]{1,0:T(8,128)S(1)}, f32[256,128]{1,0:T(8,128)}, u32[]{:S(2)}) copy-start(f32[256,128]{1,0:T(8,128)} %constant.27.clone.step_ref) | copy-start | bytes 393220
  63.1 15.3 %all-to-all-start.1 = ((f32[32,2,8,128]{3,2,1,0:T(8,128)}), f32[32,2,8,128]{3,2,1,0:T(8,128)S(1)}, u32[]{:S(2)}, u32[]{:S(2)}) async-start(f32[32,2,8,128]{3,2,1,0:T(8,128)} %far.1), calls=%async_computation.1 | async-start | bytes 524288 | tf_op jit(solution)/shard_map/all_to_all | solution.py:557
  66.9 4.7 %collective-permute-start.9 = (f32[256,128]{1,0:T(8,128)S(1)}, f32[256,128]{1,0:T(8,128)S(1)}, u32[]{:S(2)}, u32[]{:S(2)}) collective-permute-start(f32[256,128]{1,0:T(8,128)S(1)} %get-tuple-element.22), channel_id=1, source_target_pairs={{0,1},{1,2},{2,3},{3,4},{4,5},{5,6},{6,7},{7,8},{8,9},{9,10},{10,1... | collective-permute-start | bytes 393224 | tf_op jit(solution)/shard_map/ppermute | solution.py:547
  68.7 5.3 %collective-permute-start.10 = (f32[256,128]{1,0:T(8,128)S(1)}, f32[256,128]{1,0:T(8,128)S(1)}, u32[]{:S(2)}, u32[]{:S(2)}) collective-permute-start(f32[256,128]{1,0:T(8,128)S(1)} %get-tuple-element.23), channel_id=1, source_target_pairs={{1,0},{2,1},{3,2},{4,3},{5,4},{6,5},{7,6},{8,7},{9,8},{10,9},{11,1... | collective-permute-start | bytes 393224 | tf_op jit(solution)/shard_map/ppermute | solution.py:548

commit v3 on v2

--- a/solution.py
+++ b/solution.py
@@ -100,39 +100,46 @@
     return pl.ds(first, count, stride=ROWS)
 
 
-def fringe_kernel(start_ref, vel_ref, q0, q1, q2, q3, sems):
-    first = pl.multiple_of(start_ref[0] * ROWS, ROWS)
-    rows = FR * ROWS
-    quarter = 3 * rows // 4
-    pairs = []
-    for k, out in enumerate((q0, q1, q2, q3)):
-        at = k * quarter
-        while at < (k + 1) * quarter:
-            c, inner = divmod(at, rows)
-            size = min(rows - inner, (k + 1) * quarter - at)
-            pairs.append((vel_ref.at[c, pl.ds(first + inner, size)], out.at[pl.ds(at - k * quarter, size)]))
-            at += size
-    wait_all(start_all(pairs, sems))
-
-
 EDGE_CHUNKS = 4
 
 
-def edges_kernel(vel_in, visc_in, low_ref, high_ref, vel_ref, visc_ref, sems):
+def edges_kernel(
+    start_ref, vel_in, visc_in, q0, q1, q2, q3, low_out, high_out,
+    vel_ref, visc_ref, low_ref, high_ref, sems, out_sems, piece_sems,
+):
     part = CELLS // EDGE_CHUNKS
     pairs = []
     for k in range(EDGE_CHUNKS):
         rows = pl.ds(k * part, part)
-        pairs += [(vel_in.at[c, rows], vel_ref.at[c, rows]) for c in range(3)]
-        pairs.append((visc_in.at[rows], visc_ref.at[rows]))
+        pairs += [(vel_in.at[:, rows], vel_ref.at[:, rows]), (visc_in.at[rows], visc_ref.at[rows])]
     copies = start_all(pairs, sems)
     count = NX // EDGE_CHUNKS
+    outs = []
     for k in range(EDGE_CHUNKS):
-        wait_all(copies[4 * k : 4 * k + 4])
+        wait_all(copies[2 * k : 2 * k + 2])
+        planes = pl.ds(k * count, count)
         for row, out in ((0, low_ref), (ROWS - 1, high_ref)):
             for c in range(3):
-                out[c, pl.ds(k * count, count), :] = vel_ref[c, every8(k * part + row, count), :]
-            out[3, pl.ds(k * count, count), :] = visc_ref[every8(k * part + row, count), :]
+                out[c, planes, :] = vel_ref[c, every8(k * part + row, count), :]
+            out[3, planes, :] = visc_ref[every8(k * part + row, count), :]
+        if k == EDGE_CHUNKS - 1:
+            first = pl.multiple_of(start_ref[0] * ROWS, ROWS)
+            rows = FR * ROWS
+            quarter = 3 * rows // 4
+            pairs = []
+            for n, out in enumerate((q0, q1, q2, q3)):
+                at = n * quarter
+                while at < (n + 1) * quarter:
+                    c, inner = divmod(at, rows)
+                    size = min(rows - inner, (n + 1) * quarter - at)
+                    from_rows, to_rows = pl.ds(first + inner, size), pl.ds(at - n * quarter, size)
+                    pairs.append((vel_ref.at[c, from_rows], out.at[to_rows]))
+                    at += size
+            outs += start_all(pairs, piece_sems)
+        for side, (plane, to) in enumerate(((low_ref, low_out), (high_ref, high_out))):
+            outs.append(pltpu.make_async_copy(plane.at[:, planes], to.at[:, planes], out_sems.at[2 * k + side]))
+            outs[-1].start()
+    wait_all(outs)
 
 
 def iotas():
@@ -146,69 +153,44 @@
     return pl.ds(pl.multiple_of(x * ROWS, ROWS), ROWS)
 
 
-CHUNKS = 8
-
-
-def diffuse_kernel(vel_in, visc_in, turb_in, prev_in, next_in, out_ref, vel_ref, visc_ref, turb_ref, prev_ref, next_ref, rim, sems):
-    part = CELLS // CHUNKS
-    spans = [pl.ds(k * part, part) for k in (CHUNKS - 1, *range(CHUNKS - 1))]
-    pairs = [(prev_in, prev_ref), (next_in, next_ref)]
-    for span in spans:
-        pairs += [(vel_in.at[:, span], vel_ref.at[:, span]), (visc_in.at[span], visc_ref.at[span])]
-        pairs.append((turb_in.at[span], turb_ref.at[span]))
-    copies = start_all(pairs, sems)
-    wait_all(copies[:2])
-    for c in range(4):
-        rim[c, every8(0), :] = prev_ref[c]
-        rim[c, every8(ROWS - 1), :] = next_ref[c]
-    wait_all(copies[2:8])
+def diffuse_kernel(vel_ref, visc_ref, turb_ref, *refs):
+    *_, out_ref, disc_ref = refs
     row, lane = iotas()
-    first_row, last_row = row == 0, row == ROWS - 1
-    first_lane, last_lane = lane == 0, lane == NZ - 1
+    last_row, last_lane = row == ROWS - 1, lane == NZ - 1
+    inner = jnp.where((row == 0) | last_row, 0.0, DRAG).astype(jnp.float32)
 
     def fields_at(x):
         return [vel_ref[c, tile(x), :] for c in range(3)], visc_ref[tile(x), :]
-
-    def flux(nu_sum, a, b):
-        return nu_sum * (b - a)
 
     def step(x, carry):
         now, nu, back = carry
         ahead, nu_ahead = fields_at(lax.rem(x + 1, NX))
-        nu_rim = rim[3, tile(x), :]
         half = 0.5 * nu
         sum_x = half + 0.5 * nu_ahead
-        half_rim = half + 0.5 * nu_rim
-        sum_y = jnp.where(last_row, half_rim, half + pltpu.roll(half, ROWS - 1, 0))
+        sum_y = jnp.where(last_row, 0.0, half + pltpu.roll(half, ROWS - 1, 0))
         sum_z = jnp.where(last_lane, 0.0, half + pltpu.roll(half, NZ - 1, 1))
         fluxes = []
         for c in range(3):
             u = now[c]
-            edge = rim[c, tile(x), :]
             flux_x = sum_x * (ahead[c] - u)
-            flux_y = sum_y * (jnp.where(last_row, edge, pltpu.roll(u, ROWS - 1, 0)) - u)
-            down_y = jnp.where(first_row, half_rim * (u - edge), pltpu.roll(flux_y, 1, 0))
+            flux_y = sum_y * (pltpu.roll(u, ROWS - 1, 0) - u)
             flux_z = sum_z * (pltpu.roll(u, NZ - 1, 1) - u)
-            down_z = pltpu.roll(flux_z, 1, 1)
+            down_y, down_z = pltpu.roll(flux_y, 1, 0), pltpu.roll(flux_z, 1, 1)
             new = u + (flux_x - back[c]) + (flux_y - down_y) + (flux_z - down_z)
             if c == 0:
                 disc = turb_ref[tile(x), :].astype(jnp.float32)
-                new = new - DRAG * disc * new * jnp.abs(new)
+                new = new - inner * disc * new * jnp.abs(new)
             out_ref[c, tile(x), :] = new
             fluxes.append(flux_x)
         return ahead, nu_ahead, fluxes
 
-    del first_lane
-    last, nu_last = fields_at(NX - 1)
+    before, nu_before = fields_at(NX - 1)
     now, nu = fields_at(0)
-    sum_x = 0.5 * nu_last + 0.5 * nu
-    back = [flux(sum_x, last[c], now[c]) for c in range(3)]
-    carry = (now, nu, back)
-    count = NX // CHUNKS
-    for k in range(CHUNKS):
-        if k < CHUNKS - 2:
-            wait_all(copies[8 + 3 * k : 11 + 3 * k])
-        carry = lax.fori_loop(k * count, (k + 1) * count, step, carry, unroll=16)
+    sum_x = 0.5 * nu_before + 0.5 * nu
+    back = [sum_x * (now[c] - before[c]) for c in range(3)]
+    lax.fori_loop(0, NX, step, (now, nu, back), unroll=16)
+    for side, at in enumerate((0, ROWS - 1)):
+        disc_ref[side] = turb_ref[every8(at), :].astype(jnp.float32)
 
 
 def centred_z(value, first_lane, last_lane):
@@ -230,9 +212,11 @@
 
 
 def forward_kernel(
-    start_ref, field_ref, q0, q1, q2, q3, profile_ref, table_ref, later_ref,
-    store, pay_ref, low_ref, high_ref, out_ref, fringe, div, modes, hat_ref, sems,
+    start_ref, field_ref, disc_ref, low_in, high_in, prev_in, next_in, q0, q1, q2, q3, profile_ref, table_ref, later_ref,
+    store, pay_ref, low_ref, high_ref, out_ref, rims, fringe, div, modes, hat_ref, sems, rim_sems,
 ):
+    del field_ref
+    planes = start_all([(p, rims.at[k]) for k, p in enumerate((low_in, prev_in, high_in, next_in))], rim_sems)
     copies = start_all([(later_ref, store.at[pl.ds(STORE_LATER, LATER)])], sems)
     me = lax.axis_index("sim")
     active = jnp.where(me == 0, 0.0, 1.0).astype(jnp.float32)
@@ -244,8 +228,16 @@
     first_row, last_row = row == 0, row == ROWS - 1
     first_lane, last_lane = lane == 0, lane == NZ - 1
 
-    for c in range(3):
-        out_ref[c] = field_ref[c]
+    for side in range(2):
+        wait_all(planes[2 * side : 2 * side + 2])
+        at = every8(side * (ROWS - 1))
+        own, other = 2 * side, 2 * side + 1
+        faces = 0.5 * (rims[own, 3] + rims[other, 3])
+        for c in range(3):
+            plane = out_ref[c, at, :] + faces * (rims[other, c] - rims[own, c])
+            if c == 0:
+                plane = plane - DRAG * disc_ref[side] * plane * jnp.abs(plane)
+            out_ref[c, at, :] = plane
     start = start_ref[0]
 
     def blend(i, _):
@@ -450,14 +442,33 @@
     wait_all(copies)
 
 
-def fringe_quarters(piece):
+def pick_kernel(which, count, *refs):
+    *pieces, out_ref = refs[: count] + refs[-1:]
     me = lax.axis_index("sim")
-    mine = piece[0]
-    for k in (1, 2, 3):
-        came = lax.ppermute(piece[k], "sim", [(0, k)])
-        mine = jnp.where(me == k, came, mine)
-    came = lax.ppermute(mine, "sim", [(i, i + 4) for i in range(4)])
-    mine = jnp.where(me >= 4, came, mine)
+    for k, piece in enumerate(pieces):
+
+        @pl.when(which(me) == k)
+        def _(piece=piece):
+            out_ref[...] = piece[...]
+
+
+def pick(name, which, pieces, *after):
+    (out,) = call(
+        functools.partial(pick_kernel, which, len(pieces)),
+        [pieces[0].shape],
+        name,
+        in_specs=[VM] * len(pieces) + [HB] * len(after),
+        nbytes=2**18,
+    )(*pieces, *after)
+    return out
+
+
+def scatter_y(piece):
+    came = [lax.ppermute(piece[k], "sim", [(0, k)]) for k in (1, 2, 3)]
+    return pick("pick_y", lambda me: lax.rem(me, 4), [piece[0], *came])
+
+
+def gather_y(mine):
     quarters = [mine]
     for k in (1, 2, 3):
         pairs = [(4 * z + i, 4 * z + (i + k) % 4) for z in range(2) for i in range(4)]
@@ -483,67 +494,59 @@
     f32 = jnp.float32
     quarter = (3 * FR * ROWS // 4, NZ)
     plane = (NX, NZ)
-    pieces = call(
-        fringe_kernel,
-        [quarter] * 4,
-        "fringe",
-        room=60,
-        in_specs=[SM, HB],
-        scratch=[pltpu.SemaphoreType.DMA((6,))],
-        nbytes=2**19,
-    )(fringe_start, vel)
-    quarters = fringe_quarters(pieces)
-    low, high = call(
+    *pieces, low, high = call(
         edges_kernel,
-        [(4, NX, NZ), (4, NX, NZ)],
+        [quarter] * 4 + [(4, NX, NZ)] * 2,
         "edges",
         room=60,
-        in_specs=[HB, HB],
+        in_specs=[SM, HB, HB],
+        out_specs=[HB] * 6,
         scratch=[
             pltpu.VMEM((3, CELLS, NZ), f32),
             pltpu.VMEM((CELLS, NZ), f32),
-            pltpu.SemaphoreType.DMA((4 * EDGE_CHUNKS,)),
+            pltpu.VMEM((4, NX, NZ), f32),
+            pltpu.VMEM((4, NX, NZ), f32),
+            pltpu.SemaphoreType.DMA((2 * EDGE_CHUNKS,)),
+            pltpu.SemaphoreType.DMA((2 * EDGE_CHUNKS,)),
+            pltpu.SemaphoreType.DMA((6,)),
         ],
         nbytes=6 * 2**20,
-    )(vel, visc)
+    )(fringe_start, vel, visc)
     prev = lax.ppermute(high, "slab", upward)
     following = lax.ppermute(low, "slab", downward)
-    (fields,) = call(
+
+    mine = scatter_y(pieces)
+    came = lax.ppermute(mine, "sim", [(i, i + 4) for i in range(4)])
+    fields, discs = call(
         diffuse_kernel,
-        [(3, CELLS, NZ)],
+        [(3, CELLS, NZ), (2, NX, NZ)],
         "diffuse",
         room=DIFFUSE_ROOM,
-        in_specs=[HB] * 5,
-        scratch=[
-            pltpu.VMEM((3, CELLS, NZ), f32),
-            pltpu.VMEM((CELLS, NZ), f32),
-            pltpu.VMEM((CELLS, NZ), jnp.int32),
-            pltpu.VMEM((4, NX, NZ), f32),
-            pltpu.VMEM((4, NX, NZ), f32),
-            pltpu.VMEM((4, CELLS, NZ), f32),
-            pltpu.SemaphoreType.DMA((2 + 3 * CHUNKS,)),
-        ],
+        in_specs=[VM] * 3 + [HB],
         flops=2**26,
-        nbytes=12 * 2**20,
-    )(vel, visc, turb, prev, following)
-    store, pay, v_low, v_high = call(
+        nbytes=8 * 2**20,
+    )(vel, visc, turb, mine)
+    quarters = gather_y(pick("pick_z", lambda me: me // 4, [mine, came], discs))
+    store, pay, v_low, v_high, _ = call(
         forward_kernel,
-        [(STORE, NZ), (SLABS, 2, ROWS, NZ), plane, plane],
+        [(STORE, NZ), (SLABS, 2, ROWS, NZ), plane, plane, (3, CELLS, NZ)],
         "forward",
         room=FORWARD_ROOM,
-        in_specs=[SM] + [VM] * 5 + [SM] + [VM] * 2,
-        out_specs=[HB, VM, VM, VM],
+        in_specs=[SM] + [VM] * 2 + [HB] * 4 + [VM] * 4 + [SM] + [VM] * 2,
+        out_specs=[HB, VM, VM, VM, VM],
         scratch=[
-            pltpu.VMEM((3, CELLS, NZ), f32),
+            pltpu.VMEM((4, 4, NX, NZ), f32),
             pltpu.VMEM((3 * FR * ROWS, NZ), f32),
             pltpu.VMEM((CELLS, NZ), f32),
             pltpu.VMEM((CELLS, NZ), f32),
             pltpu.VMEM((EXT, NX, NZ), f32),
             pltpu.SemaphoreType.DMA((4 + EXT,)),
+            pltpu.SemaphoreType.DMA((4,)),
         ],
         flops=2**30,
         nbytes=10 * 2**20,
-    )(fringe_start, fields, *quarters, profile, table, later)
+        input_output_aliases={1: 4},
+    )(fringe_start, fields, discs, low, high, prev, following, *quarters, profile, table, later)
     v_prev = lax.ppermute(v_high, "slab", upward)
     v_next = lax.ppermute(v_low, "slab", downward)
     pay = lax.all_to_all(pay, "slab", split_axis=0, concat_axis=0, tiled=True)

time: 86.1 us -> 84.8 us (0.985)
  Pallas kernels: 25.1 us -> 19.9 us
  waiting for transfers between devices: 11.4 us -> 16.6 us
  starting transfers between devices: 24.2 us -> 21.2 us
  blocking collectives: 20.4 us -> 22.3 us
    ppermute x7, waiting for transfers between devices: 1.63 us -> 6.9 us  [the longest x3 4.98 us: gather_y(): quarters.append(lax.ppermute(mine, 'sim', pairs))]
    pallas_call x4 -> x5, Pallas kernels: 17.6 us -> 12.4 us  [the longest x1 5.08 us: local(): call(forward_kernel, [(STORE, NZ), (SLABS, 2, ROWS, NZ), plane, plane, (3...]
    ppermute x7, starting transfers between devices: 16.5 us -> 12.3 us  [the longest x3 6.22 us: scatter_y(): came = [lax.ppermute(piece[k], 'sim', [(0, k)]) for k in (1, 2, 3)]]
    ppermute x1, starting transfers between devices: 0.01 us -> 3.32 us  [local(): following = lax.ppermute(low, 'slab', downward)]
    ppermute x1, starting transfers between devices: 2.13 us -> 0.01 us  [local(): prev = lax.ppermute(high, 'slab', upward)]
    all_to_all x1, blocking collectives: 20.4 us -> 22.3 us  [local(): pay = lax.all_to_all(pay, 'slab', split_axis=0, concat_axis=0, tiled=True)]
    unnamed x20 -> x22, local copies, waits for them, and re-layouts: 3.11 us -> 3.37 us
  transfers between devices with their start and end apart: 12 -> 12, of which waited for: 4 -> 8; matrix products, arithmetic and copies ran while one was open for 0% -> 0% of each run, Pallas kernels for 13% -> 5%
where the time goes in v3:
time: 84.8 us; the launch traced here: 84.4 us
  blocking collectives  22.3 us (26%)
  starting transfers between devices  21.2 us (25%)
  Pallas kernels  19.9 us (23%)
  waiting for transfers between devices  16.6 us (20%)
  local copies, waits for them, and re-layouts  3.37 us (4%)
  between operations  0.98 us (1%)
    all_to_all x1, blocking collectives, local(): pay = lax.all_to_all(pay, 'slab', split_axis=0, concat_axis=0, tiled=True)  22.3 us
    pallas_call x1, Pallas kernels, local(): call(final_kernel, [(3, CELLS, NZ)], 'final', room=FORWARD_ROOM, in_specs...  6.64 us
    ppermute x3, starting transfers between devices, scatter_y(): came = [lax.ppermute(piece[k], 'sim', [(0, k)]) for k in (1, 2, 3)]  6.22 us
    pallas_call x1, Pallas kernels, local(): call(forward_kernel, [(STORE, NZ), (SLABS, 2, ROWS, NZ), plane, plane, (3...  5.08 us
    ppermute x3, waiting for transfers between devices, gather_y(): quarters.append(lax.ppermute(mine, 'sim', pairs))  4.98 us
    all_to_all x1, waiting for transfers between devices, local(): ret = lax.all_to_all(ret, 'slab', split_axis=0, concat_axis=0, tiled=True)  4.39 us
    pallas_call x1, Pallas kernels, local(): call(diffuse_kernel, [(3, CELLS, NZ), (2, NX, NZ)], 'diffuse', room=DIFFU...  3.94 us
    ppermute x3, starting transfers between devices, gather_y(): quarters.append(lax.ppermute(mine, 'sim', pairs))  3.84 us
  transfers between devices with their start and end apart: 12, of which 8 were waited for; matrix products, arithmetic and copies ran while one was open for 0% of the time, Pallas kernels for 5%

profile of v3, /device:TPU:1, one launch (start us, length us, event | category | flops | bytes accessed | tf_op | source)
XLA Modules:
  0.0 84.4 jit_solution(6182251434623476280)
XLA Ops:
  0.0 0.0 copy-start
  0.8 3.4 %edges.1 = (f32[192,128]{1,0:T(8,128)}, f32[192,128]{1,0:T(8,128)}, f32[192,128]{1,0:T(8,128)}, f32[192,128]{1,0:T(8,128)}, f32[4,256,128]{2,1,0:T(8,128)}, /*index=5*/f32[4,256,128]{2,1,0:T(8,128)}) custom-call(s32[1]{0:T(128)S(6)} %copy.12.start_ref, f32[3,2048,128]{2,1,0:T(8,128)} %bitcast.4, f32[2048,128]{1,0:T(8,128)} %bitcast.6), custom_call_target="tpu_custom_call" | custom-call | bytes 6291456 | tf_op jit(solution)/shard_map/edges/pallas_call | solution.py:497
  4.2 3.3 %collective-permute-start.4 = (f32[4,256,128]{2,1,0:T(8,128)}, f32[4,256,128]{2,1,0:T(8,128)S(1)}, u32[]{:S(2)}, u32[]{:S(2)}) collective-permute-start(f32[4,256,128]{2,1,0:T(8,128)} %get-tuple-element.23.low_in), channel_id=1, source_target_pairs={{1,0},{2,1},{3,2},{4,3},{5,4},{6,5},{7,6},{8,7},{9,8},{10,9},{11,1... | collective-permute-start | bytes 1572872 | tf_op jit(solution)/shard_map/ppermute | solution.py:516
  7.5 0.0 collective-permute-start.3
  7.5 2.6 %collective-permute-start = (f32[192,128]{1,0:T(8,128)}, f32[192,128]{1,0:T(8,128)S(1)}, u32[]{:S(2)}, u32[]{:S(2)}) collective-permute-start(f32[192,128]{1,0:T(8,128)} %get-tuple-element.18), channel_id=1, source_target_pairs={{0,32},{1,33},{2,34},{3,35},{4,36},{5,37},{6,38},{7,39},{8,40},{9,... | collective-permute-start | bytes 294920 | tf_op jit(solution)/shard_map/ppermute | solution.py:467
  10.2 2.3 %collective-permute-start.1 = (f32[192,128]{1,0:T(8,128)}, f32[192,128]{1,0:T(8,128)S(1)}, u32[]{:S(2)}, u32[]{:S(2)}) collective-permute-start(f32[192,128]{1,0:T(8,128)} %get-tuple-element.19), channel_id=1, source_target_pairs={{0,64},{1,65},{2,66},{3,67},{4,68},{5,69},{6,70},{7,71},{8,72},{9,... | collective-permute-start | bytes 294920 | tf_op jit(solution)/shard_map/ppermute | solution.py:467
  12.4 1.3 %collective-permute-start.2 = (f32[192,128]{1,0:T(8,128)}, f32[192,128]{1,0:T(8,128)S(1)}, u32[]{:S(2)}, u32[]{:S(2)}) collective-permute-start(f32[192,128]{1,0:T(8,128)} %get-tuple-element.20), channel_id=1, source_target_pairs={{0,96},{1,97},{2,98},{3,99},{4,100},{5,101},{6,102},{7,103},{8,104... | collective-permute-start | bytes 294920 | tf_op jit(solution)/shard_map/ppermute | solution.py:467
  13.7 0.0 collective-permute-done.refs_1_
  13.8 0.6 collective-permute-done.1.refs_2_
  14.4 1.3 %collective-permute-done.2.refs_3_ = f32[192,128]{1,0:T(8,128)S(1)} collective-permute-done((f32[192,128]{1,0:T(8,128)}, f32[192,128]{1,0:T(8,128)S(1)}, u32[]{:S(2)}, u32[]{:S(2)}) %collective-permute-start.2) | collective-permute-done | bytes 98336 | tf_op jit(solution)/shard_map/ppermute | solution.py:467
  15.7 0.0 copy-start.9
  15.7 0.9 %copy-done.9 = f32[192,128]{1,0:T(8,128)S(1)} copy-done((f32[192,128]{1,0:T(8,128)S(1)}, f32[192,128]{1,0:T(8,128)}, u32[]{:S(2)}) %copy-start.9) | copy-done | bytes 98328
  16.6 0.0 copy-start.5
  16.6 0.0 copy-start.10
  16.6 2.3 %collective-permute-start.5 = (f32[192,128]{1,0:T(8,128)S(1)}, f32[192,128]{1,0:T(8,128)S(1)}, u32[]{:S(2)}, u32[]{:S(2)}) collective-permute-start(f32[192,128]{1,0:T(8,128)S(1)} %pick_y.1.refs_0_), channel_id=1, source_target_pairs={{0,128},{32,160},{64,192},{96,224},{1,129},{33,161},{65,193},{97,2... | collective-permute-start | bytes 294920 | tf_op jit(solution)/shard_map/ppermute | solution.py:519
  18.9 0.0 copy-done
  18.9 0.0 copy-start.1
  18.9 1.2 %copy-done.1 = f32[1,256,8,128]{3,2,1,0:T(8,128)S(1)} copy-done((f32[1,256,8,128]{3,2,1,0:T(8,128)S(1)}, f32[1,256,8,128]{3,2,1,0:T(8,128)}, u32[]{:S(2)}) %copy-start.1) | copy-done | bytes 1048600
  20.1 1.2 %copy-done.2 = s32[1,256,8,128]{3,2,1,0:T(8,128)S(1)} copy-done((s32[1,256,8,128]{3,2,1,0:T(8,128)S(1)}, s32[1,256,8,128]{3,2,1,0:T(8,128)}, u32[]{:S(2)}) %copy-start.2) | copy-done | bytes 1048600
  21.3 3.9 %diffuse.1 = (f32[3,2048,128]{2,1,0:T(8,128)S(1)}, f32[2,256,128]{2,1,0:T(8,128)S(1)}) custom-call(f32[3,2048,128]{2,1,0:T(8,128)S(1)} %bitcast.5, f32[2048,128]{1,0:T(8,128)S(1)} %bitcast.7, s32[2048,128]{1,0:T(8,128)S(1)} %bitcast.8, f32[192,128]{1,0:T(8,128)S(1)} %pick_y.1.refs_0_), custom_call_target="tpu_custom_call" | custom-call | flops 67108864 | bytes 8388608 | tf_op jit(solution)/shard_map/diffuse/pallas_call | solution.py:520
  25.3 0.0 collective-permute-done.5.refs_1_
  25.3 2.8 %collective-permute-start.8 = (f32[192,128]{1,0:T(8,128)S(1)}, f32[192,128]{1,0:T(8,128)S(1)}, u32[]{:S(2)}, u32[]{:S(2)}) collective-permute-start(f32[192,128]{1,0:T(8,128)S(1)} %pick_z.1.q0), channel_id=1, source_target_pairs={{0,96},{32,0},{64,32},{96,64},{128,224},{160,128},{192,160},{224,1... | collective-permute-start | bytes 294920 | tf_op jit(solution)/shard_map/ppermute | solution.py:475
  28.1 0.4 collective-permute-start.7
  28.5 0.7 collective-permute-start.6
  29.2 0.6 collective-permute-done.8.q3
  29.8 3.4 %collective-permute-done.7.q2 = f32[192,128]{1,0:T(8,128)S(1)} collective-permute-done((f32[192,128]{1,0:T(8,128)S(1)}, f32[192,128]{1,0:T(8,128)S(1)}, u32[]{:S(2)}, u32[]{:S(2)}) %collective-permute-start.7) | collective-permute-done | bytes 98336 | tf_op jit(solution)/shard_map/ppermute | solution.py:475
  33.2 0.9 %collective-permute-done.6.q1 = f32[192,128]{1,0:T(8,128)S(1)} collective-permute-done((f32[192,128]{1,0:T(8,128)S(1)}, f32[192,128]{1,0:T(8,128)S(1)}, u32[]{:S(2)}, u32[]{:S(2)}) %collective-permute-start.6) | collective-permute-done | bytes 98336 | tf_op jit(solution)/shard_map/ppermute | solution.py:475
  34.2 0.0 collective-permute-done.4.next_in
  34.2 0.0 collective-permute-done.3.prev_in
  34.2 0.0 copy-done.5
  34.2 0.0 copy-done.10
  34.2 0.0 copy-done.3
  34.2 0.0 copy-done.4
  34.2 0.0 copy-done.6
  34.2 0.0 copy-start.7
  34.2 0.0 copy-start.8
  34.2 5.1 %forward.1 = (f32[81920,128]{1,0:T(8,128)}, f32[32,2,8,128]{3,2,1,0:T(8,128)S(1)}, f32[256,128]{1,0:T(8,128)S(1)}, f32[256,128]{1,0:T(8,128)S(1)}, f32[3,2048,128]{2,1,0:T(8,128)S(1)}) custom-call(s32[1]{0:T(128)S(6)} %copy.12.start_ref, f32[3,2048,128]{2,1,0:T(8,128)S(1)} %get-tuple-element.21.field_ref, ...), custom_call_target="tpu_custom_call", output_to_operand_aliasing={{4}: (1, {})} | custom-call | flops 1073741824 | bytes 10485760 | tf_op jit(solution)/shard_map/forward/pallas_call | solution.py:530
  39.3 22.3 %all_to_all.10.pay_ref = f32[32,2,8,128]{3,2,1,0:T(8,128)S(1)} all-to-all(f32[32,2,8,128]{3,2,1,0:T(8,128)S(1)} %get-tuple-element.25), channel_id=1, replica_groups=mesh['sim'=8,'slab'=32] {'slab'}, dimensions={0} | all-to-all | bytes 524288 | tf_op jit(solution)/shard_map/all_to_all | solution.py:552
  61.6 0.0 copy-done.7
  61.6 0.0 copy-done.8
  61.6 0.8 %far.1 = f32[32,2,8,128]{3,2,1,0:T(8,128)} custom-call(f32[32,2,8,128]{3,2,1,0:T(8,128)S(1)} %all_to_all.10.pay_ref, f32[256,128]{1,0:T(8,128)S(1)} %copy-done.8, f32[256,128]{1,0:T(8,128)S(1)} %copy-done.7), custom_call_target="tpu_custom_call" | custom-call | bytes 524288 | tf_op jit(solution)/shard_map/far/pallas_call | solution.py:553
  62.5 3.8 %all-to-all-start.1 = ((f32[32,2,8,128]{3,2,1,0:T(8,128)}), f32[32,2,8,128]{3,2,1,0:T(8,128)S(1)}, u32[]{:S(2)}, u32[]{:S(2)}) async-start(f32[32,2,8,128]{3,2,1,0:T(8,128)} %far.1), calls=%async_computation.1 | async-start | bytes 524288 | tf_op jit(solution)/shard_map/all_to_all | solution.py:560
  66.3 1.7 %collective-permute-start.9 = (f32[256,128]{1,0:T(8,128)S(1)}, f32[256,128]{1,0:T(8,128)S(1)}, u32[]{:S(2)}, u32[]{:S(2)}) collective-permute-start(f32[256,128]{1,0:T(8,128)S(1)} %get-tuple-element.26), channel_id=1, source_target_pairs={{0,1},{1,2},{2,3},{3,4},{4,5},{5,6},{6,7},{7,8},{8,9},{9,10},{10,1... | collective-permute-start | bytes 393224 | tf_op jit(solution)/shard_map/ppermute | solution.py:550
  68.0 0.0 collective-permute-start.10
  68.0 3.0 %collective-permute-done.9.prev_ref = f32[256,128]{1,0:T(8,128)S(1)} collective-permute-done((f32[256,128]{1,0:T(8,128)S(1)}, f32[256,128]{1,0:T(8,128)S(1)}, u32[]{:S(2)}, u32[]{:S(2)}) %collective-permute-start.9) | collective-permute-done | bytes 131104 | tf_op jit(solution)/shard_map/ppermute | solution.py:550
  71.0 2.4 %collective-permute-done.10.next_ref = f32[256,128]{1,0:T(8,128)S(1)} collective-permute-done((f32[256,128]{1,0:T(8,128)S(1)}, f32[256,128]{1,0:T(8,128)S(1)}, u32[]{:S(2)}, u32[]{:S(2)}) %collective-permute-start.10) | collective-permute-done | bytes 131104 | tf_op jit(solution)/shard_map/ppermute | solution.py:551
  73.4 4.4 %all-to-all-done.1.ret_ref = f32[32,2,8,128]{3,2,1,0:T(8,128)S(1)} async-done(((f32[32,2,8,128]{3,2,1,0:T(8,128)}), f32[32,2,8,128]{3,2,1,0:T(8,128)S(1)}, u32[]{:S(2)}, u32[]{:S(2)}) %all-to-all-start.1) | async-done | bytes 262176 | tf_op jit(solution)/shard_map/all_to_all | solution.py:560
  77.8 6.6 %final.1 = f32[3,2048,128]{2,1,0:T(8,128)} custom-call(f32[32,2,8,128]{3,2,1,0:T(8,128)S(1)} %all-to-all-done.1.ret_ref, f32[256,128]{1,0:T(8,128)S(1)} %collective-permute-done.9.prev_ref, f32[256,128]{1,0:T(8,128)S(1)} %collective-permute-done.10.next_ref, f32[81920,128]{1,0:T(8,128)} %get-tuple-element.28.store), custom_call_target="tpu_custom_call" | custom-call | flops 1073741824 | bytes 10485760 | tf_op jit(solution)/shard_map/final/pallas_call | solution.py:561
  (6 shorter events, 0.1 us)
Async XLA Ops:
  0.0 18.9 %copy-start = (f32[1,3,256,8,128]{4,3,2,1,0:T(8,128)S(1)}, f32[1,3,256,8,128]{4,3,2,1,0:T(8,128)}, u32[]{:S(2)}) copy-start(f32[1,3,256,8,128]{4,3,2,1,0:T(8,128)} %param.9) | copy-start | bytes 9437188
  4.2 30.0 %collective-permute-start.4 = (f32[4,256,128]{2,1,0:T(8,128)}, f32[4,256,128]{2,1,0:T(8,128)S(1)}, u32[]{:S(2)}, u32[]{:S(2)}) collective-permute-start(f32[4,256,128]{2,1,0:T(8,128)} %get-tuple-element.23.low_in), channel_id=1, source_target_pairs={{1,0},{2,1},{3,2},{4,3},{5,4},{6,5},{7,6},{8,7},{9,8},{10,9},{11,1... | collective-permute-start | bytes 1572872 | tf_op jit(solution)/shard_map/ppermute | solution.py:516
  7.5 26.7 %collective-permute-start.3 = (f32[4,256,128]{2,1,0:T(8,128)}, f32[4,256,128]{2,1,0:T(8,128)S(1)}, u32[]{:S(2)}, u32[]{:S(2)}) collective-permute-start(f32[4,256,128]{2,1,0:T(8,128)} %get-tuple-element.24.high_in), channel_id=1, source_target_pairs={{0,1},{1,2},{2,3},{3,4},{4,5},{5,6},{6,7},{7,8},{8,9},{9,10},{10,1... | collective-permute-start | bytes 1572872 | tf_op jit(solution)/shard_map/ppermute | solution.py:515
  7.5 6.2 %collective-permute-start = (f32[192,128]{1,0:T(8,128)}, f32[192,128]{1,0:T(8,128)S(1)}, u32[]{:S(2)}, u32[]{:S(2)}) collective-permute-start(f32[192,128]{1,0:T(8,128)} %get-tuple-element.18), channel_id=1, source_target_pairs={{0,32},{1,33},{2,34},{3,35},{4,36},{5,37},{6,38},{7,39},{8,40},{9,... | collective-permute-start | bytes 294920 | tf_op jit(solution)/shard_map/ppermute | solution.py:467
  10.2 4.2 %collective-permute-start.1 = (f32[192,128]{1,0:T(8,128)}, f32[192,128]{1,0:T(8,128)S(1)}, u32[]{:S(2)}, u32[]{:S(2)}) collective-permute-start(f32[192,128]{1,0:T(8,128)} %get-tuple-element.19), channel_id=1, source_target_pairs={{0,64},{1,65},{2,66},{3,67},{4,68},{5,69},{6,70},{7,71},{8,72},{9,... | collective-permute-start | bytes 294920 | tf_op jit(solution)/shard_map/ppermute | solution.py:467
  12.4 3.2 %collective-permute-start.2 = (f32[192,128]{1,0:T(8,128)}, f32[192,128]{1,0:T(8,128)S(1)}, u32[]{:S(2)}, u32[]{:S(2)}) collective-permute-start(f32[192,128]{1,0:T(8,128)} %get-tuple-element.20), channel_id=1, source_target_pairs={{0,96},{1,97},{2,98},{3,99},{4,100},{5,101},{6,102},{7,103},{8,104... | collective-permute-start | bytes 294920 | tf_op jit(solution)/shard_map/ppermute | solution.py:467
  15.7 0.9 %copy-start.9 = (f32[192,128]{1,0:T(8,128)S(1)}, f32[192,128]{1,0:T(8,128)}, u32[]{:S(2)}) copy-start(f32[192,128]{1,0:T(8,128)} %get-tuple-element.17.refs_0_) | copy-start | bytes 294916
  16.6 17.6 %copy-start.5 = (f32[896,128]{1,0:T(8,128)S(1)}, f32[896,128]{1,0:T(8,128)}, u32[]{:S(2)}) copy-start(f32[896,128]{1,0:T(8,128)} %constant.12.clone.later_ref) | copy-start | bytes 1376260
  16.6 17.6 %copy-start.10 = (f32[32]{0:T(128)S(1)}, f32[32]{0:T(128)}, u32[]{:S(2)}) copy-start(f32[32]{0:T(128)} %constant.10.clone.profile_ref) | copy-start | bytes 388
  16.6 8.7 %collective-permute-start.5 = (f32[192,128]{1,0:T(8,128)S(1)}, f32[192,128]{1,0:T(8,128)S(1)}, u32[]{:S(2)}, u32[]{:S(2)}) collective-permute-start(f32[192,128]{1,0:T(8,128)S(1)} %pick_y.1.refs_0_), channel_id=1, source_target_pairs={{0,128},{32,160},{64,192},{96,224},{1,129},{33,161},{65,193},{97,2... | collective-permute-start | bytes 294920 | tf_op jit(solution)/shard_map/ppermute | solution.py:519
  18.9 1.2 %copy-start.1 = (f32[1,256,8,128]{3,2,1,0:T(8,128)S(1)}, f32[1,256,8,128]{3,2,1,0:T(8,128)}, u32[]{:S(2)}) copy-start(f32[1,256,8,128]{3,2,1,0:T(8,128)} %param.10) | copy-start | bytes 3145732
  20.1 1.2 %copy-start.2 = (s32[1,256,8,128]{3,2,1,0:T(8,128)S(1)}, s32[1,256,8,128]{3,2,1,0:T(8,128)}, u32[]{:S(2)}) copy-start(s32[1,256,8,128]{3,2,1,0:T(8,128)} %param.11) | copy-start | bytes 3145732
  21.3 12.8 %copy-start.3 = (f32[4,256,128]{2,1,0:T(8,128)S(1)}, f32[4,256,128]{2,1,0:T(8,128)}, u32[]{:S(2)}) copy-start(f32[4,256,128]{2,1,0:T(8,128)} %get-tuple-element.23.low_in) | copy-start | bytes 1572868
  21.3 12.9 %copy-start.4 = (f32[4,256,128]{2,1,0:T(8,128)S(1)}, f32[4,256,128]{2,1,0:T(8,128)}, u32[]{:S(2)}) copy-start(f32[4,256,128]{2,1,0:T(8,128)} %get-tuple-element.24.high_in) | copy-start | bytes 1572868
  21.3 12.9 %copy-start.6 = (f32[896,128]{1,0:T(8,128)S(1)}, f32[896,128]{1,0:T(8,128)}, u32[]{:S(2)}) copy-start(f32[896,128]{1,0:T(8,128)} %constant.11.clone.table_ref) | copy-start | bytes 1376260
  25.3 4.4 %collective-permute-start.8 = (f32[192,128]{1,0:T(8,128)S(1)}, f32[192,128]{1,0:T(8,128)S(1)}, u32[]{:S(2)}, u32[]{:S(2)}) collective-permute-start(f32[192,128]{1,0:T(8,128)S(1)} %pick_z.1.q0), channel_id=1, source_target_pairs={{0,96},{32,0},{64,32},{96,64},{128,224},{160,128},{192,160},{224,1... | collective-permute-start | bytes 294920 | tf_op jit(solution)/shard_map/ppermute | solution.py:475
  28.1 5.1 %collective-permute-start.7 = (f32[192,128]{1,0:T(8,128)S(1)}, f32[192,128]{1,0:T(8,128)S(1)}, u32[]{:S(2)}, u32[]{:S(2)}) collective-permute-start(f32[192,128]{1,0:T(8,128)S(1)} %pick_z.1.q0), channel_id=1, source_target_pairs={{0,64},{32,96},{64,0},{96,32},{128,192},{160,224},{192,128},{224,1... | collective-permute-start | bytes 294920 | tf_op jit(solution)/shard_map/ppermute | solution.py:475
  28.5 5.7 %collective-permute-start.6 = (f32[192,128]{1,0:T(8,128)S(1)}, f32[192,128]{1,0:T(8,128)S(1)}, u32[]{:S(2)}, u32[]{:S(2)}) collective-permute-start(f32[192,128]{1,0:T(8,128)S(1)} %pick_z.1.q0), channel_id=1, source_target_pairs={{0,32},{32,64},{64,96},{96,0},{128,160},{160,192},{192,224},{224,1... | collective-permute-start | bytes 294920 | tf_op jit(solution)/shard_map/ppermute | solution.py:475
  34.2 27.4 %copy-start.7 = (f32[256,128]{1,0:T(8,128)S(1)}, f32[256,128]{1,0:T(8,128)}, u32[]{:S(2)}) copy-start(f32[256,128]{1,0:T(8,128)} %constant.14.clone.wrap_ref) | copy-start | bytes 393220
  34.2 27.4 %copy-start.8 = (f32[256,128]{1,0:T(8,128)S(1)}, f32[256,128]{1,0:T(8,128)}, u32[]{:S(2)}) copy-start(f32[256,128]{1,0:T(8,128)} %constant.13.clone.step_ref) | copy-start | bytes 393220
  62.5 15.3 %all-to-all-start.1 = ((f32[32,2,8,128]{3,2,1,0:T(8,128)}), f32[32,2,8,128]{3,2,1,0:T(8,128)S(1)}, u32[]{:S(2)}, u32[]{:S(2)}) async-start(f32[32,2,8,128]{3,2,1,0:T(8,128)} %far.1), calls=%async_computation.1 | async-start | bytes 524288 | tf_op jit(solution)/shard_map/all_to_all | solution.py:560
  66.3 4.7 %collective-permute-start.9 = (f32[256,128]{1,0:T(8,128)S(1)}, f32[256,128]{1,0:T(8,128)S(1)}, u32[]{:S(2)}, u32[]{:S(2)}) collective-permute-start(f32[256,128]{1,0:T(8,128)S(1)} %get-tuple-element.26), channel_id=1, source_target_pairs={{0,1},{1,2},{2,3},{3,4},{4,5},{5,6},{6,7},{7,8},{8,9},{9,10},{10,1... | collective-permute-start | bytes 393224 | tf_op jit(solution)/shard_map/ppermute | solution.py:550
  68.0 5.3 %collective-permute-start.10 = (f32[256,128]{1,0:T(8,128)S(1)}, f32[256,128]{1,0:T(8,128)S(1)}, u32[]{:S(2)}, u32[]{:S(2)}) collective-permute-start(f32[256,128]{1,0:T(8,128)S(1)} %get-tuple-element.27), channel_id=1, source_target_pairs={{1,0},{2,1},{3,2},{4,3},{5,4},{6,5},{7,6},{8,7},{9,8},{10,9},{11,1... | collective-permute-start | bytes 393224 | tf_op jit(solution)/shard_map/ppermute | solution.py:551

commit v4 on v3

--- a/solution.py
+++ b/solution.py
@@ -211,22 +211,31 @@
     return jnp.concatenate([table_ref[pl.ds(TAB_X, NX), :], table_ref[pl.ds(TAB_X + NX, NX), :]], 1)
 
 
-def forward_kernel(
-    start_ref, field_ref, disc_ref, low_in, high_in, prev_in, next_in, q0, q1, q2, q3, profile_ref, table_ref, later_ref,
-    store, pay_ref, low_ref, high_ref, out_ref, rims, fringe, div, modes, hat_ref, sems, rim_sems,
-):
-    del field_ref
-    planes = start_all([(p, rims.at[k]) for k, p in enumerate((low_in, prev_in, high_in, next_in))], rim_sems)
-    copies = start_all([(later_ref, store.at[pl.ds(STORE_LATER, LATER)])], sems)
-    me = lax.axis_index("sim")
-    active = jnp.where(me == 0, 0.0, 1.0).astype(jnp.float32)
-    quarter = 3 * FR * ROWS // 4
-    for k, part in enumerate((q0, q1, q2, q3)):
-        at = lax.rem(lax.rem(me, 4) + 4 - k, 4)
-        fringe[pl.ds(pl.multiple_of(at * quarter, ROWS), quarter), :] = part[...]
+def source_loop(read_x, v_ref, w_ref, out_ref, count, carry):
     row, lane = iotas()
     first_row, last_row = row == 0, row == ROWS - 1
     first_lane, last_lane = lane == 0, lane == NZ - 1
+
+    def source(x, carry):
+        behind, now = carry
+        ahead = read_x(x)
+        v, w = v_ref(x), w_ref(x)
+        up = jnp.where(last_row, 0.0, pltpu.roll(v, ROWS - 1, 0))
+        down = jnp.where(first_row, 0.0, pltpu.roll(v, 1, 0))
+        out_ref[tile(x), :] = 0.5 * ((ahead - behind) + (up - down) + centred_z(w, first_lane, last_lane))
+        return now, ahead
+
+    lax.fori_loop(0, count, source, carry, unroll=16)
+
+
+def forward_kernel(
+    start_ref, field_ref, disc_ref, low_in, high_in, prev_in, next_in, after, profile_ref, table_ref, later_ref,
+    store, hat_ref, low_ref, high_ref, out_ref, rims, div, modes, sems, rim_sems,
+):
+    del field_ref, after
+    planes = start_all([(p, rims.at[k]) for k, p in enumerate((low_in, prev_in, high_in, next_in))], rim_sems)
+    copies = start_all([(later_ref, store.at[pl.ds(STORE_LATER, LATER)])], sems)
+    active = jnp.where(lax.axis_index("sim") == 0, 0.0, 1.0).astype(jnp.float32)
 
     for side in range(2):
         wait_all(planes[2 * side : 2 * side + 2])
@@ -241,10 +250,9 @@
     start = start_ref[0]
 
     def blend(i, _):
-        weight = profile_ref[i] * active
+        kept = 1.0 - profile_ref[i] * active
         for c in range(3):
-            old = out_ref[c, tile(start + i), :]
-            out_ref[c, tile(start + i), :] = old + weight * (fringe[tile(c * FR + i), :] - old)
+            out_ref[c, tile(start + i), :] = kept * out_ref[c, tile(start + i), :]
         return 0
 
     lax.fori_loop(0, FR, blend, 0, unroll=8)
@@ -252,18 +260,14 @@
         copies.append(pltpu.make_async_copy(out_ref.at[c], store.at[pl.ds(c * CELLS, CELLS)], sems.at[1 + c]))
         copies[-1].start()
 
-    def source(x, carry):
-        behind, now = carry
-        ahead = out_ref[0, tile(lax.rem(x + 1, NX)), :]
-        v = out_ref[1, tile(x), :]
-        w = out_ref[2, tile(x), :]
-        up = jnp.where(last_row, 0.0, pltpu.roll(v, ROWS - 1, 0))
-        down = jnp.where(first_row, 0.0, pltpu.roll(v, 1, 0))
-        div[tile(x), :] = 0.5 * ((ahead - behind) + (up - down) + centred_z(w, first_lane, last_lane))
-        return now, ahead
-
-    lax.fori_loop(0, NX, source, (out_ref[0, tile(NX - 1), :], out_ref[0, tile(0), :]), unroll=16)
-
+    source_loop(
+        lambda x: out_ref[0, tile(lax.rem(x + 1, NX)), :],
+        lambda x: out_ref[1, tile(x), :],
+        lambda x: out_ref[2, tile(x), :],
+        div,
+        NX,
+        (out_ref[0, tile(NX - 1), :], out_ref[0, tile(0), :]),
+    )
     z_high, z_low = parts(table_ref[pl.ds(TAB_Z, NZ), :])
     for block in range(8):
         rows = pl.ds(block * NX, NX)
@@ -282,16 +286,104 @@
         both = dot3(x_high, x_low, *parts(jnp.concatenate(pair, 1)))
         hat_ref[r] = both[:, :NZ]
         hat_ref[r + 1] = both[:, NZ:]
+    wait_all(copies)
+
+
+WINDOW = 48
+EDGE_WINDOW = FR + 8
+TAB_WINDOW = NX + NZ
+WINDOW_ROWS = NX + 2 * ROWS
+
+
+def dot3_rows(a, b):
+    dims = (((0,), (0,)), ((), ()))
+    dot = functools.partial(lax.dot_general, dimension_numbers=dims, preferred_element_type=jnp.float32)
+    (a_high, a_low), (b_high, b_low) = a, b
+    return dot(a_high, b_high) + (dot(a_high, b_low) + dot(a_low, b_high))
+
+
+def precursor_kernel(
+    start_ref, q0, q1, q2, q3, profile_ref, hat_ref, low_ref, high_ref, table_ref, store_in,
+    store, pay_ref, low_out, high_out, fringe, share, div, modes, rows_ref, edge, sums_ref, sems, row_sems,
+):
+    del store_in
+    start = start_ref[0]
+    me = lax.axis_index("sim")
+    active = jnp.where(me == 0, 0.0, 1.0).astype(jnp.float32)
+    length = FR * ROWS
+    spans = [store.at[pl.ds(pl.multiple_of(c * CELLS + start * ROWS, ROWS), length)] for c in range(3)]
+    loads = start_all([(span, rows_ref.at[c]) for c, span in enumerate(spans)], row_sems)
+    quarter = 3 * length // 4
+    for k, part in enumerate((q0, q1, q2, q3)):
+        at = lax.rem(lax.rem(me, 4) + 4 - k, 4)
+        fringe[pl.ds(pl.multiple_of(at * quarter, ROWS), quarter), :] = part[...]
+
+    base = (start + 7) // 8 * 8 - 8
+    offset = start - base
+    share[...] = jnp.zeros_like(share)
+
+    def weigh_rows(i, _):
+        weight = profile_ref[i] * active
+        for c in range(3):
+            share[c, tile(i + offset + 1), :] = weight * fringe[tile(c * FR + i), :]
+        return 0
+
+    lax.fori_loop(0, FR, weigh_rows, 0, unroll=8)
+    source_loop(
+        lambda x: share[0, tile(x + 2), :],
+        lambda x: share[1, tile(x + 1), :],
+        lambda x: share[2, tile(x + 1), :],
+        div,
+        WINDOW,
+        (share[0, tile(0), :], share[0, tile(1), :]),
+    )
+    z_high, z_low = parts(table_ref[pl.ds(NX, NZ), :])
+    modes[...] = dot3(*parts(div[...]), z_high, z_low)
+    ends = [share[1, every8(ROWS + y, WINDOW), :] for y in (0, ROWS - 1)]
+    low = dot3(*parts(0.5 * ends[0]), z_high, z_low)
+    high = dot3(*parts(-0.5 * ends[1]), z_high, z_low)
+    at = pl.multiple_of(base + 8, ROWS)
+    basis = parts(
+        jnp.concatenate(
+            [table_ref[pl.ds(TAB_WINDOW + half * WINDOW_ROWS + at, WINDOW), :] for half in range(2)], 1
+        )
+    )
+    copies = []
+    for r in range(0, EXT, 2):
+        pair = []
         for k in (r, r + 1):
+            pair.append(low if k == 0 else high if k == EXT - 1 else modes[every8(k - 1, WINDOW), :])
+        both = dot3_rows(basis, parts(jnp.concatenate(pair, 1)))
+        for k in (r, r + 1):
+            sums_ref[k] = hat_ref[k] + (both[:, :NZ] if k == r else both[:, NZ:])
             to = store.at[pl.ds(STORE_HAT + k * NX, NX)]
-            copies.append(pltpu.make_async_copy(hat_ref.at[k], to, sems.at[4 + k]))
+            copies.append(pltpu.make_async_copy(sums_ref.at[k], to, sems.at[k]))
             copies[-1].start()
 
+    wait_all(loads)
+
+    def add_rows(i, _):
+        for c in range(3):
+            rows_ref[c, tile(i), :] = rows_ref[c, tile(i), :] + share[c, tile(i + offset + 1), :]
+        return 0
+
+    lax.fori_loop(0, FR, add_rows, 0, unroll=8)
+    for c, span in enumerate(spans):
+        copies.append(pltpu.make_async_copy(rows_ref.at[c], span, sems.at[EXT + c]))
+        copies[-1].start()
+    first = pl.multiple_of(start // 8 * 8, ROWS)
+    for y, own, out in ((0, low_ref, low_out), (ROWS - 1, high_ref, high_out)):
+        edge[pl.ds(0, NX), :] = own[...]
+        to = pl.ds(first, EDGE_WINDOW)
+        edge[to, :] = edge[to, :] + share[1, every8((first - base + 1) * ROWS + y, EDGE_WINDOW), :]
+        out[...] = edge[pl.ds(0, NX), :]
+
+    row, lane = iotas()
     origin = (row == 0) & (lane == 0)
 
     def sums(block, at):
         mu = table_ref[at, :]
-        rows = [hat_ref[r, at, :] for r in range(EXT)]
+        rows = [sums_ref[r, at, :] for r in range(EXT)]
         right = rows[0]
         for value in rows[1:]:
             right = mu * right + value
@@ -487,6 +579,9 @@
         np.concatenate([mu, x[:, :NZ], x[:, NZ:], z]).astype(np.float32)
         for x, z in ((x_basis, z_basis.T), (x_basis.T, z_basis))
     )
+    around = np.arange(-ROWS, NX + ROWS) % NX
+    near = x_basis.T[around]
+    near_table = np.concatenate([mu, z_basis.T, near[:, :NZ], near[:, NZ:]]).astype(np.float32)
     profile = (np.sin(math.pi * (np.arange(FR) + 0.5) / FR) ** 2).astype(np.float32)
     upward = [(i, (i + 1) % SLABS) for i in range(SLABS)]
     downward = [((i + 1) % SLABS, i) for i in range(SLABS)]
@@ -527,26 +622,46 @@
         nbytes=8 * 2**20,
     )(vel, visc, turb, mine)
     quarters = gather_y(pick("pick_z", lambda me: me // 4, [mine, came], discs))
-    store, pay, v_low, v_high, _ = call(
+    store, hat, v_low, v_high, _ = call(
         forward_kernel,
-        [(STORE, NZ), (SLABS, 2, ROWS, NZ), plane, plane, (3, CELLS, NZ)],
+        [(STORE, NZ), (EXT, NX, NZ), plane, plane, (3, CELLS, NZ)],
         "forward",
         room=FORWARD_ROOM,
-        in_specs=[SM] + [VM] * 2 + [HB] * 4 + [VM] * 4 + [SM] + [VM] * 2,
+        in_specs=[SM] + [VM] * 2 + [HB] * 5 + [SM] + [VM] * 2,
         out_specs=[HB, VM, VM, VM, VM],
         scratch=[
             pltpu.VMEM((4, 4, NX, NZ), f32),
-            pltpu.VMEM((3 * FR * ROWS, NZ), f32),
             pltpu.VMEM((CELLS, NZ), f32),
             pltpu.VMEM((CELLS, NZ), f32),
-            pltpu.VMEM((EXT, NX, NZ), f32),
-            pltpu.SemaphoreType.DMA((4 + EXT,)),
+            pltpu.SemaphoreType.DMA((4,)),
             pltpu.SemaphoreType.DMA((4,)),
         ],
         flops=2**30,
         nbytes=10 * 2**20,
         input_output_aliases={1: 4},
-    )(fringe_start, fields, discs, low, high, prev, following, *quarters, profile, table, later)
+    )(fringe_start, fields, discs, low, high, prev, following, quarters[0], profile, table, later)
+    store, pay, v_low, v_high = call(
+        precursor_kernel,
+        [(STORE, NZ), (SLABS, 2, ROWS, NZ), plane, plane],
+        "precursor",
+        room=FORWARD_ROOM,
+        in_specs=[SM] + [VM] * 4 + [SM] + [VM] * 4 + [HB],
+        out_specs=[HB, VM, VM, VM],
+        scratch=[
+            pltpu.VMEM((3 * FR * ROWS, NZ), f32),
+            pltpu.VMEM((3, (WINDOW + 2) * ROWS, NZ), f32),
+            pltpu.VMEM((WINDOW * ROWS, NZ), f32),
+            pltpu.VMEM((WINDOW * ROWS, NZ), f32),
+            pltpu.VMEM((3, FR * ROWS, NZ), f32),
+            pltpu.VMEM((NX + ROWS, NZ), f32),
+            pltpu.VMEM((EXT, NX, NZ), f32),
+            pltpu.SemaphoreType.DMA((EXT + 3,)),
+            pltpu.SemaphoreType.DMA((3,)),
+        ],
+        flops=2**28,
+        nbytes=3 * 2**20,
+        input_output_aliases={10: 0},
+    )(fringe_start, *quarters, profile, hat, v_low, v_high, near_table, store)
     v_prev = lax.ppermute(v_high, "slab", upward)
     v_next = lax.ppermute(v_low, "slab", downward)
     pay = lax.all_to_all(pay, "slab", split_axis=0, concat_axis=0, tiled=True)

time: 84.8 us -> 82.6 us (0.974)
  waiting for transfers between devices: 16.6 us -> 12.3 us
  Pallas kernels: 19.9 us -> 22 us
    ppermute x3, waiting for transfers between devices: 4.98 us -> 0.68 us  [gather_y(): quarters.append(lax.ppermute(mine, 'sim', pairs))]
    pallas_call x1 -> x2, Pallas kernels: 5.08 us -> 7.18 us  [the longest x1 4.21 us: local(): call(forward_kernel, [(STORE, NZ), (EXT, NX, NZ), plane, plane, (3, CELLS...]
    unnamed x22 -> x24, local copies, waits for them, and re-layouts: 3.37 us -> 3.37 us
  transfers between devices with their start and end apart: 12 -> 12, of which waited for: 8 -> 6; matrix products, arithmetic and copies ran while one was open for 0% -> 0% of each run, Pallas kernels for 5% -> 10%
where the time goes in v4:
time: 82.6 us; the launch traced here: 82.2 us
  blocking collectives  22.3 us (27%)
  Pallas kernels  22 us (27%)
  starting transfers between devices  21.2 us (26%)
  waiting for transfers between devices  12.3 us (15%)
  local copies, waits for them, and re-layouts  3.37 us (4%)
  between operations  1 us (1%)
    all_to_all x1, blocking collectives, local(): pay = lax.all_to_all(pay, 'slab', split_axis=0, concat_axis=0, tiled=True)  22.3 us
    pallas_call x1, Pallas kernels, local(): call(final_kernel, [(3, CELLS, NZ)], 'final', room=FORWARD_ROOM, in_specs...  6.64 us
    ppermute x3, starting transfers between devices, scatter_y(): came = [lax.ppermute(piece[k], 'sim', [(0, k)]) for k in (1, 2, 3)]  6.22 us
    all_to_all x1, waiting for transfers between devices, local(): ret = lax.all_to_all(ret, 'slab', split_axis=0, concat_axis=0, tiled=True)  4.39 us
    pallas_call x1, Pallas kernels, local(): call(forward_kernel, [(STORE, NZ), (EXT, NX, NZ), plane, plane, (3, CELLS...  4.21 us
    pallas_call x1, Pallas kernels, local(): call(diffuse_kernel, [(3, CELLS, NZ), (2, NX, NZ)], 'diffuse', room=DIFFU...  3.94 us
    ppermute x3, starting transfers between devices, gather_y(): quarters.append(lax.ppermute(mine, 'sim', pairs))  3.84 us
    all_to_all x1, starting transfers between devices, local(): ret = lax.all_to_all(ret, 'slab', split_axis=0, concat_axis=0, tiled=True)  3.83 us
  transfers between devices with their start and end apart: 12, of which 6 were waited for; matrix products, arithmetic and copies ran while one was open for 0% of the time, Pallas kernels for 10%

profile of v4, /device:TPU:1, one launch (start us, length us, event | category | flops | bytes accessed | tf_op | source)
XLA Modules:
  0.0 82.2 jit_solution(14208926175027707464)
XLA Ops:
  0.0 0.0 copy-start
  0.8 3.4 %edges.1 = (f32[192,128]{1,0:T(8,128)}, f32[192,128]{1,0:T(8,128)}, f32[192,128]{1,0:T(8,128)}, f32[192,128]{1,0:T(8,128)}, f32[4,256,128]{2,1,0:T(8,128)}, /*index=5*/f32[4,256,128]{2,1,0:T(8,128)}) custom-call(s32[1]{0:T(128)S(6)} %copy.15.start_ref, f32[3,2048,128]{2,1,0:T(8,128)} %bitcast.4, f32[2048,128]{1,0:T(8,128)} %bitcast.6), custom_call_target="tpu_custom_call" | custom-call | bytes 6291456 | tf_op jit(solution)/shard_map/edges/pallas_call | solution.py:592
  4.2 3.3 %collective-permute-start.8 = (f32[4,256,128]{2,1,0:T(8,128)}, f32[4,256,128]{2,1,0:T(8,128)S(1)}, u32[]{:S(2)}, u32[]{:S(2)}) collective-permute-start(f32[4,256,128]{2,1,0:T(8,128)} %get-tuple-element.27.low_in), channel_id=1, source_target_pairs={{1,0},{2,1},{3,2},{4,3},{5,4},{6,5},{7,6},{8,7},{9,8},{10,9},{11,1... | collective-permute-start | bytes 1572872 | tf_op jit(solution)/shard_map/ppermute | solution.py:611
  7.5 0.0 collective-permute-start.7
  7.5 2.6 %collective-permute-start = (f32[192,128]{1,0:T(8,128)}, f32[192,128]{1,0:T(8,128)S(1)}, u32[]{:S(2)}, u32[]{:S(2)}) collective-permute-start(f32[192,128]{1,0:T(8,128)} %get-tuple-element.22), channel_id=1, source_target_pairs={{0,32},{1,33},{2,34},{3,35},{4,36},{5,37},{6,38},{7,39},{8,40},{9,... | collective-permute-start | bytes 294920 | tf_op jit(solution)/shard_map/ppermute | solution.py:559
  10.2 2.3 %collective-permute-start.1 = (f32[192,128]{1,0:T(8,128)}, f32[192,128]{1,0:T(8,128)S(1)}, u32[]{:S(2)}, u32[]{:S(2)}) collective-permute-start(f32[192,128]{1,0:T(8,128)} %get-tuple-element.23), channel_id=1, source_target_pairs={{0,64},{1,65},{2,66},{3,67},{4,68},{5,69},{6,70},{7,71},{8,72},{9,... | collective-permute-start | bytes 294920 | tf_op jit(solution)/shard_map/ppermute | solution.py:559
  12.4 1.3 %collective-permute-start.2 = (f32[192,128]{1,0:T(8,128)}, f32[192,128]{1,0:T(8,128)S(1)}, u32[]{:S(2)}, u32[]{:S(2)}) collective-permute-start(f32[192,128]{1,0:T(8,128)} %get-tuple-element.24), channel_id=1, source_target_pairs={{0,96},{1,97},{2,98},{3,99},{4,100},{5,101},{6,102},{7,103},{8,104... | collective-permute-start | bytes 294920 | tf_op jit(solution)/shard_map/ppermute | solution.py:559
  13.7 0.0 collective-permute-done.refs_1_
  13.8 0.6 collective-permute-done.1.refs_2_
  14.4 1.3 %collective-permute-done.2.refs_3_ = f32[192,128]{1,0:T(8,128)S(1)} collective-permute-done((f32[192,128]{1,0:T(8,128)}, f32[192,128]{1,0:T(8,128)S(1)}, u32[]{:S(2)}, u32[]{:S(2)}) %collective-permute-start.2) | collective-permute-done | bytes 98336 | tf_op jit(solution)/shard_map/ppermute | solution.py:559
  15.7 0.0 copy-start.10
  15.7 0.9 %copy-done.10 = f32[192,128]{1,0:T(8,128)S(1)} copy-done((f32[192,128]{1,0:T(8,128)S(1)}, f32[192,128]{1,0:T(8,128)}, u32[]{:S(2)}) %copy-start.10) | copy-done | bytes 98328
  16.6 0.0 copy-start.6
  16.6 2.3 %collective-permute-start.3 = (f32[192,128]{1,0:T(8,128)S(1)}, f32[192,128]{1,0:T(8,128)S(1)}, u32[]{:S(2)}, u32[]{:S(2)}) collective-permute-start(f32[192,128]{1,0:T(8,128)S(1)} %pick_y.1.refs_0_), channel_id=1, source_target_pairs={{0,128},{32,160},{64,192},{96,224},{1,129},{33,161},{65,193},{97,2... | collective-permute-start | bytes 294920 | tf_op jit(solution)/shard_map/ppermute | solution.py:614
  18.9 0.0 copy-done
  18.9 0.0 copy-start.1
  18.9 1.2 %copy-done.1 = f32[1,256,8,128]{3,2,1,0:T(8,128)S(1)} copy-done((f32[1,256,8,128]{3,2,1,0:T(8,128)S(1)}, f32[1,256,8,128]{3,2,1,0:T(8,128)}, u32[]{:S(2)}) %copy-start.1) | copy-done | bytes 1048600
  20.1 1.2 %copy-done.2 = s32[1,256,8,128]{3,2,1,0:T(8,128)S(1)} copy-done((s32[1,256,8,128]{3,2,1,0:T(8,128)S(1)}, s32[1,256,8,128]{3,2,1,0:T(8,128)}, u32[]{:S(2)}) %copy-start.2) | copy-done | bytes 1048600
  21.3 3.9 %diffuse.1 = (f32[3,2048,128]{2,1,0:T(8,128)S(1)}, f32[2,256,128]{2,1,0:T(8,128)S(1)}) custom-call(f32[3,2048,128]{2,1,0:T(8,128)S(1)} %bitcast.5, f32[2048,128]{1,0:T(8,128)S(1)} %bitcast.7, s32[2048,128]{1,0:T(8,128)S(1)} %bitcast.8, f32[192,128]{1,0:T(8,128)S(1)} %pick_y.1.refs_0_), custom_call_target="tpu_custom_call" | custom-call | flops 67108864 | bytes 8388608 | tf_op jit(solution)/shard_map/diffuse/pallas_call | solution.py:615
  25.3 0.0 collective-permute-done.3.refs_1_
  25.3 2.8 %collective-permute-start.6 = (f32[192,128]{1,0:T(8,128)S(1)}, f32[192,128]{1,0:T(8,128)S(1)}, u32[]{:S(2)}, u32[]{:S(2)}) collective-permute-start(f32[192,128]{1,0:T(8,128)S(1)} %pick_z.1.after.q0), channel_id=1, source_target_pairs={{0,96},{32,0},{64,32},{96,64},{128,224},{160,128},{192,160},{224,1... | collective-permute-start | bytes 294920 | tf_op jit(solution)/shard_map/ppermute | solution.py:567
  28.1 0.4 collective-permute-start.5
  28.5 0.7 collective-permute-start.4
  29.2 0.0 collective-permute-done.8.next_in
  29.2 0.0 collective-permute-done.7.prev_in
  29.2 0.0 copy-done.6
  29.2 0.0 copy-done.11
  29.2 0.0 copy-done.3
  29.2 0.0 copy-done.4
  29.2 0.0 copy-done.7
  29.2 0.0 copy-start.5
  29.2 4.2 %forward.1 = (f32[81920,128]{1,0:T(8,128)}, f32[10,256,128]{2,1,0:T(8,128)S(1)}, f32[256,128]{1,0:T(8,128)S(1)}, f32[256,128]{1,0:T(8,128)S(1)}, f32[3,2048,128]{2,1,0:T(8,128)S(1)}) custom-call(s32[1]{0:T(128)S(6)} %copy.15.start_ref, f32[3,2048,128]{2,1,0:T(8,128)S(1)} %get-tuple-element.26.field_ref, ...), custom_call_target="tpu_custom_call", output_to_operand_aliasing={{4}: (1, {})} | custom-call | flops 1073741824 | bytes 10485760 | tf_op jit(solution)/shard_map/forward/pallas_call | solution.py:625
  33.5 0.0 collective-permute-done.6.q3
  33.5 0.0 collective-permute-done.5.q2
  33.5 0.7 collective-permute-done.4.q1
  34.2 0.0 copy-done.5
  34.2 3.0 %precursor.1 = (f32[81920,128]{1,0:T(8,128)}, f32[32,2,8,128]{3,2,1,0:T(8,128)S(1)}, f32[256,128]{1,0:T(8,128)S(1)}, f32[256,128]{1,0:T(8,128)S(1)}) custom-call(s32[1]{0:T(128)S(6)} %copy.15.start_ref, f32[192,128]{1,0:T(8,128)S(1)} %pick_z.1.after.q0, f32[192,128]{1,0:T(8,128)S(1)} %collective-permute-done.4.q1, ...), custom_call_target="tpu_custom_call", output_to_operand_aliasing={{0}: (10, {})} | custom-call | flops 268435456 | bytes 3145728 | tf_op jit(solution)/shard_map/precursor/pallas_call | solution.py:643
  37.1 22.3 %all_to_all.10.pay_ref = f32[32,2,8,128]{3,2,1,0:T(8,128)S(1)} all-to-all(f32[32,2,8,128]{3,2,1,0:T(8,128)S(1)} %get-tuple-element.33), channel_id=1, replica_groups=mesh['sim'=8,'slab'=32] {'slab'}, dimensions={0} | all-to-all | bytes 524288 | tf_op jit(solution)/shard_map/all_to_all | solution.py:667
  59.5 0.0 copy-done.8
  59.5 0.0 copy-done.9
  59.5 0.8 %far.1 = f32[32,2,8,128]{3,2,1,0:T(8,128)} custom-call(f32[32,2,8,128]{3,2,1,0:T(8,128)S(1)} %all_to_all.10.pay_ref, f32[256,128]{1,0:T(8,128)S(1)} %copy-done.9, f32[256,128]{1,0:T(8,128)S(1)} %copy-done.8), custom_call_target="tpu_custom_call" | custom-call | bytes 524288 | tf_op jit(solution)/shard_map/far/pallas_call | solution.py:668
  60.3 3.8 %all-to-all-start.1 = ((f32[32,2,8,128]{3,2,1,0:T(8,128)}), f32[32,2,8,128]{3,2,1,0:T(8,128)S(1)}, u32[]{:S(2)}, u32[]{:S(2)}) async-start(f32[32,2,8,128]{3,2,1,0:T(8,128)} %far.1), calls=%async_computation.1 | async-start | bytes 524288 | tf_op jit(solution)/shard_map/all_to_all | solution.py:675
  64.1 1.7 %collective-permute-start.9 = (f32[256,128]{1,0:T(8,128)S(1)}, f32[256,128]{1,0:T(8,128)S(1)}, u32[]{:S(2)}, u32[]{:S(2)}) collective-permute-start(f32[256,128]{1,0:T(8,128)S(1)} %get-tuple-element.34), channel_id=1, source_target_pairs={{0,1},{1,2},{2,3},{3,4},{4,5},{5,6},{6,7},{7,8},{8,9},{9,10},{10,1... | collective-permute-start | bytes 393224 | tf_op jit(solution)/shard_map/ppermute | solution.py:665
  65.9 0.0 collective-permute-start.10
  65.9 3.0 %collective-permute-done.9.prev_ref = f32[256,128]{1,0:T(8,128)S(1)} collective-permute-done((f32[256,128]{1,0:T(8,128)S(1)}, f32[256,128]{1,0:T(8,128)S(1)}, u32[]{:S(2)}, u32[]{:S(2)}) %collective-permute-start.9) | collective-permute-done | bytes 131104 | tf_op jit(solution)/shard_map/ppermute | solution.py:665
  68.8 2.4 %collective-permute-done.10.next_ref = f32[256,128]{1,0:T(8,128)S(1)} collective-permute-done((f32[256,128]{1,0:T(8,128)S(1)}, f32[256,128]{1,0:T(8,128)S(1)}, u32[]{:S(2)}, u32[]{:S(2)}) %collective-permute-start.10) | collective-permute-done | bytes 131104 | tf_op jit(solution)/shard_map/ppermute | solution.py:666
  71.2 4.4 %all-to-all-done.1.ret_ref = f32[32,2,8,128]{3,2,1,0:T(8,128)S(1)} async-done(((f32[32,2,8,128]{3,2,1,0:T(8,128)}), f32[32,2,8,128]{3,2,1,0:T(8,128)S(1)}, u32[]{:S(2)}, u32[]{:S(2)}) %all-to-all-start.1) | async-done | bytes 262176 | tf_op jit(solution)/shard_map/all_to_all | solution.py:675
  75.6 6.6 %final.1 = f32[3,2048,128]{2,1,0:T(8,128)} custom-call(f32[32,2,8,128]{3,2,1,0:T(8,128)S(1)} %all-to-all-done.1.ret_ref, f32[256,128]{1,0:T(8,128)S(1)} %collective-permute-done.9.prev_ref, f32[256,128]{1,0:T(8,128)S(1)} %collective-permute-done.10.next_ref, f32[81920,128]{1,0:T(8,128)} %get-tuple-element.36.store), custom_call_target="tpu_custom_call" | custom-call | flops 1073741824 | bytes 10485760 | tf_op jit(solution)/shard_map/final/pallas_call | solution.py:676
  (9 shorter events, 0.1 us)
Async XLA Ops:
  0.0 18.9 %copy-start = (f32[1,3,256,8,128]{4,3,2,1,0:T(8,128)S(1)}, f32[1,3,256,8,128]{4,3,2,1,0:T(8,128)}, u32[]{:S(2)}) copy-start(f32[1,3,256,8,128]{4,3,2,1,0:T(8,128)} %param.10) | copy-start | bytes 9437188
  4.2 25.0 %collective-permute-start.8 = (f32[4,256,128]{2,1,0:T(8,128)}, f32[4,256,128]{2,1,0:T(8,128)S(1)}, u32[]{:S(2)}, u32[]{:S(2)}) collective-permute-start(f32[4,256,128]{2,1,0:T(8,128)} %get-tuple-element.27.low_in), channel_id=1, source_target_pairs={{1,0},{2,1},{3,2},{4,3},{5,4},{6,5},{7,6},{8,7},{9,8},{10,9},{11,1... | collective-permute-start | bytes 1572872 | tf_op jit(solution)/shard_map/ppermute | solution.py:611
  7.5 21.7 %collective-permute-start.7 = (f32[4,256,128]{2,1,0:T(8,128)}, f32[4,256,128]{2,1,0:T(8,128)S(1)}, u32[]{:S(2)}, u32[]{:S(2)}) collective-permute-start(f32[4,256,128]{2,1,0:T(8,128)} %get-tuple-element.28.high_in), channel_id=1, source_target_pairs={{0,1},{1,2},{2,3},{3,4},{4,5},{5,6},{6,7},{7,8},{8,9},{9,10},{10,1... | collective-permute-start | bytes 1572872 | tf_op jit(solution)/shard_map/ppermute | solution.py:610
  7.5 6.2 %collective-permute-start = (f32[192,128]{1,0:T(8,128)}, f32[192,128]{1,0:T(8,128)S(1)}, u32[]{:S(2)}, u32[]{:S(2)}) collective-permute-start(f32[192,128]{1,0:T(8,128)} %get-tuple-element.22), channel_id=1, source_target_pairs={{0,32},{1,33},{2,34},{3,35},{4,36},{5,37},{6,38},{7,39},{8,40},{9,... | collective-permute-start | bytes 294920 | tf_op jit(solution)/shard_map/ppermute | solution.py:559
  10.2 4.2 %collective-permute-start.1 = (f32[192,128]{1,0:T(8,128)}, f32[192,128]{1,0:T(8,128)S(1)}, u32[]{:S(2)}, u32[]{:S(2)}) collective-permute-start(f32[192,128]{1,0:T(8,128)} %get-tuple-element.23), channel_id=1, source_target_pairs={{0,64},{1,65},{2,66},{3,67},{4,68},{5,69},{6,70},{7,71},{8,72},{9,... | collective-permute-start | bytes 294920 | tf_op jit(solution)/shard_map/ppermute | solution.py:559
  12.4 3.2 %collective-permute-start.2 = (f32[192,128]{1,0:T(8,128)}, f32[192,128]{1,0:T(8,128)S(1)}, u32[]{:S(2)}, u32[]{:S(2)}) collective-permute-start(f32[192,128]{1,0:T(8,128)} %get-tuple-element.24), channel_id=1, source_target_pairs={{0,96},{1,97},{2,98},{3,99},{4,100},{5,101},{6,102},{7,103},{8,104... | collective-permute-start | bytes 294920 | tf_op jit(solution)/shard_map/ppermute | solution.py:559
  15.7 0.9 %copy-start.10 = (f32[192,128]{1,0:T(8,128)S(1)}, f32[192,128]{1,0:T(8,128)}, u32[]{:S(2)}) copy-start(f32[192,128]{1,0:T(8,128)} %get-tuple-element.21.refs_0_) | copy-start | bytes 294916
  16.6 12.6 %copy-start.6 = (f32[896,128]{1,0:T(8,128)S(1)}, f32[896,128]{1,0:T(8,128)}, u32[]{:S(2)}) copy-start(f32[896,128]{1,0:T(8,128)} %constant.14.clone.later_ref) | copy-start | bytes 1376260
  16.6 12.6 %copy-start.11 = (f32[32]{0:T(128)S(1)}, f32[32]{0:T(128)}, u32[]{:S(2)}) copy-start(f32[32]{0:T(128)} %constant.12.clone.profile_ref) | copy-start | bytes 388
  16.6 8.7 %collective-permute-start.3 = (f32[192,128]{1,0:T(8,128)S(1)}, f32[192,128]{1,0:T(8,128)S(1)}, u32[]{:S(2)}, u32[]{:S(2)}) collective-permute-start(f32[192,128]{1,0:T(8,128)S(1)} %pick_y.1.refs_0_), channel_id=1, source_target_pairs={{0,128},{32,160},{64,192},{96,224},{1,129},{33,161},{65,193},{97,2... | collective-permute-start | bytes 294920 | tf_op jit(solution)/shard_map/ppermute | solution.py:614
  18.9 1.2 %copy-start.1 = (f32[1,256,8,128]{3,2,1,0:T(8,128)S(1)}, f32[1,256,8,128]{3,2,1,0:T(8,128)}, u32[]{:S(2)}) copy-start(f32[1,256,8,128]{3,2,1,0:T(8,128)} %param.11) | copy-start | bytes 3145732
  20.1 1.2 %copy-start.2 = (s32[1,256,8,128]{3,2,1,0:T(8,128)S(1)}, s32[1,256,8,128]{3,2,1,0:T(8,128)}, u32[]{:S(2)}) copy-start(s32[1,256,8,128]{3,2,1,0:T(8,128)} %param.12) | copy-start | bytes 3145732
  21.3 7.9 %copy-start.3 = (f32[4,256,128]{2,1,0:T(8,128)S(1)}, f32[4,256,128]{2,1,0:T(8,128)}, u32[]{:S(2)}) copy-start(f32[4,256,128]{2,1,0:T(8,128)} %get-tuple-element.27.low_in) | copy-start | bytes 1572868
  21.3 7.9 %copy-start.4 = (f32[4,256,128]{2,1,0:T(8,128)S(1)}, f32[4,256,128]{2,1,0:T(8,128)}, u32[]{:S(2)}) copy-start(f32[4,256,128]{2,1,0:T(8,128)} %get-tuple-element.28.high_in) | copy-start | bytes 1572868
  21.3 7.9 %copy-start.7 = (f32[896,128]{1,0:T(8,128)S(1)}, f32[896,128]{1,0:T(8,128)}, u32[]{:S(2)}) copy-start(f32[896,128]{1,0:T(8,128)} %constant.13.clone.table_ref) | copy-start | bytes 1376260
  25.3 8.1 %collective-permute-start.6 = (f32[192,128]{1,0:T(8,128)S(1)}, f32[192,128]{1,0:T(8,128)S(1)}, u32[]{:S(2)}, u32[]{:S(2)}) collective-permute-start(f32[192,128]{1,0:T(8,128)S(1)} %pick_z.1.after.q0), channel_id=1, source_target_pairs={{0,96},{32,0},{64,32},{96,64},{128,224},{160,128},{192,160},{224,1... | collective-permute-start | bytes 294920 | tf_op jit(solution)/shard_map/ppermute | solution.py:567
  28.1 5.3 %collective-permute-start.5 = (f32[192,128]{1,0:T(8,128)S(1)}, f32[192,128]{1,0:T(8,128)S(1)}, u32[]{:S(2)}, u32[]{:S(2)}) collective-permute-start(f32[192,128]{1,0:T(8,128)S(1)} %pick_z.1.after.q0), channel_id=1, source_target_pairs={{0,64},{32,96},{64,0},{96,32},{128,192},{160,224},{192,128},{224,1... | collective-permute-start | bytes 294920 | tf_op jit(solution)/shard_map/ppermute | solution.py:567
  28.5 5.7 %collective-permute-start.4 = (f32[192,128]{1,0:T(8,128)S(1)}, f32[192,128]{1,0:T(8,128)S(1)}, u32[]{:S(2)}, u32[]{:S(2)}) collective-permute-start(f32[192,128]{1,0:T(8,128)S(1)} %pick_z.1.after.q0), channel_id=1, source_target_pairs={{0,32},{32,64},{64,96},{96,0},{128,160},{160,192},{192,224},{224,1... | collective-permute-start | bytes 294920 | tf_op jit(solution)/shard_map/ppermute | solution.py:567
  29.2 4.9 %copy-start.5 = (f32[928,128]{1,0:T(8,128)S(1)}, f32[928,128]{1,0:T(8,128)}, u32[]{:S(2)}) copy-start(f32[928,128]{1,0:T(8,128)} %constant.15.clone.table_ref) | copy-start | bytes 1425412
  34.2 25.3 %copy-start.8 = (f32[256,128]{1,0:T(8,128)S(1)}, f32[256,128]{1,0:T(8,128)}, u32[]{:S(2)}) copy-start(f32[256,128]{1,0:T(8,128)} %constant.17.clone.wrap_ref) | copy-start | bytes 393220
  34.2 25.3 %copy-start.9 = (f32[256,128]{1,0:T(8,128)S(1)}, f32[256,128]{1,0:T(8,128)}, u32[]{:S(2)}) copy-start(f32[256,128]{1,0:T(8,128)} %constant.16.clone.step_ref) | copy-start | bytes 393220
  60.3 15.3 %all-to-all-start.1 = ((f32[32,2,8,128]{3,2,1,0:T(8,128)}), f32[32,2,8,128]{3,2,1,0:T(8,128)S(1)}, u32[]{:S(2)}, u32[]{:S(2)}) async-start(f32[32,2,8,128]{3,2,1,0:T(8,128)} %far.1), calls=%async_computation.1 | async-start | bytes 524288 | tf_op jit(solution)/shard_map/all_to_all | solution.py:675
  64.1 4.7 %collective-permute-start.9 = (f32[256,128]{1,0:T(8,128)S(1)}, f32[256,128]{1,0:T(8,128)S(1)}, u32[]{:S(2)}, u32[]{:S(2)}) collective-permute-start(f32[256,128]{1,0:T(8,128)S(1)} %get-tuple-element.34), channel_id=1, source_target_pairs={{0,1},{1,2},{2,3},{3,4},{4,5},{5,6},{6,7},{7,8},{8,9},{9,10},{10,1... | collective-permute-start | bytes 393224 | tf_op jit(solution)/shard_map/ppermute | solution.py:665
  65.9 5.3 %collective-permute-start.10 = (f32[256,128]{1,0:T(8,128)S(1)}, f32[256,128]{1,0:T(8,128)S(1)}, u32[]{:S(2)}, u32[]{:S(2)}) collective-permute-start(f32[256,128]{1,0:T(8,128)S(1)} %get-tuple-element.35), channel_id=1, source_target_pairs={{1,0},{2,1},{3,2},{4,3},{5,4},{6,5},{7,6},{8,7},{9,8},{10,9},{11,1... | collective-permute-start | bytes 393224 | tf_op jit(solution)/shard_map/ppermute | solution.py:666

commit v5 on v4

--- a/solution.py
+++ b/solution.py
@@ -63,6 +63,15 @@
     high = value.astype(jnp.bfloat16)
     low = (value - high.astype(jnp.float32)).astype(jnp.bfloat16)
     return high, low
+
+
+def twice(matrix):
+    zero = jnp.zeros_like(matrix)
+    return jnp.concatenate([jnp.concatenate([matrix, zero], 1), jnp.concatenate([zero, matrix], 1)], 0)
+
+
+def halves(value):
+    return value[:, :NZ], value[:, NZ:]
 
 
 def call(body, outs, name, scratch=(), in_specs=None, out_specs=None, room=20, flops=0, nbytes=0, **kw):
@@ -153,11 +162,11 @@
     return pl.ds(pl.multiple_of(x * ROWS, ROWS), ROWS)
 
 
-def diffuse_kernel(vel_ref, visc_ref, turb_ref, *refs):
-    *_, out_ref, disc_ref = refs
+def diffuse_kernel(vel_ref, visc_ref, after, out_ref, done_ref):
+    del after
+    done_ref[...] = jnp.zeros_like(done_ref)
     row, lane = iotas()
     last_row, last_lane = row == ROWS - 1, lane == NZ - 1
-    inner = jnp.where((row == 0) | last_row, 0.0, DRAG).astype(jnp.float32)
 
     def fields_at(x):
         return [vel_ref[c, tile(x), :] for c in range(3)], visc_ref[tile(x), :]
@@ -177,9 +186,6 @@
             flux_z = sum_z * (pltpu.roll(u, NZ - 1, 1) - u)
             down_y, down_z = pltpu.roll(flux_y, 1, 0), pltpu.roll(flux_z, 1, 1)
             new = u + (flux_x - back[c]) + (flux_y - down_y) + (flux_z - down_z)
-            if c == 0:
-                disc = turb_ref[tile(x), :].astype(jnp.float32)
-                new = new - inner * disc * new * jnp.abs(new)
             out_ref[c, tile(x), :] = new
             fluxes.append(flux_x)
         return ahead, nu_ahead, fluxes
@@ -189,8 +195,6 @@
     sum_x = 0.5 * nu_before + 0.5 * nu
     back = [sum_x * (now[c] - before[c]) for c in range(3)]
     lax.fori_loop(0, NX, step, (now, nu, back), unroll=16)
-    for side, at in enumerate((0, ROWS - 1)):
-        disc_ref[side] = turb_ref[every8(at), :].astype(jnp.float32)
 
 
 def centred_z(value, first_lane, last_lane):
@@ -229,7 +233,7 @@
 
 
 def forward_kernel(
-    start_ref, field_ref, disc_ref, low_in, high_in, prev_in, next_in, after, profile_ref, table_ref, later_ref,
+    start_ref, field_ref, turb_ref, low_in, high_in, prev_in, next_in, after, profile_ref, table_ref, later_ref,
     store, hat_ref, low_ref, high_ref, out_ref, rims, div, modes, sems, rim_sems,
 ):
     del field_ref, after
@@ -243,11 +247,15 @@
         own, other = 2 * side, 2 * side + 1
         faces = 0.5 * (rims[own, 3] + rims[other, 3])
         for c in range(3):
-            plane = out_ref[c, at, :] + faces * (rims[other, c] - rims[own, c])
-            if c == 0:
-                plane = plane - DRAG * disc_ref[side] * plane * jnp.abs(plane)
-            out_ref[c, at, :] = plane
+            out_ref[c, at, :] = out_ref[c, at, :] + faces * (rims[other, c] - rims[own, c])
     start = start_ref[0]
+
+    def drag(x, _):
+        u = out_ref[0, tile(x), :]
+        out_ref[0, tile(x), :] = u - DRAG * turb_ref[tile(x), :].astype(jnp.float32) * u * jnp.abs(u)
+        return 0
+
+    lax.fori_loop(0, NX, drag, 0, unroll=16)
 
     def blend(i, _):
         kept = 1.0 - profile_ref[i] * active
@@ -268,16 +276,16 @@
         NX,
         (out_ref[0, tile(NX - 1), :], out_ref[0, tile(0), :]),
     )
-    z_high, z_low = parts(table_ref[pl.ds(TAB_Z, NZ), :])
-    for block in range(8):
-        rows = pl.ds(block * NX, NX)
-        modes[rows, :] = dot3(*parts(div[rows, :]), z_high, z_low)
+    z_high, z_low = parts(twice(table_ref[pl.ds(TAB_Z, NZ), :]))
+    for block in range(0, ROWS, 2):
+        first, second = pl.ds(block * NX, NX), pl.ds((block + 1) * NX, NX)
+        pair = jnp.concatenate([div[first, :], div[second, :]], 1)
+        modes[first, :], modes[second, :] = halves(dot3(*parts(pair), z_high, z_low))
     low = out_ref[1, every8(0), :]
     high = out_ref[1, every8(ROWS - 1), :]
     low_ref[...] = low
     high_ref[...] = high
-    low = dot3(*parts(0.5 * low), z_high, z_low)
-    high = dot3(*parts(-0.5 * high), z_high, z_low)
+    low, high = halves(dot3(*parts(jnp.concatenate([0.5 * low, -0.5 * high], 1)), z_high, z_low))
     x_high, x_low = parts(x_matrix(table_ref))
     for r in range(0, EXT, 2):
         pair = []
@@ -337,11 +345,13 @@
         WINDOW,
         (share[0, tile(0), :], share[0, tile(1), :]),
     )
-    z_high, z_low = parts(table_ref[pl.ds(NX, NZ), :])
-    modes[...] = dot3(*parts(div[...]), z_high, z_low)
+    z_high, z_low = parts(twice(table_ref[pl.ds(NX, NZ), :]))
+    half = WINDOW * ROWS // 2
+    first, second = pl.ds(0, half), pl.ds(half, half)
+    pair = jnp.concatenate([div[first, :], div[second, :]], 1)
+    modes[first, :], modes[second, :] = halves(dot3(*parts(pair), z_high, z_low))
     ends = [share[1, every8(ROWS + y, WINDOW), :] for y in (0, ROWS - 1)]
-    low = dot3(*parts(0.5 * ends[0]), z_high, z_low)
-    high = dot3(*parts(-0.5 * ends[1]), z_high, z_low)
+    low, high = halves(dot3(*parts(jnp.concatenate([0.5 * ends[0], -0.5 * ends[1]], 1)), z_high, z_low))
     at = pl.multiple_of(base + 8, ROWS)
     basis = parts(
         jnp.concatenate(
@@ -439,7 +449,8 @@
         left = step * left + pay_ref[t, 1]
 
 
-OUT_CHUNKS = 4
+OUT_CHUNKS = 8
+HAT_CHUNKS = 4
 
 
 def green0(j):
@@ -450,12 +461,16 @@
     ret_ref, prev_ref, next_ref, store,
     out_hbm, press, field, rim, out_ref, field_ref, hat_ref, table_ref, sems, out_sems,
 ):
-    hats = [(store.at[pl.ds(STORE_HAT + r * NX, NX)], hat_ref.at[r]) for r in range(EXT)]
+    part = NX // HAT_CHUNKS
+    hats = []
+    for k in range(HAT_CHUNKS):
+        hats += [(store.at[pl.ds(STORE_HAT + r * NX + k * part, part)], hat_ref.at[r, pl.ds(k * part, part)]) for r in range(EXT)]
     lines = (pl.ds(0, NX), pl.ds(NX, LATER - NX))
     later = [(store.at[pl.ds(STORE_LATER + s.start, s.size)], table_ref.at[s]) for s in lines]
     fields = [(store.at[pl.ds(c * CELLS, CELLS)], field_ref.at[c]) for c in range(3)]
     copies = start_all([later[0], *hats, later[1], *fields], sems)
     wait_all(copies[: 1 + EXT])
+    copies = copies[1 + EXT :]
     row, lane = iotas()
     first_row, last_row = row == 0, row == ROWS - 1
     first_lane, last_lane = lane == 0, lane == NZ - 1
@@ -482,7 +497,12 @@
             press[r, at, :] = values[r]
         return 0
 
-    lax.fori_loop(1, NX // ROWS, line, 0, unroll=4)
+    count = part // ROWS
+    for k in range(HAT_CHUNKS):
+        if k:
+            wait_all(copies[:EXT])
+            copies = copies[EXT:]
+        lax.fori_loop(k * count, (k + 1) * count, line, 0, unroll=4)
     at = pl.ds(0, ROWS)
     values, rows = solve(0, at)
     slope, curve = ret_ref[0, 0], ret_ref[0, 1]
@@ -494,15 +514,13 @@
                 mean_line = mean_line + green0(float(abs(r - k))) * rows[k]
         press[r, at, :] = jnp.where(origin, mean_line, values[r])
 
-    copies[1 + EXT].wait()
+    copies[0].wait()
     x_high, x_low = parts(x_matrix(table_ref))
-    z_high, z_low = parts(table_ref[pl.ds(TAB_Z, NZ), :])
+    z_high, z_low = parts(twice(table_ref[pl.ds(TAB_Z, NZ), :]))
     for r in range(0, EXT, 2):
         pair = jnp.concatenate([press[r], press[r + 1]], 1)
-        both = dot3(x_high, x_low, *parts(pair))
-        for k in (r, r + 1):
-            plane = both[:, :NZ] if k == r else both[:, NZ:]
-            plane = dot3(*parts(plane), z_high, z_low)
+        both = dot3(*parts(dot3(x_high, x_low, *parts(pair))), z_high, z_low)
+        for k, plane in zip((r, r + 1), halves(both)):
             if k == 0:
                 rim[every8(0), :] = plane - 0.5 * prev_ref[...]
             elif k == EXT - 1:
@@ -522,7 +540,7 @@
         return now, ahead
 
     carry = (field[tile(NX - 1), :], field[tile(0), :])
-    wait_all(copies[2 + EXT :])
+    wait_all(copies[1:])
     copies = []
     part = CELLS // OUT_CHUNKS
     count = NX // OUT_CHUNKS
@@ -612,16 +630,16 @@
 
     mine = scatter_y(pieces)
     came = lax.ppermute(mine, "sim", [(i, i + 4) for i in range(4)])
-    fields, discs = call(
+    fields, done = call(
         diffuse_kernel,
-        [(3, CELLS, NZ), (2, NX, NZ)],
+        [(3, CELLS, NZ), (ROWS, NZ)],
         "diffuse",
         room=DIFFUSE_ROOM,
-        in_specs=[VM] * 3 + [HB],
+        in_specs=[VM] * 2 + [HB],
         flops=2**26,
         nbytes=8 * 2**20,
-    )(vel, visc, turb, mine)
-    quarters = gather_y(pick("pick_z", lambda me: me // 4, [mine, came], discs))
+    )(vel, visc, mine)
+    quarters = gather_y(pick("pick_z", lambda me: me // 4, [mine, came], done))
     store, hat, v_low, v_high, _ = call(
         forward_kernel,
         [(STORE, NZ), (EXT, NX, NZ), plane, plane, (3, CELLS, NZ)],
@@ -639,7 +657,7 @@
         flops=2**30,
         nbytes=10 * 2**20,
         input_output_aliases={1: 4},
-    )(fringe_start, fields, discs, low, high, prev, following, quarters[0], profile, table, later)
+    )(fringe_start, fields, turb, low, high, prev, following, quarters[0], profile, table, later)
     store, pay, v_low, v_high = call(
         precursor_kernel,
         [(STORE, NZ), (SLABS, 2, ROWS, NZ), plane, plane],
@@ -688,7 +706,7 @@
             pltpu.VMEM((3, CELLS, NZ), f32),
             pltpu.VMEM((EXT, NX, NZ), f32),
             pltpu.VMEM((LATER, NZ), f32),
-            pltpu.SemaphoreType.DMA((5 + EXT,)),
+            pltpu.SemaphoreType.DMA((5 + HAT_CHUNKS * EXT,)),
             pltpu.SemaphoreType.DMA((OUT_CHUNKS,)),
         ],
         flops=2**30,

time: 82.6 us -> 81 us (0.981)
  local copies, waits for them, and re-layouts: 3.37 us -> 2.16 us
    unnamed x24, local copies, waits for them, and re-layouts: 3.37 us -> 2.16 us
  transfers between devices with their start and end apart: 12 -> 12, of which waited for: 6 -> 6; matrix products, arithmetic and copies ran while one was open for 0% -> 0% of each run, Pallas kernels for 10% -> 11%
where the time goes in v5:
time: 81 us; the launch traced here: 80.5 us
  blocking collectives  22.3 us (28%)
  Pallas kernels  22 us (27%)
  starting transfers between devices  21.1 us (26%)
  waiting for transfers between devices  11.8 us (15%)
  local copies, waits for them, and re-layouts  2.16 us (3%)
  between operations  1.17 us (1%)
    all_to_all x1, blocking collectives, local(): pay = lax.all_to_all(pay, 'slab', split_axis=0, concat_axis=0, tiled=True)  22.3 us
    ppermute x3, starting transfers between devices, scatter_y(): came = [lax.ppermute(piece[k], 'sim', [(0, k)]) for k in (1, 2, 3)]  6.22 us
    pallas_call x1, Pallas kernels, local(): call(final_kernel, [(3, CELLS, NZ)], 'final', room=FORWARD_ROOM, in_specs...  6.11 us
    pallas_call x1, Pallas kernels, local(): call(forward_kernel, [(STORE, NZ), (EXT, NX, NZ), plane, plane, (3, CELLS...  4.7 us
    all_to_all x1, waiting for transfers between devices, local(): ret = lax.all_to_all(ret, 'slab', split_axis=0, concat_axis=0, tiled=True)  4.39 us
    pallas_call x1, Pallas kernels, local(): call(diffuse_kernel, [(3, CELLS, NZ), (ROWS, NZ)], 'diffuse', room=DIFFUS...  3.92 us
    ppermute x3, starting transfers between devices, gather_y(): quarters.append(lax.ppermute(mine, 'sim', pairs))  3.85 us
    all_to_all x1, starting transfers between devices, local(): ret = lax.all_to_all(ret, 'slab', split_axis=0, concat_axis=0, tiled=True)  3.83 us
  transfers between devices with their start and end apart: 12, of which 6 were waited for; matrix products, arithmetic and copies ran while one was open for 0% of the time, Pallas kernels for 11%

profile of v5, /device:TPU:1, one launch (start us, length us, event | category | flops | bytes accessed | tf_op | source)
XLA Modules:
  0.0 80.5 jit_solution(5703674387083013859)
XLA Ops:
  0.8 0.0 copy-start.7
  0.8 0.0 copy-start.11
  0.8 3.4 %edges.1 = (f32[192,128]{1,0:T(8,128)}, f32[192,128]{1,0:T(8,128)}, f32[192,128]{1,0:T(8,128)}, f32[192,128]{1,0:T(8,128)}, f32[4,256,128]{2,1,0:T(8,128)}, /*index=5*/f32[4,256,128]{2,1,0:T(8,128)}) custom-call(s32[1]{0:T(128)S(6)} %copy.15.start_ref, f32[3,2048,128]{2,1,0:T(8,128)} %bitcast.4, f32[2048,128]{1,0:T(8,128)} %bitcast.6), custom_call_target="tpu_custom_call" | custom-call | bytes 6291456 | tf_op jit(solution)/shard_map/edges/pallas_call | solution.py:610
  4.2 0.0 copy-start.6
  4.2 3.3 %collective-permute-start.8 = (f32[4,256,128]{2,1,0:T(8,128)}, f32[4,256,128]{2,1,0:T(8,128)S(1)}, u32[]{:S(2)}, u32[]{:S(2)}) collective-permute-start(f32[4,256,128]{2,1,0:T(8,128)} %get-tuple-element.27.low_in), channel_id=1, source_target_pairs={{1,0},{2,1},{3,2},{4,3},{5,4},{6,5},{7,6},{8,7},{9,8},{10,9},{11,1... | collective-permute-start | bytes 1572872 | tf_op jit(solution)/shard_map/ppermute | solution.py:629
  7.6 0.0 collective-permute-start.7
  7.6 2.6 %collective-permute-start = (f32[192,128]{1,0:T(8,128)}, f32[192,128]{1,0:T(8,128)S(1)}, u32[]{:S(2)}, u32[]{:S(2)}) collective-permute-start(f32[192,128]{1,0:T(8,128)} %get-tuple-element.22), channel_id=1, source_target_pairs={{0,32},{1,33},{2,34},{3,35},{4,36},{5,37},{6,38},{7,39},{8,40},{9,... | collective-permute-start | bytes 294920 | tf_op jit(solution)/shard_map/ppermute | solution.py:577
  10.2 2.3 %collective-permute-start.1 = (f32[192,128]{1,0:T(8,128)}, f32[192,128]{1,0:T(8,128)S(1)}, u32[]{:S(2)}, u32[]{:S(2)}) collective-permute-start(f32[192,128]{1,0:T(8,128)} %get-tuple-element.23), channel_id=1, source_target_pairs={{0,64},{1,65},{2,66},{3,67},{4,68},{5,69},{6,70},{7,71},{8,72},{9,... | collective-permute-start | bytes 294920 | tf_op jit(solution)/shard_map/ppermute | solution.py:577
  12.5 1.3 %collective-permute-start.2 = (f32[192,128]{1,0:T(8,128)}, f32[192,128]{1,0:T(8,128)S(1)}, u32[]{:S(2)}, u32[]{:S(2)}) collective-permute-start(f32[192,128]{1,0:T(8,128)} %get-tuple-element.24), channel_id=1, source_target_pairs={{0,96},{1,97},{2,98},{3,99},{4,100},{5,101},{6,102},{7,103},{8,104... | collective-permute-start | bytes 294920 | tf_op jit(solution)/shard_map/ppermute | solution.py:577
  13.8 0.0 collective-permute-done.refs_1_
  13.8 0.6 collective-permute-done.1.refs_2_
  14.4 1.3 %collective-permute-done.2.refs_3_ = f32[192,128]{1,0:T(8,128)S(1)} collective-permute-done((f32[192,128]{1,0:T(8,128)}, f32[192,128]{1,0:T(8,128)S(1)}, u32[]{:S(2)}, u32[]{:S(2)}) %collective-permute-start.2) | collective-permute-done | bytes 98336 | tf_op jit(solution)/shard_map/ppermute | solution.py:577
  15.7 0.9 %copy-done.10 = f32[192,128]{1,0:T(8,128)S(1)} copy-done((f32[192,128]{1,0:T(8,128)S(1)}, f32[192,128]{1,0:T(8,128)}, u32[]{:S(2)}) %copy-start.10) | copy-done | bytes 98328
  16.6 2.1 %collective-permute-start.3 = (f32[192,128]{1,0:T(8,128)S(1)}, f32[192,128]{1,0:T(8,128)S(1)}, u32[]{:S(2)}, u32[]{:S(2)}) collective-permute-start(f32[192,128]{1,0:T(8,128)S(1)} %pick_y.1.after.refs_0_), channel_id=1, source_target_pairs={{0,128},{32,160},{64,192},{96,224},{1,129},{33,161},{65,193},{97,2... | collective-permute-start | bytes 294920 | tf_op jit(solution)/shard_map/ppermute | solution.py:632
  18.8 0.0 copy-done
  18.8 0.0 copy-start.1
  18.8 1.2 %copy-done.1 = f32[1,256,8,128]{3,2,1,0:T(8,128)S(1)} copy-done((f32[1,256,8,128]{3,2,1,0:T(8,128)S(1)}, f32[1,256,8,128]{3,2,1,0:T(8,128)}, u32[]{:S(2)}) %copy-start.1) | copy-done | bytes 1048600
  20.0 3.9 %diffuse.1 = (f32[3,2048,128]{2,1,0:T(8,128)S(1)}, f32[8,128]{1,0:T(8,128)S(1)}) custom-call(f32[3,2048,128]{2,1,0:T(8,128)S(1)} %bitcast.5, f32[2048,128]{1,0:T(8,128)S(1)} %bitcast.7, f32[192,128]{1,0:T(8,128)S(1)} %pick_y.1.after.refs_0_), custom_call_target="tpu_custom_call" | custom-call | flops 67108864 | bytes 8388608 | tf_op jit(solution)/shard_map/diffuse/pallas_call | solution.py:633
  23.9 0.0 collective-permute-done.3.refs_1_
  24.0 2.8 %collective-permute-start.6 = (f32[192,128]{1,0:T(8,128)S(1)}, f32[192,128]{1,0:T(8,128)S(1)}, u32[]{:S(2)}, u32[]{:S(2)}) collective-permute-start(f32[192,128]{1,0:T(8,128)S(1)} %pick_z.1.after.q0), channel_id=1, source_target_pairs={{0,96},{32,0},{64,32},{96,64},{128,224},{160,128},{192,160},{224,1... | collective-permute-start | bytes 294920 | tf_op jit(solution)/shard_map/ppermute | solution.py:585
  26.8 0.4 collective-permute-start.5
  27.1 0.7 collective-permute-start.4
  27.8 0.0 collective-permute-done.8.next_in
  27.8 0.0 collective-permute-done.7.prev_in
  27.8 0.0 copy-done.7
  27.8 0.0 copy-done.11
  27.9 0.0 copy-done.6
  27.9 0.0 copy-done.2
  27.9 0.0 copy-done.3
  27.9 0.0 copy-done.4
  27.9 0.0 copy-start.5
  27.9 4.7 %forward.1 = (f32[81920,128]{1,0:T(8,128)}, f32[10,256,128]{2,1,0:T(8,128)S(1)}, f32[256,128]{1,0:T(8,128)S(1)}, f32[256,128]{1,0:T(8,128)S(1)}, f32[3,2048,128]{2,1,0:T(8,128)S(1)}) custom-call(s32[1]{0:T(128)S(6)} %copy.15.start_ref, f32[3,2048,128]{2,1,0:T(8,128)S(1)} %get-tuple-element.26.field_ref, ...), custom_call_target="tpu_custom_call", output_to_operand_aliasing={{4}: (1, {})} | custom-call | flops 1073741824 | bytes 10485760 | tf_op jit(solution)/shard_map/forward/pallas_call | solution.py:643
  32.6 0.0 collective-permute-done.6.q3
  32.6 0.0 collective-permute-done.5.q2
  32.6 0.2 collective-permute-done.4.q1
  32.8 0.0 copy-done.5
  32.8 3.0 %precursor.1 = (f32[81920,128]{1,0:T(8,128)}, f32[32,2,8,128]{3,2,1,0:T(8,128)S(1)}, f32[256,128]{1,0:T(8,128)S(1)}, f32[256,128]{1,0:T(8,128)S(1)}) custom-call(s32[1]{0:T(128)S(6)} %copy.15.start_ref, f32[192,128]{1,0:T(8,128)S(1)} %pick_z.1.after.q0, f32[192,128]{1,0:T(8,128)S(1)} %collective-permute-done.4.q1, ...), custom_call_target="tpu_custom_call", output_to_operand_aliasing={{0}: (10, {})} | custom-call | flops 268435456 | bytes 3145728 | tf_op jit(solution)/shard_map/precursor/pallas_call | solution.py:661
  35.8 22.3 %all_to_all.10.pay_ref = f32[32,2,8,128]{3,2,1,0:T(8,128)S(1)} all-to-all(f32[32,2,8,128]{3,2,1,0:T(8,128)S(1)} %get-tuple-element.33), channel_id=1, replica_groups=mesh['sim'=8,'slab'=32] {'slab'}, dimensions={0} | all-to-all | bytes 524288 | tf_op jit(solution)/shard_map/all_to_all | solution.py:685
  58.2 0.0 copy-done.8
  58.2 0.0 copy-done.9
  58.2 0.8 %far.1 = f32[32,2,8,128]{3,2,1,0:T(8,128)} custom-call(f32[32,2,8,128]{3,2,1,0:T(8,128)S(1)} %all_to_all.10.pay_ref, f32[256,128]{1,0:T(8,128)S(1)} %copy-done.9, f32[256,128]{1,0:T(8,128)S(1)} %copy-done.8), custom_call_target="tpu_custom_call" | custom-call | bytes 524288 | tf_op jit(solution)/shard_map/far/pallas_call | solution.py:686
  59.0 3.8 %all-to-all-start.1 = ((f32[32,2,8,128]{3,2,1,0:T(8,128)}), f32[32,2,8,128]{3,2,1,0:T(8,128)S(1)}, u32[]{:S(2)}, u32[]{:S(2)}) async-start(f32[32,2,8,128]{3,2,1,0:T(8,128)} %far.1), calls=%async_computation.1 | async-start | bytes 524288 | tf_op jit(solution)/shard_map/all_to_all | solution.py:693
  62.8 1.7 %collective-permute-start.9 = (f32[256,128]{1,0:T(8,128)S(1)}, f32[256,128]{1,0:T(8,128)S(1)}, u32[]{:S(2)}, u32[]{:S(2)}) collective-permute-start(f32[256,128]{1,0:T(8,128)S(1)} %get-tuple-element.34), channel_id=1, source_target_pairs={{0,1},{1,2},{2,3},{3,4},{4,5},{5,6},{6,7},{7,8},{8,9},{9,10},{10,1... | collective-permute-start | bytes 393224 | tf_op jit(solution)/shard_map/ppermute | solution.py:683
  64.5 0.0 collective-permute-start.10
  64.6 3.0 %collective-permute-done.9.prev_ref = f32[256,128]{1,0:T(8,128)S(1)} collective-permute-done((f32[256,128]{1,0:T(8,128)S(1)}, f32[256,128]{1,0:T(8,128)S(1)}, u32[]{:S(2)}, u32[]{:S(2)}) %collective-permute-start.9) | collective-permute-done | bytes 131104 | tf_op jit(solution)/shard_map/ppermute | solution.py:683
  67.5 2.4 %collective-permute-done.10.next_ref = f32[256,128]{1,0:T(8,128)S(1)} collective-permute-done((f32[256,128]{1,0:T(8,128)S(1)}, f32[256,128]{1,0:T(8,128)S(1)}, u32[]{:S(2)}, u32[]{:S(2)}) %collective-permute-start.10) | collective-permute-done | bytes 131104 | tf_op jit(solution)/shard_map/ppermute | solution.py:684
  69.9 4.4 %all-to-all-done.1.ret_ref = f32[32,2,8,128]{3,2,1,0:T(8,128)S(1)} async-done(((f32[32,2,8,128]{3,2,1,0:T(8,128)}), f32[32,2,8,128]{3,2,1,0:T(8,128)S(1)}, u32[]{:S(2)}, u32[]{:S(2)}) %all-to-all-start.1) | async-done | bytes 262176 | tf_op jit(solution)/shard_map/all_to_all | solution.py:693
  74.3 6.1 %final.1 = f32[3,2048,128]{2,1,0:T(8,128)} custom-call(f32[32,2,8,128]{3,2,1,0:T(8,128)S(1)} %all-to-all-done.1.ret_ref, f32[256,128]{1,0:T(8,128)S(1)} %collective-permute-done.9.prev_ref, f32[256,128]{1,0:T(8,128)S(1)} %collective-permute-done.10.next_ref, f32[81920,128]{1,0:T(8,128)} %get-tuple-element.36.store), custom_call_target="tpu_custom_call" | custom-call | flops 1073741824 | bytes 10485760 | tf_op jit(solution)/shard_map/final/pallas_call | solution.py:694
  (9 shorter events, 0.0 us)
Async XLA Ops:
  0.0 18.8 %copy-start = (f32[1,3,256,8,128]{4,3,2,1,0:T(8,128)S(1)}, f32[1,3,256,8,128]{4,3,2,1,0:T(8,128)}, u32[]{:S(2)}) copy-start(f32[1,3,256,8,128]{4,3,2,1,0:T(8,128)} %param.10) | copy-start | bytes 9437188
  0.8 27.0 %copy-start.7 = (f32[896,128]{1,0:T(8,128)S(1)}, f32[896,128]{1,0:T(8,128)}, u32[]{:S(2)}) copy-start(f32[896,128]{1,0:T(8,128)} %constant.13.clone.table_ref) | copy-start | bytes 1376260
  0.8 27.0 %copy-start.11 = (f32[32]{0:T(128)S(1)}, f32[32]{0:T(128)}, u32[]{:S(2)}) copy-start(f32[32]{0:T(128)} %constant.12.clone.profile_ref) | copy-start | bytes 388
  4.2 23.6 %copy-start.6 = (f32[896,128]{1,0:T(8,128)S(1)}, f32[896,128]{1,0:T(8,128)}, u32[]{:S(2)}) copy-start(f32[896,128]{1,0:T(8,128)} %constant.14.clone.later_ref) | copy-start | bytes 1376260
  4.2 23.6 %collective-permute-start.8 = (f32[4,256,128]{2,1,0:T(8,128)}, f32[4,256,128]{2,1,0:T(8,128)S(1)}, u32[]{:S(2)}, u32[]{:S(2)}) collective-permute-start(f32[4,256,128]{2,1,0:T(8,128)} %get-tuple-element.27.low_in), channel_id=1, source_target_pairs={{1,0},{2,1},{3,2},{4,3},{5,4},{6,5},{7,6},{8,7},{9,8},{10,9},{11,1... | collective-permute-start | bytes 1572872 | tf_op jit(solution)/shard_map/ppermute | solution.py:629
  7.6 20.3 %collective-permute-start.7 = (f32[4,256,128]{2,1,0:T(8,128)}, f32[4,256,128]{2,1,0:T(8,128)S(1)}, u32[]{:S(2)}, u32[]{:S(2)}) collective-permute-start(f32[4,256,128]{2,1,0:T(8,128)} %get-tuple-element.28.high_in), channel_id=1, source_target_pairs={{0,1},{1,2},{2,3},{3,4},{4,5},{5,6},{6,7},{7,8},{8,9},{9,10},{10,1... | collective-permute-start | bytes 1572872 | tf_op jit(solution)/shard_map/ppermute | solution.py:628
  7.6 6.2 %collective-permute-start = (f32[192,128]{1,0:T(8,128)}, f32[192,128]{1,0:T(8,128)S(1)}, u32[]{:S(2)}, u32[]{:S(2)}) collective-permute-start(f32[192,128]{1,0:T(8,128)} %get-tuple-element.22), channel_id=1, source_target_pairs={{0,32},{1,33},{2,34},{3,35},{4,36},{5,37},{6,38},{7,39},{8,40},{9,... | collective-permute-start | bytes 294920 | tf_op jit(solution)/shard_map/ppermute | solution.py:577
  10.2 4.2 %collective-permute-start.1 = (f32[192,128]{1,0:T(8,128)}, f32[192,128]{1,0:T(8,128)S(1)}, u32[]{:S(2)}, u32[]{:S(2)}) collective-permute-start(f32[192,128]{1,0:T(8,128)} %get-tuple-element.23), channel_id=1, source_target_pairs={{0,64},{1,65},{2,66},{3,67},{4,68},{5,69},{6,70},{7,71},{8,72},{9,... | collective-permute-start | bytes 294920 | tf_op jit(solution)/shard_map/ppermute | solution.py:577
  12.5 3.2 %collective-permute-start.2 = (f32[192,128]{1,0:T(8,128)}, f32[192,128]{1,0:T(8,128)S(1)}, u32[]{:S(2)}, u32[]{:S(2)}) collective-permute-start(f32[192,128]{1,0:T(8,128)} %get-tuple-element.24), channel_id=1, source_target_pairs={{0,96},{1,97},{2,98},{3,99},{4,100},{5,101},{6,102},{7,103},{8,104... | collective-permute-start | bytes 294920 | tf_op jit(solution)/shard_map/ppermute | solution.py:577
  15.7 0.9 %copy-start.10 = (f32[192,128]{1,0:T(8,128)S(1)}, f32[192,128]{1,0:T(8,128)}, u32[]{:S(2)}) copy-start(f32[192,128]{1,0:T(8,128)} %get-tuple-element.21.refs_0_) | copy-start | bytes 294916
  16.6 7.3 %collective-permute-start.3 = (f32[192,128]{1,0:T(8,128)S(1)}, f32[192,128]{1,0:T(8,128)S(1)}, u32[]{:S(2)}, u32[]{:S(2)}) collective-permute-start(f32[192,128]{1,0:T(8,128)S(1)} %pick_y.1.after.refs_0_), channel_id=1, source_target_pairs={{0,128},{32,160},{64,192},{96,224},{1,129},{33,161},{65,193},{97,2... | collective-permute-start | bytes 294920 | tf_op jit(solution)/shard_map/ppermute | solution.py:632
  18.8 1.2 %copy-start.1 = (f32[1,256,8,128]{3,2,1,0:T(8,128)S(1)}, f32[1,256,8,128]{3,2,1,0:T(8,128)}, u32[]{:S(2)}) copy-start(f32[1,256,8,128]{3,2,1,0:T(8,128)} %param.11) | copy-start | bytes 3145732
  20.0 7.9 %copy-start.2 = (s32[1,256,8,128]{3,2,1,0:T(8,128)S(1)}, s32[1,256,8,128]{3,2,1,0:T(8,128)}, u32[]{:S(2)}) copy-start(s32[1,256,8,128]{3,2,1,0:T(8,128)} %param.12) | copy-start | bytes 3145732
  20.0 7.9 %copy-start.3 = (f32[4,256,128]{2,1,0:T(8,128)S(1)}, f32[4,256,128]{2,1,0:T(8,128)}, u32[]{:S(2)}) copy-start(f32[4,256,128]{2,1,0:T(8,128)} %get-tuple-element.27.low_in) | copy-start | bytes 1572868
  20.0 7.9 %copy-start.4 = (f32[4,256,128]{2,1,0:T(8,128)S(1)}, f32[4,256,128]{2,1,0:T(8,128)}, u32[]{:S(2)}) copy-start(f32[4,256,128]{2,1,0:T(8,128)} %get-tuple-element.28.high_in) | copy-start | bytes 1572868
  24.0 8.6 %collective-permute-start.6 = (f32[192,128]{1,0:T(8,128)S(1)}, f32[192,128]{1,0:T(8,128)S(1)}, u32[]{:S(2)}, u32[]{:S(2)}) collective-permute-start(f32[192,128]{1,0:T(8,128)S(1)} %pick_z.1.after.q0), channel_id=1, source_target_pairs={{0,96},{32,0},{64,32},{96,64},{128,224},{160,128},{192,160},{224,1... | collective-permute-start | bytes 294920 | tf_op jit(solution)/shard_map/ppermute | solution.py:585
  26.8 5.8 %collective-permute-start.5 = (f32[192,128]{1,0:T(8,128)S(1)}, f32[192,128]{1,0:T(8,128)S(1)}, u32[]{:S(2)}, u32[]{:S(2)}) collective-permute-start(f32[192,128]{1,0:T(8,128)S(1)} %pick_z.1.after.q0), channel_id=1, source_target_pairs={{0,64},{32,96},{64,0},{96,32},{128,192},{160,224},{192,128},{224,1... | collective-permute-start | bytes 294920 | tf_op jit(solution)/shard_map/ppermute | solution.py:585
  27.1 5.7 %collective-permute-start.4 = (f32[192,128]{1,0:T(8,128)S(1)}, f32[192,128]{1,0:T(8,128)S(1)}, u32[]{:S(2)}, u32[]{:S(2)}) collective-permute-start(f32[192,128]{1,0:T(8,128)S(1)} %pick_z.1.after.q0), channel_id=1, source_target_pairs={{0,32},{32,64},{64,96},{96,0},{128,160},{160,192},{192,224},{224,1... | collective-permute-start | bytes 294920 | tf_op jit(solution)/shard_map/ppermute | solution.py:585
  27.9 4.9 %copy-start.5 = (f32[928,128]{1,0:T(8,128)S(1)}, f32[928,128]{1,0:T(8,128)}, u32[]{:S(2)}) copy-start(f32[928,128]{1,0:T(8,128)} %constant.15.clone.table_ref) | copy-start | bytes 1425412
  32.8 25.3 %copy-start.8 = (f32[256,128]{1,0:T(8,128)S(1)}, f32[256,128]{1,0:T(8,128)}, u32[]{:S(2)}) copy-start(f32[256,128]{1,0:T(8,128)} %constant.17.clone.wrap_ref) | copy-start | bytes 393220
  32.8 25.3 %copy-start.9 = (f32[256,128]{1,0:T(8,128)S(1)}, f32[256,128]{1,0:T(8,128)}, u32[]{:S(2)}) copy-start(f32[256,128]{1,0:T(8,128)} %constant.16.clone.step_ref) | copy-start | bytes 393220
  59.0 15.3 %all-to-all-start.1 = ((f32[32,2,8,128]{3,2,1,0:T(8,128)}), f32[32,2,8,128]{3,2,1,0:T(8,128)S(1)}, u32[]{:S(2)}, u32[]{:S(2)}) async-start(f32[32,2,8,128]{3,2,1,0:T(8,128)} %far.1), calls=%async_computation.1 | async-start | bytes 524288 | tf_op jit(solution)/shard_map/all_to_all | solution.py:693
  62.8 4.7 %collective-permute-start.9 = (f32[256,128]{1,0:T(8,128)S(1)}, f32[256,128]{1,0:T(8,128)S(1)}, u32[]{:S(2)}, u32[]{:S(2)}) collective-permute-start(f32[256,128]{1,0:T(8,128)S(1)} %get-tuple-element.34), channel_id=1, source_target_pairs={{0,1},{1,2},{2,3},{3,4},{4,5},{5,6},{6,7},{7,8},{8,9},{9,10},{10,1... | collective-permute-start | bytes 393224 | tf_op jit(solution)/shard_map/ppermute | solution.py:683
  64.5 5.3 %collective-permute-start.10 = (f32[256,128]{1,0:T(8,128)S(1)}, f32[256,128]{1,0:T(8,128)S(1)}, u32[]{:S(2)}, u32[]{:S(2)}) collective-permute-start(f32[256,128]{1,0:T(8,128)S(1)} %get-tuple-element.35), channel_id=1, source_target_pairs={{1,0},{2,1},{3,2},{4,3},{5,4},{6,5},{7,6},{8,7},{9,8},{10,9},{11,1... | collective-permute-start | bytes 393224 | tf_op jit(solution)/shard_map/ppermute | solution.py:684

commit v6 on v5

--- a/solution.py
+++ b/solution.py
@@ -255,7 +255,7 @@
         out_ref[0, tile(x), :] = u - DRAG * turb_ref[tile(x), :].astype(jnp.float32) * u * jnp.abs(u)
         return 0
 
-    lax.fori_loop(0, NX, drag, 0, unroll=16)
+    lax.fori_loop(0, NX, drag, 0, unroll=32)
 
     def blend(i, _):
         kept = 1.0 - profile_ref[i] * active
@@ -263,7 +263,7 @@
             out_ref[c, tile(start + i), :] = kept * out_ref[c, tile(start + i), :]
         return 0
 
-    lax.fori_loop(0, FR, blend, 0, unroll=8)
+    lax.fori_loop(0, FR, blend, 0, unroll=16)
     for c in range(3):
         copies.append(pltpu.make_async_copy(out_ref.at[c], store.at[pl.ds(c * CELLS, CELLS)], sems.at[1 + c]))
         copies[-1].start()
@@ -408,7 +408,7 @@
         pay_ref[block, 1] = left
         return 0
 
-    lax.fori_loop(1, NX // ROWS, weigh, 0, unroll=4)
+    lax.fori_loop(1, NX // ROWS, weigh, 0, unroll=8)
     right, left, rows = sums(0, tile(0))
     moment0 = functools.reduce(jnp.add, rows)
     moment1 = functools.reduce(jnp.add, [float(r - 1) * rows[r] for r in range(EXT) if r != 1])
@@ -449,8 +449,8 @@
         left = step * left + pay_ref[t, 1]
 
 
-OUT_CHUNKS = 8
-HAT_CHUNKS = 4
+OUT_CHUNKS = 4
+HAT_CHUNKS = 2
 
 
 def green0(j):
@@ -502,7 +502,7 @@
         if k:
             wait_all(copies[:EXT])
             copies = copies[EXT:]
-        lax.fori_loop(k * count, (k + 1) * count, line, 0, unroll=4)
+        lax.fori_loop(k * count, (k + 1) * count, line, 0, unroll=8)
     at = pl.ds(0, ROWS)
     values, rows = solve(0, at)
     slope, curve = ret_ref[0, 0], ret_ref[0, 1]
@@ -545,7 +545,7 @@
     part = CELLS // OUT_CHUNKS
     count = NX // OUT_CHUNKS
     for k in range(OUT_CHUNKS):
-        carry = lax.fori_loop(k * count, (k + 1) * count, project, carry, unroll=16)
+        carry = lax.fori_loop(k * count, (k + 1) * count, project, carry, unroll=32)
         rows = pl.ds(k * part, part)
         copies.append(pltpu.make_async_copy(out_ref.at[:, rows], out_hbm.at[:, rows], out_sems.at[k]))
         copies[-1].start()

time: 81 us -> 80.2 us (level)
  no operation moved by 1% of the time
where the time goes in v6:
time: 80.2 us; the launch traced here: 79.8 us
  blocking collectives  22.3 us (28%)
  Pallas kernels  21.3 us (27%)
  starting transfers between devices  21.1 us (26%)
  waiting for transfers between devices  11.9 us (15%)
  local copies, waits for them, and re-layouts  2.16 us (3%)
  between operations  1.01 us (1%)
    all_to_all x1, blocking collectives, local(): pay = lax.all_to_all(pay, 'slab', split_axis=0, concat_axis=0, tiled=True)  22.3 us
    ppermute x3, starting transfers between devices, scatter_y(): came = [lax.ppermute(piece[k], 'sim', [(0, k)]) for k in (1, 2, 3)]  6.22 us
    pallas_call x1, Pallas kernels, local(): call(final_kernel, [(3, CELLS, NZ)], 'final', room=FORWARD_ROOM, in_specs...  5.49 us
    pallas_call x1, Pallas kernels, local(): call(forward_kernel, [(STORE, NZ), (EXT, NX, NZ), plane, plane, (3, CELLS...  4.63 us
    all_to_all x1, waiting for transfers between devices, local(): ret = lax.all_to_all(ret, 'slab', split_axis=0, concat_axis=0, tiled=True)  4.39 us
    pallas_call x1, Pallas kernels, local(): call(diffuse_kernel, [(3, CELLS, NZ), (ROWS, NZ)], 'diffuse', room=DIFFUS...  3.92 us
    ppermute x3, starting transfers between devices, gather_y(): quarters.append(lax.ppermute(mine, 'sim', pairs))  3.85 us
    all_to_all x1, starting transfers between devices, local(): ret = lax.all_to_all(ret, 'slab', split_axis=0, concat_axis=0, tiled=True)  3.83 us
  transfers between devices with their start and end apart: 12, of which 6 were waited for; matrix products, arithmetic and copies ran while one was open for 0% of the time, Pallas kernels for 11%

profile of v6, /device:TPU:1, one launch (start us, length us, event | category | flops | bytes accessed | tf_op | source)
XLA Modules:
  0.0 79.8 jit_solution(6955571790299840530)
XLA Ops:
  0.8 0.0 copy-start.7
  0.8 0.0 copy-start.11
  0.8 3.4 %edges.1 = (f32[192,128]{1,0:T(8,128)}, f32[192,128]{1,0:T(8,128)}, f32[192,128]{1,0:T(8,128)}, f32[192,128]{1,0:T(8,128)}, f32[4,256,128]{2,1,0:T(8,128)}, /*index=5*/f32[4,256,128]{2,1,0:T(8,128)}) custom-call(s32[1]{0:T(128)S(6)} %copy.15.start_ref, f32[3,2048,128]{2,1,0:T(8,128)} %bitcast.4, f32[2048,128]{1,0:T(8,128)} %bitcast.6), custom_call_target="tpu_custom_call" | custom-call | bytes 6291456 | tf_op jit(solution)/shard_map/edges/pallas_call | solution.py:610
  4.2 0.0 copy-start.6
  4.2 3.3 %collective-permute-start.8 = (f32[4,256,128]{2,1,0:T(8,128)}, f32[4,256,128]{2,1,0:T(8,128)S(1)}, u32[]{:S(2)}, u32[]{:S(2)}) collective-permute-start(f32[4,256,128]{2,1,0:T(8,128)} %get-tuple-element.27.low_in), channel_id=1, source_target_pairs={{1,0},{2,1},{3,2},{4,3},{5,4},{6,5},{7,6},{8,7},{9,8},{10,9},{11,1... | collective-permute-start | bytes 1572872 | tf_op jit(solution)/shard_map/ppermute | solution.py:629
  7.6 0.0 collective-permute-start.7
  7.6 2.6 %collective-permute-start = (f32[192,128]{1,0:T(8,128)}, f32[192,128]{1,0:T(8,128)S(1)}, u32[]{:S(2)}, u32[]{:S(2)}) collective-permute-start(f32[192,128]{1,0:T(8,128)} %get-tuple-element.22), channel_id=1, source_target_pairs={{0,32},{1,33},{2,34},{3,35},{4,36},{5,37},{6,38},{7,39},{8,40},{9,... | collective-permute-start | bytes 294920 | tf_op jit(solution)/shard_map/ppermute | solution.py:577
  10.2 2.3 %collective-permute-start.1 = (f32[192,128]{1,0:T(8,128)}, f32[192,128]{1,0:T(8,128)S(1)}, u32[]{:S(2)}, u32[]{:S(2)}) collective-permute-start(f32[192,128]{1,0:T(8,128)} %get-tuple-element.23), channel_id=1, source_target_pairs={{0,64},{1,65},{2,66},{3,67},{4,68},{5,69},{6,70},{7,71},{8,72},{9,... | collective-permute-start | bytes 294920 | tf_op jit(solution)/shard_map/ppermute | solution.py:577
  12.5 1.3 %collective-permute-start.2 = (f32[192,128]{1,0:T(8,128)}, f32[192,128]{1,0:T(8,128)S(1)}, u32[]{:S(2)}, u32[]{:S(2)}) collective-permute-start(f32[192,128]{1,0:T(8,128)} %get-tuple-element.24), channel_id=1, source_target_pairs={{0,96},{1,97},{2,98},{3,99},{4,100},{5,101},{6,102},{7,103},{8,104... | collective-permute-start | bytes 294920 | tf_op jit(solution)/shard_map/ppermute | solution.py:577
  13.8 0.0 collective-permute-done.refs_1_
  13.8 0.6 collective-permute-done.1.refs_2_
  14.4 1.3 %collective-permute-done.2.refs_3_ = f32[192,128]{1,0:T(8,128)S(1)} collective-permute-done((f32[192,128]{1,0:T(8,128)}, f32[192,128]{1,0:T(8,128)S(1)}, u32[]{:S(2)}, u32[]{:S(2)}) %collective-permute-start.2) | collective-permute-done | bytes 98336 | tf_op jit(solution)/shard_map/ppermute | solution.py:577
  15.7 0.9 %copy-done.10 = f32[192,128]{1,0:T(8,128)S(1)} copy-done((f32[192,128]{1,0:T(8,128)S(1)}, f32[192,128]{1,0:T(8,128)}, u32[]{:S(2)}) %copy-start.10) | copy-done | bytes 98328
  16.6 2.1 %collective-permute-start.3 = (f32[192,128]{1,0:T(8,128)S(1)}, f32[192,128]{1,0:T(8,128)S(1)}, u32[]{:S(2)}, u32[]{:S(2)}) collective-permute-start(f32[192,128]{1,0:T(8,128)S(1)} %pick_y.1.after.refs_0_), channel_id=1, source_target_pairs={{0,128},{32,160},{64,192},{96,224},{1,129},{33,161},{65,193},{97,2... | collective-permute-start | bytes 294920 | tf_op jit(solution)/shard_map/ppermute | solution.py:632
  18.8 0.0 copy-done
  18.8 0.0 copy-start.1
  18.8 1.2 %copy-done.1 = f32[1,256,8,128]{3,2,1,0:T(8,128)S(1)} copy-done((f32[1,256,8,128]{3,2,1,0:T(8,128)S(1)}, f32[1,256,8,128]{3,2,1,0:T(8,128)}, u32[]{:S(2)}) %copy-start.1) | copy-done | bytes 1048600
  20.0 3.9 %diffuse.1 = (f32[3,2048,128]{2,1,0:T(8,128)S(1)}, f32[8,128]{1,0:T(8,128)S(1)}) custom-call(f32[3,2048,128]{2,1,0:T(8,128)S(1)} %bitcast.5, f32[2048,128]{1,0:T(8,128)S(1)} %bitcast.7, f32[192,128]{1,0:T(8,128)S(1)} %pick_y.1.after.refs_0_), custom_call_target="tpu_custom_call" | custom-call | flops 67108864 | bytes 8388608 | tf_op jit(solution)/shard_map/diffuse/pallas_call | solution.py:633
  23.9 0.0 collective-permute-done.3.refs_1_
  24.0 2.8 %collective-permute-start.6 = (f32[192,128]{1,0:T(8,128)S(1)}, f32[192,128]{1,0:T(8,128)S(1)}, u32[]{:S(2)}, u32[]{:S(2)}) collective-permute-start(f32[192,128]{1,0:T(8,128)S(1)} %pick_z.1.after.q0), channel_id=1, source_target_pairs={{0,96},{32,0},{64,32},{96,64},{128,224},{160,128},{192,160},{224,1... | collective-permute-start | bytes 294920 | tf_op jit(solution)/shard_map/ppermute | solution.py:585
  26.8 0.4 collective-permute-start.5
  27.1 0.7 collective-permute-start.4
  27.8 0.0 collective-permute-done.8.next_in
  27.8 0.0 collective-permute-done.7.prev_in
  27.8 0.0 copy-done.7
  27.8 0.0 copy-done.11
  27.9 0.0 copy-done.6
  27.9 0.0 copy-done.2
  27.9 0.0 copy-done.3
  27.9 0.0 copy-done.4
  27.9 0.0 copy-start.5
  27.9 4.6 %forward.1 = (f32[81920,128]{1,0:T(8,128)}, f32[10,256,128]{2,1,0:T(8,128)S(1)}, f32[256,128]{1,0:T(8,128)S(1)}, f32[256,128]{1,0:T(8,128)S(1)}, f32[3,2048,128]{2,1,0:T(8,128)S(1)}) custom-call(s32[1]{0:T(128)S(6)} %copy.15.start_ref, f32[3,2048,128]{2,1,0:T(8,128)S(1)} %get-tuple-element.26.field_ref, ...), custom_call_target="tpu_custom_call", output_to_operand_aliasing={{4}: (1, {})} | custom-call | flops 1073741824 | bytes 10485760 | tf_op jit(solution)/shard_map/forward/pallas_call | solution.py:643
  32.5 0.0 collective-permute-done.6.q3
  32.6 0.0 collective-permute-done.5.q2
  32.6 0.2 collective-permute-done.4.q1
  32.8 0.0 copy-done.5
  32.8 3.0 %precursor.1 = (f32[81920,128]{1,0:T(8,128)}, f32[32,2,8,128]{3,2,1,0:T(8,128)S(1)}, f32[256,128]{1,0:T(8,128)S(1)}, f32[256,128]{1,0:T(8,128)S(1)}) custom-call(s32[1]{0:T(128)S(6)} %copy.15.start_ref, f32[192,128]{1,0:T(8,128)S(1)} %pick_z.1.after.q0, f32[192,128]{1,0:T(8,128)S(1)} %collective-permute-done.4.q1, ...), custom_call_target="tpu_custom_call", output_to_operand_aliasing={{0}: (10, {})} | custom-call | flops 268435456 | bytes 3145728 | tf_op jit(solution)/shard_map/precursor/pallas_call | solution.py:661
  35.8 22.3 %all_to_all.10.pay_ref = f32[32,2,8,128]{3,2,1,0:T(8,128)S(1)} all-to-all(f32[32,2,8,128]{3,2,1,0:T(8,128)S(1)} %get-tuple-element.33), channel_id=1, replica_groups=mesh['sim'=8,'slab'=32] {'slab'}, dimensions={0} | all-to-all | bytes 524288 | tf_op jit(solution)/shard_map/all_to_all | solution.py:685
  58.1 0.0 copy-done.8
  58.1 0.0 copy-done.9
  58.1 0.8 %far.1 = f32[32,2,8,128]{3,2,1,0:T(8,128)} custom-call(f32[32,2,8,128]{3,2,1,0:T(8,128)S(1)} %all_to_all.10.pay_ref, f32[256,128]{1,0:T(8,128)S(1)} %copy-done.9, f32[256,128]{1,0:T(8,128)S(1)} %copy-done.8), custom_call_target="tpu_custom_call" | custom-call | bytes 524288 | tf_op jit(solution)/shard_map/far/pallas_call | solution.py:686
  59.0 3.8 %all-to-all-start.1 = ((f32[32,2,8,128]{3,2,1,0:T(8,128)}), f32[32,2,8,128]{3,2,1,0:T(8,128)S(1)}, u32[]{:S(2)}, u32[]{:S(2)}) async-start(f32[32,2,8,128]{3,2,1,0:T(8,128)} %far.1), calls=%async_computation.1 | async-start | bytes 524288 | tf_op jit(solution)/shard_map/all_to_all | solution.py:693
  62.8 1.7 %collective-permute-start.9 = (f32[256,128]{1,0:T(8,128)S(1)}, f32[256,128]{1,0:T(8,128)S(1)}, u32[]{:S(2)}, u32[]{:S(2)}) collective-permute-start(f32[256,128]{1,0:T(8,128)S(1)} %get-tuple-element.34), channel_id=1, source_target_pairs={{0,1},{1,2},{2,3},{3,4},{4,5},{5,6},{6,7},{7,8},{8,9},{9,10},{10,1... | collective-permute-start | bytes 393224 | tf_op jit(solution)/shard_map/ppermute | solution.py:683
  64.5 0.0 collective-permute-start.10
  64.5 3.0 %collective-permute-done.9.prev_ref = f32[256,128]{1,0:T(8,128)S(1)} collective-permute-done((f32[256,128]{1,0:T(8,128)S(1)}, f32[256,128]{1,0:T(8,128)S(1)}, u32[]{:S(2)}, u32[]{:S(2)}) %collective-permute-start.9) | collective-permute-done | bytes 131104 | tf_op jit(solution)/shard_map/ppermute | solution.py:683
  67.5 2.4 %collective-permute-done.10.next_ref = f32[256,128]{1,0:T(8,128)S(1)} collective-permute-done((f32[256,128]{1,0:T(8,128)S(1)}, f32[256,128]{1,0:T(8,128)S(1)}, u32[]{:S(2)}, u32[]{:S(2)}) %collective-permute-start.10) | collective-permute-done | bytes 131104 | tf_op jit(solution)/shard_map/ppermute | solution.py:684
  69.9 4.4 %all-to-all-done.1.ret_ref = f32[32,2,8,128]{3,2,1,0:T(8,128)S(1)} async-done(((f32[32,2,8,128]{3,2,1,0:T(8,128)}), f32[32,2,8,128]{3,2,1,0:T(8,128)S(1)}, u32[]{:S(2)}, u32[]{:S(2)}) %all-to-all-start.1) | async-done | bytes 262176 | tf_op jit(solution)/shard_map/all_to_all | solution.py:693
  74.3 5.5 %final.1 = f32[3,2048,128]{2,1,0:T(8,128)} custom-call(f32[32,2,8,128]{3,2,1,0:T(8,128)S(1)} %all-to-all-done.1.ret_ref, f32[256,128]{1,0:T(8,128)S(1)} %collective-permute-done.9.prev_ref, f32[256,128]{1,0:T(8,128)S(1)} %collective-permute-done.10.next_ref, f32[81920,128]{1,0:T(8,128)} %get-tuple-element.36.store), custom_call_target="tpu_custom_call" | custom-call | flops 1073741824 | bytes 10485760 | tf_op jit(solution)/shard_map/final/pallas_call | solution.py:694
  (9 shorter events, 0.0 us)
Async XLA Ops:
  0.0 18.8 %copy-start = (f32[1,3,256,8,128]{4,3,2,1,0:T(8,128)S(1)}, f32[1,3,256,8,128]{4,3,2,1,0:T(8,128)}, u32[]{:S(2)}) copy-start(f32[1,3,256,8,128]{4,3,2,1,0:T(8,128)} %param.10) | copy-start | bytes 9437188
  0.8 27.0 %copy-start.7 = (f32[896,128]{1,0:T(8,128)S(1)}, f32[896,128]{1,0:T(8,128)}, u32[]{:S(2)}) copy-start(f32[896,128]{1,0:T(8,128)} %constant.13.clone.table_ref) | copy-start | bytes 1376260
  0.8 27.0 %copy-start.11 = (f32[32]{0:T(128)S(1)}, f32[32]{0:T(128)}, u32[]{:S(2)}) copy-start(f32[32]{0:T(128)} %constant.12.clone.profile_ref) | copy-start | bytes 388
  4.2 23.6 %copy-start.6 = (f32[896,128]{1,0:T(8,128)S(1)}, f32[896,128]{1,0:T(8,128)}, u32[]{:S(2)}) copy-start(f32[896,128]{1,0:T(8,128)} %constant.14.clone.later_ref) | copy-start | bytes 1376260
  4.2 23.6 %collective-permute-start.8 = (f32[4,256,128]{2,1,0:T(8,128)}, f32[4,256,128]{2,1,0:T(8,128)S(1)}, u32[]{:S(2)}, u32[]{:S(2)}) collective-permute-start(f32[4,256,128]{2,1,0:T(8,128)} %get-tuple-element.27.low_in), channel_id=1, source_target_pairs={{1,0},{2,1},{3,2},{4,3},{5,4},{6,5},{7,6},{8,7},{9,8},{10,9},{11,1... | collective-permute-start | bytes 1572872 | tf_op jit(solution)/shard_map/ppermute | solution.py:629
  7.6 20.3 %collective-permute-start.7 = (f32[4,256,128]{2,1,0:T(8,128)}, f32[4,256,128]{2,1,0:T(8,128)S(1)}, u32[]{:S(2)}, u32[]{:S(2)}) collective-permute-start(f32[4,256,128]{2,1,0:T(8,128)} %get-tuple-element.28.high_in), channel_id=1, source_target_pairs={{0,1},{1,2},{2,3},{3,4},{4,5},{5,6},{6,7},{7,8},{8,9},{9,10},{10,1... | collective-permute-start | bytes 1572872 | tf_op jit(solution)/shard_map/ppermute | solution.py:628
  7.6 6.2 %collective-permute-start = (f32[192,128]{1,0:T(8,128)}, f32[192,128]{1,0:T(8,128)S(1)}, u32[]{:S(2)}, u32[]{:S(2)}) collective-permute-start(f32[192,128]{1,0:T(8,128)} %get-tuple-element.22), channel_id=1, source_target_pairs={{0,32},{1,33},{2,34},{3,35},{4,36},{5,37},{6,38},{7,39},{8,40},{9,... | collective-permute-start | bytes 294920 | tf_op jit(solution)/shard_map/ppermute | solution.py:577
  10.2 4.2 %collective-permute-start.1 = (f32[192,128]{1,0:T(8,128)}, f32[192,128]{1,0:T(8,128)S(1)}, u32[]{:S(2)}, u32[]{:S(2)}) collective-permute-start(f32[192,128]{1,0:T(8,128)} %get-tuple-element.23), channel_id=1, source_target_pairs={{0,64},{1,65},{2,66},{3,67},{4,68},{5,69},{6,70},{7,71},{8,72},{9,... | collective-permute-start | bytes 294920 | tf_op jit(solution)/shard_map/ppermute | solution.py:577
  12.5 3.2 %collective-permute-start.2 = (f32[192,128]{1,0:T(8,128)}, f32[192,128]{1,0:T(8,128)S(1)}, u32[]{:S(2)}, u32[]{:S(2)}) collective-permute-start(f32[192,128]{1,0:T(8,128)} %get-tuple-element.24), channel_id=1, source_target_pairs={{0,96},{1,97},{2,98},{3,99},{4,100},{5,101},{6,102},{7,103},{8,104... | collective-permute-start | bytes 294920 | tf_op jit(solution)/shard_map/ppermute | solution.py:577
  15.7 0.9 %copy-start.10 = (f32[192,128]{1,0:T(8,128)S(1)}, f32[192,128]{1,0:T(8,128)}, u32[]{:S(2)}) copy-start(f32[192,128]{1,0:T(8,128)} %get-tuple-element.21.refs_0_) | copy-start | bytes 294916
  16.6 7.3 %collective-permute-start.3 = (f32[192,128]{1,0:T(8,128)S(1)}, f32[192,128]{1,0:T(8,128)S(1)}, u32[]{:S(2)}, u32[]{:S(2)}) collective-permute-start(f32[192,128]{1,0:T(8,128)S(1)} %pick_y.1.after.refs_0_), channel_id=1, source_target_pairs={{0,128},{32,160},{64,192},{96,224},{1,129},{33,161},{65,193},{97,2... | collective-permute-start | bytes 294920 | tf_op jit(solution)/shard_map/ppermute | solution.py:632
  18.8 1.2 %copy-start.1 = (f32[1,256,8,128]{3,2,1,0:T(8,128)S(1)}, f32[1,256,8,128]{3,2,1,0:T(8,128)}, u32[]{:S(2)}) copy-start(f32[1,256,8,128]{3,2,1,0:T(8,128)} %param.11) | copy-start | bytes 3145732
  20.0 7.9 %copy-start.2 = (s32[1,256,8,128]{3,2,1,0:T(8,128)S(1)}, s32[1,256,8,128]{3,2,1,0:T(8,128)}, u32[]{:S(2)}) copy-start(s32[1,256,8,128]{3,2,1,0:T(8,128)} %param.12) | copy-start | bytes 3145732
  20.0 7.9 %copy-start.3 = (f32[4,256,128]{2,1,0:T(8,128)S(1)}, f32[4,256,128]{2,1,0:T(8,128)}, u32[]{:S(2)}) copy-start(f32[4,256,128]{2,1,0:T(8,128)} %get-tuple-element.27.low_in) | copy-start | bytes 1572868
  20.0 7.9 %copy-start.4 = (f32[4,256,128]{2,1,0:T(8,128)S(1)}, f32[4,256,128]{2,1,0:T(8,128)}, u32[]{:S(2)}) copy-start(f32[4,256,128]{2,1,0:T(8,128)} %get-tuple-element.28.high_in) | copy-start | bytes 1572868
  24.0 8.6 %collective-permute-start.6 = (f32[192,128]{1,0:T(8,128)S(1)}, f32[192,128]{1,0:T(8,128)S(1)}, u32[]{:S(2)}, u32[]{:S(2)}) collective-permute-start(f32[192,128]{1,0:T(8,128)S(1)} %pick_z.1.after.q0), channel_id=1, source_target_pairs={{0,96},{32,0},{64,32},{96,64},{128,224},{160,128},{192,160},{224,1... | collective-permute-start | bytes 294920 | tf_op jit(solution)/shard_map/ppermute | solution.py:585
  26.8 5.8 %collective-permute-start.5 = (f32[192,128]{1,0:T(8,128)S(1)}, f32[192,128]{1,0:T(8,128)S(1)}, u32[]{:S(2)}, u32[]{:S(2)}) collective-permute-start(f32[192,128]{1,0:T(8,128)S(1)} %pick_z.1.after.q0), channel_id=1, source_target_pairs={{0,64},{32,96},{64,0},{96,32},{128,192},{160,224},{192,128},{224,1... | collective-permute-start | bytes 294920 | tf_op jit(solution)/shard_map/ppermute | solution.py:585
  27.1 5.7 %collective-permute-start.4 = (f32[192,128]{1,0:T(8,128)S(1)}, f32[192,128]{1,0:T(8,128)S(1)}, u32[]{:S(2)}, u32[]{:S(2)}) collective-permute-start(f32[192,128]{1,0:T(8,128)S(1)} %pick_z.1.after.q0), channel_id=1, source_target_pairs={{0,32},{32,64},{64,96},{96,0},{128,160},{160,192},{192,224},{224,1... | collective-permute-start | bytes 294920 | tf_op jit(solution)/shard_map/ppermute | solution.py:585
  27.9 4.9 %copy-start.5 = (f32[928,128]{1,0:T(8,128)S(1)}, f32[928,128]{1,0:T(8,128)}, u32[]{:S(2)}) copy-start(f32[928,128]{1,0:T(8,128)} %constant.15.clone.table_ref) | copy-start | bytes 1425412
  32.8 25.3 %copy-start.8 = (f32[256,128]{1,0:T(8,128)S(1)}, f32[256,128]{1,0:T(8,128)}, u32[]{:S(2)}) copy-start(f32[256,128]{1,0:T(8,128)} %constant.17.clone.wrap_ref) | copy-start | bytes 393220
  32.8 25.3 %copy-start.9 = (f32[256,128]{1,0:T(8,128)S(1)}, f32[256,128]{1,0:T(8,128)}, u32[]{:S(2)}) copy-start(f32[256,128]{1,0:T(8,128)} %constant.16.clone.step_ref) | copy-start | bytes 393220
  59.0 15.3 %all-to-all-start.1 = ((f32[32,2,8,128]{3,2,1,0:T(8,128)}), f32[32,2,8,128]{3,2,1,0:T(8,128)S(1)}, u32[]{:S(2)}, u32[]{:S(2)}) async-start(f32[32,2,8,128]{3,2,1,0:T(8,128)} %far.1), calls=%async_computation.1 | async-start | bytes 524288 | tf_op jit(solution)/shard_map/all_to_all | solution.py:693
  62.8 4.7 %collective-permute-start.9 = (f32[256,128]{1,0:T(8,128)S(1)}, f32[256,128]{1,0:T(8,128)S(1)}, u32[]{:S(2)}, u32[]{:S(2)}) collective-permute-start(f32[256,128]{1,0:T(8,128)S(1)} %get-tuple-element.34), channel_id=1, source_target_pairs={{0,1},{1,2},{2,3},{3,4},{4,5},{5,6},{6,7},{7,8},{8,9},{9,10},{10,1... | collective-permute-start | bytes 393224 | tf_op jit(solution)/shard_map/ppermute | solution.py:683
  64.5 5.3 %collective-permute-start.10 = (f32[256,128]{1,0:T(8,128)S(1)}, f32[256,128]{1,0:T(8,128)S(1)}, u32[]{:S(2)}, u32[]{:S(2)}) collective-permute-start(f32[256,128]{1,0:T(8,128)S(1)} %get-tuple-element.35), channel_id=1, source_target_pairs={{1,0},{2,1},{3,2},{4,3},{5,4},{6,5},{7,6},{8,7},{9,8},{10,9},{11,1... | collective-permute-start | bytes 393224 | tf_op jit(solution)/shard_map/ppermute | solution.py:684
